TPU v7x, 32 devices: a whole 2x2x4 slice. The times are simulated.
32 devices in a mesh: dp: 4 (over y, core), expert: 2 (over x), tensor: 4 (over z).
Axes of the slice: x: 2, y: 2, z: 4, core: 2. Of those that a mesh axis runs over, the one named last changes fastest.
Arguments:
- tokens: bfloat16 [1024, 2048], P(('dp', 'expert')), may hold values from -6 to 6
- cotangent: bfloat16 [1024, 2048], P(('dp', 'expert')), may hold values from -6 to 6
- expert_ids: int32 [1024, 1], P(('dp', 'expert')), may hold values from 0 to 31; in each aligned block of 128 rows (0 to 127, 128 to 255, ...) at most 8 rows name the same one
- gate_weight: bfloat16 [32, 2048, 1408], P('expert', 'dp', 'tensor'), may hold values from -0.125 to 0.125
- up_weight: bfloat16 [32, 2048, 1408], P('expert', 'dp', 'tensor'), may hold values from -0.125 to 0.125
- down_weight: bfloat16 [32, 2048, 1408], P('expert', 'dp', 'tensor'), may hold values from -0.15625 to 0.15625
Outputs:
- grad_tokens: bfloat16 [1024, 2048], P(('dp', 'expert'), 'tensor')
- grad_gate: bfloat16 [32, 2048, 1408], P('expert', 'dp', 'tensor')
- grad_up: bfloat16 [32, 2048, 1408], P('expert', 'dp', 'tensor')
Inputs may be any that keep to these rules, and one draw needn't show every extreme that they name: `expert_ids`: among the 128 tokens of one block no expert id occurs more than 8 times, and in every draw some block holds some id exactly 8 times.
All inputs are finite; a program needn't handle non-finite values.
Results may differ from a plain program's by a relative error of at most 0.013.
Values may be sent and summed in bfloat16 or wider, within the bound.
No kernel may reach another device: no remote copies, remote signals or barrier semaphores. Data moves between devices by JAX's collectives and lax.ppermute only.
A program may use at most 192 MiB of HBM per device.

v0:
```python
import functools

import jax
import jax.numpy as jnp
from jax import lax
from jax.experimental import pallas as pl
from jax.experimental.pallas import tpu as pltpu
from jax.sharding import PartitionSpec as P

CAP = 8
META = 16
F32 = jnp.float32
BF16 = jnp.bfloat16
VMEM_LIMIT = 48 * 1024 * 1024


def swap(value, axis, count, bit):
    return lax.ppermute(value, axis, [(i, i ^ bit) for i in range(count)])


def whole_spec(shape):
    return pl.BlockSpec(shape, lambda *_: (0,) * len(shape))


def params():
    return pltpu.CompilerParams(vmem_limit_bytes=VMEM_LIMIT)


def split_kernel(width, n_dp, where, ids, rows_ref, *outs):
    k, x = where[0], where[1]
    rows = rows_ref.shape[0]
    for rel in range(n_dp):
        start = pl.multiple_of((k ^ rel) * width, 128)
        outs[rel][0:rows, :] = rows_ref[:, pl.ds(start, width)]
    if outs[0].shape[0] == rows:
        return
    column = ids[...]
    line = lax.broadcasted_iota(jnp.int32, (rows, rows), 0)
    lane = lax.broadcasted_iota(jnp.int32, (rows, rows), 1)
    named = jnp.broadcast_to(column, (rows, rows)).astype(F32)
    along = jnp.sum(jnp.where(line == lane, named, 0.0), axis=0, keepdims=True)
    earlier = jnp.where((named == along) & (line < lane), 1.0, 0.0)
    place = jnp.sum(earlier, axis=0, keepdims=True) + (x * CAP).astype(F32)
    at = lax.broadcasted_iota(jnp.int32, (META, rows), 0)
    meta = jnp.where(at == 0, along, jnp.where(at == 1, place, 0.0)).astype(BF16)
    for rel in range(n_dp):
        outs[rel][rows:, :] = jnp.zeros((META, width), BF16)
        outs[rel][rows:, 0:rows] = meta


def split(where, ids, values, width, n_dp, with_meta):
    rows = values.shape[0]
    tall = rows + META if with_meta else rows
    return pl.pallas_call(
        functools.partial(split_kernel, width, n_dp),
        out_shape=[jax.ShapeDtypeStruct((tall, width), BF16)] * n_dp,
        in_specs=[
            pl.BlockSpec(memory_space=pltpu.SMEM),
            whole_spec(ids.shape),
            whole_spec(values.shape),
        ],
        out_specs=[whole_spec((tall, width))] * n_dp,
        compiler_params=params(),
    )(where, ids, values)


def placer_of(row, slot_count):
    every = lax.broadcasted_iota(jnp.int32, (slot_count, row.shape[1]), 0)
    return (every == row).astype(F32).astype(BF16)


def project_kernel(n_dp, weights, first, where, *refs):
    blocks, refs = refs[: 2 * n_dp], refs[2 * n_dp :]
    if not first:
        lines, refs = refs[0], refs[1:]
    weight_refs, refs = refs[:weights], refs[weights:]
    if first:
        keep, send, placed, lines = refs
    else:
        keep, send, placed = refs
    step = pl.program_id(0)
    per_step = weight_refs[0].shape[0]
    local_experts, slot_rows, width = placed.shape
    slots = slot_rows // n_dp
    rows = blocks[0].shape[0] - (META if first else 0)

    @pl.when(step == 0)
    def _():
        for rel in range(n_dp):
            pair = blocks[2 * rel], blocks[2 * rel + 1]
            if first:
                metas = [b[rows:, 0:rows].astype(F32) for b in pair]
                ids = jnp.concatenate([m[0:1] for m in metas], axis=1)
                place = jnp.concatenate([m[1:2] for m in metas], axis=1)
                low = (where[1] * local_experts).astype(F32)
                row = ((ids - low) * slots + place).astype(jnp.int32)
                lines[rel] = jnp.broadcast_to(row, (8, row.shape[1]))
            else:
                row = lines[rel][0:1]
            placer = placer_of(row, local_experts * slots)
            values = jnp.concatenate([b[0:rows, :] for b in pair], axis=0)
            found = jnp.dot(placer, values, preferred_element_type=F32).astype(BF16)
            placed[:, rel * slots : (rel + 1) * slots, :] = found.reshape(local_experts, slots, width)

    for i in range(per_step):
        mine = placed[step * per_step + i]
        for w in range(weights):
            act = jnp.dot(mine, weight_refs[w][i], preferred_element_type=F32).astype(BF16)
            for rel in range(n_dp):
                out = send if rel & 1 else keep
                out[w, rel // 2, i] = act[rel * slots : (rel + 1) * slots]


def project(where, blocks, lines, weights, n_dp, per_step):
    first = lines is None
    local_experts, width, hidden = weights[0].shape
    slots = 2 * CAP
    rows = blocks[0].shape[0] - (META if first else 0)
    count = len(weights)
    act = (count, n_dp // 2, local_experts, slots, hidden)
    act_block = (count, n_dp // 2, per_step, slots, hidden)
    act_spec = pl.BlockSpec(act_block, lambda e: (0, 0, e, 0, 0))
    placed = (local_experts, n_dp * slots, width)
    line = (n_dp, 8, 2 * rows)
    weight_spec = pl.BlockSpec((per_step, width, hidden), lambda e: (e, 0, 0))
    out_shape = [jax.ShapeDtypeStruct(act, BF16), jax.ShapeDtypeStruct(act, BF16)]
    out_specs = [act_spec, act_spec]
    scratch = []
    operands = [where, *blocks]
    in_specs = [pl.BlockSpec(memory_space=pltpu.SMEM)] + [whole_spec(b.shape) for b in blocks]
    if first:
        out_shape += [jax.ShapeDtypeStruct(placed, BF16), jax.ShapeDtypeStruct(line, jnp.int32)]
        out_specs += [whole_spec(placed), whole_spec(line)]
    else:
        operands.append(lines)
        in_specs.append(whole_spec(line))
        scratch.append(pltpu.VMEM(placed, BF16))
    flops = 2 * count * local_experts * n_dp * slots * width * hidden
    return pl.pallas_call(
        functools.partial(project_kernel, n_dp, count, first),
        grid=(local_experts // per_step,),
        out_shape=out_shape,
        in_specs=in_specs + [weight_spec] * count,
        out_specs=out_specs,
        scratch_shapes=scratch,
        compiler_params=params(),
        cost_estimate=pl.CostEstimate(
            flops=4 * flops, bytes_accessed=count * local_experts * width * hidden * 2, transcendentals=0
        ),
    )(*operands, *weights)


def back_kernel(n_dp, where, lines, h0, h1, h2, h3, gate, up, keep_x, send_x, keep_z, send_z, held):
    step = pl.program_id(0)
    held_hidden = (h0, h1, h2, h3)
    per_step = gate.shape[0]
    slots = h0.shape[2]
    for i in range(per_step):
        gate_grad = jnp.concatenate([h[0, i] for h in held_hidden], axis=0)
        up_grad = jnp.concatenate([h[1, i] for h in held_hidden], axis=0)
        dims = (((1,), (1,)), ((), ()))
        value = lax.dot_general(gate_grad, gate[i], dims, preferred_element_type=F32)
        value = value + lax.dot_general(up_grad, up[i], dims, preferred_element_type=F32)
        value = value.astype(BF16)
        start = pl.multiple_of((step * per_step + i) * slots, 16)
        for rel in range(n_dp):
            held[rel, pl.ds(start, slots), :] = value[rel * slots : (rel + 1) * slots]

    @pl.when(step == pl.num_programs(0) - 1)
    def _():
        rows, half = keep_x.shape[1], keep_x.shape[2]
        for r in range(n_dp):
            rel = where[2] ^ r
            placer = placer_of(lines[rel][0:1], held.shape[1])
            token_rows = lax.dot_general(
                placer, held[rel], (((0,), (0,)), ((), ())), preferred_element_type=F32
            ).astype(BF16)
            keep_x[r] = token_rows[0:rows, 0:half]
            send_x[r] = token_rows[rows:, 0:half]
            out = send_z if r & 1 else keep_z
            out[0, r // 2] = token_rows[0:rows, half:]
            out[1, r // 2] = token_rows[rows:, half:]


def back(where, lines, parts, gate, up, rows, per_step):
    n_dp = len(parts)
    local_experts, width, hidden = gate.shape
    slots = parts[0].shape[2]
    part_spec = pl.BlockSpec((2, per_step, slots, hidden), lambda e: (0, e, 0, 0))
    weight_spec = pl.BlockSpec((per_step, width, hidden), lambda e: (e, 0, 0))
    shape_x = (n_dp, rows, width // 2)
    shape_z = (2, n_dp // 2, rows, width // 2)
    flops = 4 * local_experts * n_dp * slots * width * hidden
    return pl.pallas_call(
        functools.partial(back_kernel, n_dp),
        grid=(local_experts // per_step,),
        out_shape=[jax.ShapeDtypeStruct(s, BF16) for s in (shape_x, shape_x, shape_z, shape_z)],
        in_specs=[pl.BlockSpec(memory_space=pltpu.SMEM), whole_spec(lines.shape)]
        + [part_spec] * n_dp
        + [weight_spec] * 2,
        out_specs=[whole_spec(s) for s in (shape_x, shape_x, shape_z, shape_z)],
        scratch_shapes=[pltpu.VMEM((n_dp, local_experts * slots, width), BF16)],
        compiler_params=params(),
        cost_estimate=pl.CostEstimate(
            flops=4 * flops, bytes_accessed=2 * local_experts * width * hidden * 2, transcendentals=0
        ),
    )(where, lines, *parts, gate, up)


def weight_kernel(which, placed, h0, h1, h2, h3, out):
    for i in range(out.shape[0]):
        grad = jnp.concatenate([h[which, i] for h in (h0, h1, h2, h3)], axis=0)
        out[i] = lax.dot_general(
            placed[i], grad, (((0,), (0,)), ((), ())), preferred_element_type=F32
        ).astype(BF16)


def weight_grad(which, placed, parts, per_step):
    local_experts, slot_rows, width = placed.shape
    _, _, slots, hidden = parts[0].shape
    part_spec = pl.BlockSpec((2, per_step, slots, hidden), lambda e: (0, e, 0, 0))
    flops = 2 * local_experts * slot_rows * width * hidden
    return pl.pallas_call(
        functools.partial(weight_kernel, which),
        grid=(local_experts // per_step,),
        out_shape=jax.ShapeDtypeStruct((local_experts, width, hidden), BF16),
        in_specs=[pl.BlockSpec((per_step, slot_rows, width), lambda e: (e, 0, 0))] + [part_spec] * len(parts),
        out_specs=pl.BlockSpec((per_step, width, hidden), lambda e: (e, 0, 0)),
        compiler_params=params(),
        cost_estimate=pl.CostEstimate(
            flops=4 * flops, bytes_accessed=local_experts * width * hidden * 2, transcendentals=0
        ),
    )(placed, *parts)


def plus(first, second):
    return first.astype(F32) + second.astype(F32)


def swiglu_grads(gate_act, up_act, hidden_grad):
    sigmoid_gate = jax.nn.sigmoid(gate_act)
    up_grad = (hidden_grad * gate_act * sigmoid_gate).astype(BF16)
    gate_grad = (
        hidden_grad * up_act * sigmoid_gate * (1.0 + gate_act * (1.0 - sigmoid_gate))
    ).astype(BF16)
    return gate_grad, up_grad


def on_small_slice(tokens, cotangent, expert_ids, gate_weight, up_weight, down_weight):
    n_dp, n_x, n_t = 4, 2, 4
    k, x, t = lax.axis_index("dp"), lax.axis_index("expert"), lax.axis_index("tensor")
    width = gate_weight.shape[1]
    rows = tokens.shape[0]
    half = width // 2
    where = jnp.stack([k, x, k ^ t]).astype(jnp.int32)

    def collect(values, with_meta):
        chunks = split(where, expert_ids, values, width, n_dp, with_meta)
        blocks = []
        for rel in range(n_dp):
            mine = chunks[0] if rel == 0 else swap(chunks[rel], "dp", n_dp, rel)
            blocks += [mine, swap(mine, "expert", n_x, 1)]
        return blocks

    token_blocks = collect(tokens, True)
    grad_blocks = collect(cotangent, False)
    keep, send, placed, lines = project(where, token_blocks, None, [gate_weight, up_weight], n_dp, 2)

    def over_dp(keep, send):
        arrived = swap(send, "dp", n_dp, 1)
        near = plus(keep[:, 0], arrived[:, 0])
        far = plus(keep[:, 1], arrived[:, 1]).astype(BF16)
        return near + swap(far, "dp", n_dp, 2).astype(F32)

    acts = over_dp(keep, send)
    keep, send = project(where, grad_blocks, lines, [down_weight], n_dp, 2)
    hidden_grad = over_dp(keep, send)[0]
    part = jnp.stack(swiglu_grads(acts[0], acts[1], hidden_grad))
    far = swap(part, "dp", n_dp, 2)
    parts = [part, swap(part, "dp", n_dp, 1), far, swap(far, "dp", n_dp, 1)]

    keep_x, send_x, keep_z, send_z = back(where, lines, parts, gate_weight, up_weight, rows, 2)
    sum_x = plus(keep_x, swap(send_x, "expert", n_x, 1))
    sum_z = plus(keep_z, swap(send_z, "tensor", n_t, 1))
    from_z = swap(jnp.stack([sum_x[1], sum_x[3]]).astype(BF16), "tensor", n_t, 1)
    from_x = swap(sum_z[1].astype(BF16), "expert", n_x, 1)
    near = jnp.concatenate([plus(sum_x[0], from_z[0]), plus(sum_z[0, 0], from_x[0])], axis=1).astype(BF16)
    far = jnp.concatenate([plus(sum_x[2], from_z[1]), plus(sum_z[0, 1], from_x[1])], axis=1).astype(BF16)
    pairs = [(i, j) for i in range(n_dp) for j in range(n_t)]
    near = lax.ppermute(near, ("dp", "tensor"), [(i * n_t + j, j * n_t + i) for i, j in pairs])
    far = lax.ppermute(far, ("dp", "tensor"), [(i * n_t + j, (j ^ 2) * n_t + i) for i, j in pairs])
    grad_tokens = plus(near, far).astype(BF16)

    grad_gate = weight_grad(0, placed, parts, 2)
    grad_up = weight_grad(1, placed, parts, 2)
    return grad_tokens, grad_gate, grad_up


def bits_of(count):
    bits = []
    bit = 1
    while bit < count:
        bits.append(bit)
        bit *= 2
    return bits


def halving_sum(parts, axis, count):
    parts = dict(parts)
    for bit in bits_of(count):
        leaving = sorted(r for r in parts if r & bit)
        arrived = swap(jnp.stack([parts[r].astype(BF16) for r in leaving]), axis, count, bit)
        for at, r in enumerate(leaving):
            parts[r ^ bit] = plus(parts[r ^ bit], arrived[at])
            del parts[r]
    return parts[0]


def doubling_gather(value, axis, count):
    held = {0: value}
    for bit in reversed(bits_of(count)):
        known = sorted(held)
        arrived = swap(jnp.stack([held[r] for r in known]), axis, count, bit)
        for at, r in enumerate(known):
            held[r ^ bit] = arrived[at]
    return [held[r] for r in range(count)]


def on_any_slice(tokens, cotangent, expert_ids, gate_weight, up_weight, down_weight):
    n_dp, n_x, n_t = lax.axis_size("dp"), lax.axis_size("expert"), lax.axis_size("tensor")
    k, x, t = lax.axis_index("dp"), lax.axis_index("expert"), lax.axis_index("tensor")
    local_experts, width, hidden = gate_weight.shape
    rows = tokens.shape[0]
    slots = n_x * CAP
    ids_row = expert_ids.reshape(1, rows)
    order = jnp.arange(rows, dtype=jnp.int32)
    earlier = (expert_ids == ids_row) & (order[:, None] < order[None, :])
    position = jnp.sum(earlier.astype(jnp.int32), axis=0)
    target = ids_row[0] * CAP + position
    targets = lax.all_gather(target, ("dp", "expert"), axis=0, tiled=False).reshape(n_dp, n_x, rows)
    pair = jnp.stack([tokens, cotangent])
    placers, slot_rows = [], []
    for rel in range(n_dp):
        columns = lax.dynamic_slice_in_dim(pair, (k ^ rel) * width, width, axis=2)
        mine = columns if rel == 0 else swap(columns, "dp", n_dp, rel)
        blocks = lax.all_gather(mine, "expert", axis=1, tiled=True)
        goal = lax.dynamic_index_in_dim(targets, k ^ rel, axis=0, keepdims=False)
        expert = goal // CAP - x * local_experts
        place = jnp.arange(n_x, dtype=jnp.int32)[:, None] * CAP + goal % CAP
        row = jnp.where((expert >= 0) & (expert < local_experts), expert * slots + place, -1)
        row = row.reshape(1, n_x * rows)
        every = jnp.arange(local_experts * slots, dtype=jnp.int32)[:, None]
        placer = (every == row).astype(BF16)
        placers.append(placer)
        slot_rows.append(
            jnp.einsum("sn,and->asd", placer, blocks, preferred_element_type=F32)
            .astype(BF16)
            .reshape(2, local_experts, slots, width)
        )
    slot_rows = jnp.concatenate(slot_rows, axis=2)
    inputs, grads_in = slot_rows[0], slot_rows[1]

    def act(values, weight):
        return jnp.einsum("esd,edf->esf", values, weight, preferred_element_type=F32).astype(BF16)

    acts = jnp.stack([act(inputs, gate_weight), act(inputs, up_weight), act(grads_in, down_weight)])
    acts = acts.reshape(3, local_experts, n_dp, slots, hidden)
    acts = halving_sum({r: acts[:, :, r] for r in range(n_dp)}, "dp", n_dp)
    grads = doubling_gather(jnp.stack(swiglu_grads(acts[0], acts[1], acts[2])), "dp", n_dp)
    grads = jnp.concatenate(grads, axis=2)
    gate_grad, up_grad = grads[0], grads[1]
    partial_value = jnp.einsum("esf,edf->esd", gate_grad, gate_weight, preferred_element_type=F32)
    partial_value = partial_value + jnp.einsum("esf,edf->esd", up_grad, up_weight, preferred_element_type=F32)
    partial_value = partial_value.astype(BF16).reshape(local_experts, n_dp, slots, width)
    per_token = []
    for rel in range(n_dp):
        flat = partial_value[:, rel].reshape(local_experts * slots, width)
        spread = lax.dot_general(placers[rel], flat, (((0,), (0,)), ((), ())), preferred_element_type=F32)
        spread = spread.astype(BF16).reshape(n_x, rows, width)
        per_token.append(lax.psum_scatter(spread, "expert", scatter_dimension=0, tiled=False))
    per_token = jnp.stack(per_token)
    terms = {r: lax.dynamic_index_in_dim(per_token, k ^ t ^ r, axis=0, keepdims=False) for r in range(n_t)}
    summed = halving_sum(terms, "tensor", n_t).astype(BF16)
    summed = lax.ppermute(
        summed, ("dp", "tensor"), [(i * n_t + j, j * n_t + i) for i in range(n_dp) for j in range(n_t)]
    )
    grad_gate = jnp.einsum("esd,esf->edf", inputs, gate_grad, preferred_element_type=F32).astype(BF16)
    grad_up = jnp.einsum("esd,esf->edf", inputs, up_grad, preferred_element_type=F32).astype(BF16)
    return summed, grad_gate, grad_up


def solution(mesh):
    placed = (
        P(("dp", "expert"), None),
        P(("dp", "expert"), None),
        P(("dp", "expert"), None),
        P("expert", "dp", "tensor"),
        P("expert", "dp", "tensor"),
        P("expert", "dp", "tensor"),
    )
    sizes = tuple(mesh.shape[name] for name in ("dp", "expert", "tensor"))
    return jax.shard_map(
        on_small_slice if sizes == (4, 2, 4) else on_any_slice,
        mesh=mesh,
        in_specs=placed,
        out_specs=(
            P(("dp", "expert"), "tensor"),
            P("expert", "dp", "tensor"),
            P("expert", "dp", "tensor"),
        ),
        check_vma=False,
    )
```

profile of v0, /device:TPU:16, one launch (start us, length us, event | category | flops | bytes accessed | tf_op | source)
XLA Modules:
  0.0 150.1 jit_solution(11489543755688153947)
XLA Ops:
  3.3 1.6 %collective-permute-start.3 = (bf16[144,512]{1,0:T(8,128)(2,1)S(1)}, bf16[144,512]{1,0:T(8,128)(2,1)S(1)}, u32[]{:S(2)}, u32[]{:S(2)}) collective-permute-start(bf16[144,512]{1,0:T(8,128)(2,1)S(1)} %get-tuple-element.23), channel_id=1, source_target_pairs={{0,16},{8,24},{16,0},{24,8},{1,17},{9,25},{17,1},{25,9},{2,18},{10... | collective-permute-start | bytes 442376 | tf_op jit(solution)/shard_map/ppermute | solution.py:18
  7.2 2.8 %collective-permute-done.3.refs_4_ = bf16[144,512]{1,0:T(8,128)(2,1)S(1)} collective-permute-done((bf16[144,512]{1,0:T(8,128)(2,1)S(1)}, bf16[144,512]{1,0:T(8,128)(2,1)S(1)}, u32[]{:S(2)}, u32[]{:S(2)}) %collective-permute-start.3) | collective-permute-done | bytes 147488 | tf_op jit(solution)/shard_map/ppermute | solution.py:18
  13.7 8.4 %copy.10.refs_8_.gate = bf16[16,512,352]{2,1,0:T(8,128)(2,1)} copy(bf16[16,512,352]{1,2,0:T(8,128)(2,1)} %param.9) | data formatting | bytes 11534336 | tf_op args[3]
  22.1 8.5 %copy.11.refs_9_.up = bf16[16,512,352]{2,1,0:T(8,128)(2,1)} copy(bf16[16,512,352]{1,2,0:T(8,128)(2,1)} %param.10) | data formatting | bytes 11534336 | tf_op args[4]
  30.6 8.5 %shard_map.86 = (bf16[2,2,16,16,352]{4,3,2,1,0:T(8,128)(2,1)S(1)}, bf16[2,2,16,16,352]{4,3,2,1,0:T(8,128)(2,1)S(1)}, bf16[16,64,512]{2,1,0:T(8,128)(2,1)S(1)}, s32[4,8,256]{2,1,0:T(8,128)S(1)}) custom-call(s32[3]{0:T(128)S(1)} %pad_add_fusion.where, bf16[144,512]{1,0:T(8,128)(2,1)S(1)} %get-tuple-element.21.refs_0_, ...), custom_call_target="tpu_custom_call" | custom-call | flops 2952790016 | bytes 11534336 | tf_op jit(solution)/shard_map/pallas_call | solution.py:139
  41.3 1.5 %collective-permute-start.10 = (bf16[128,512]{1,0:T(8,128)(2,1)S(1)}, bf16[128,512]{1,0:T(8,128)(2,1)S(1)}, u32[]{:S(2)}, u32[]{:S(2)}) collective-permute-start(bf16[128,512]{1,0:T(8,128)(2,1)S(1)} %get-tuple-element.28), channel_id=1, source_target_pairs={{0,16},{8,24},{16,0},{24,8},{1,17},{9,25},{17,1},{25,9},{2,18},{10... | collective-permute-start | bytes 393224 | tf_op jit(solution)/shard_map/ppermute | solution.py:18
  44.9 2.6 %collective-permute-done.10.refs_4_ = bf16[128,512]{1,0:T(8,128)(2,1)S(1)} collective-permute-done((bf16[128,512]{1,0:T(8,128)(2,1)S(1)}, bf16[128,512]{1,0:T(8,128)(2,1)S(1)}, u32[]{:S(2)}, u32[]{:S(2)}) %collective-permute-start.10) | collective-permute-done | bytes 131104 | tf_op jit(solution)/shard_map/ppermute | solution.py:18
  49.7 8.3 %copy.13.refs_9_ = bf16[16,512,352]{2,1,0:T(8,128)(2,1)} copy(bf16[16,512,352]{1,2,0:T(8,128)(2,1)} %param.11) | data formatting | bytes 11534336 | tf_op args[5]
  58.0 6.6 %shard_map.88 = (bf16[1,2,16,16,352]{4,3,2,1,0:T(8,128)(2,1)S(1)}, bf16[1,2,16,16,352]{4,3,2,1,0:T(8,128)(2,1)S(1)}) custom-call(s32[3]{0:T(128)S(1)} %pad_add_fusion.where, bf16[128,512]{1,0:T(8,128)(2,1)S(1)} %get-tuple-element.26.refs_0_, bf16[128,512]{1,0:T(8,128)(2,1)S(1)} %collective-permute-done.7.refs_1_, ...), custom_call_target="tpu_custom_call" | custom-call | flops 1476395008 | bytes 5767168 | tf_op jit(solution)/shard_map/pallas_call | solution.py:139
  66.3 1.6 %collective-permute-start.17 = (bf16[2,16,16,352]{3,2,1,0:T(8,128)(2,1)S(1)}, bf16[2,16,16,352]{3,2,1,0:T(8,128)(2,1)S(1)}, u32[]{:S(2)}, u32[]{:S(2)}) collective-permute-start(bf16[2,16,16,352]{3,2,1,0:T(8,128)(2,1)S(1)} %fusion), channel_id=1, source_target_pairs={{0,16},{8,24},{16,0},{24,8},{1,17},{9,25},{17,1},{25,9},{2,18},{10... | collective-permute-start | bytes 1081352 | tf_op jit(solution)/shard_map/ppermute | solution.py:18
  68.5 9.8 %collective-permute-done.17 = bf16[2,16,16,352]{3,2,1,0:T(8,128)(2,1)S(1)} collective-permute-done((bf16[2,16,16,352]{3,2,1,0:T(8,128)(2,1)S(1)}, bf16[2,16,16,352]{3,2,1,0:T(8,128)(2,1)S(1)}, u32[]{:S(2)}, u32[]{:S(2)}) %collective-permute-start.17) | collective-permute-done | bytes 360480 | tf_op jit(solution)/shard_map/ppermute | solution.py:18
  79.5 2.2 %collective-permute-done.15 = bf16[1,16,16,352]{3,2,1,0:T(8,128)(2,1)S(1)} collective-permute-done((bf16[1,16,16,352]{3,2,1,0:T(8,128)(2,1)S(1)}, bf16[1,16,16,352]{3,2,1,0:T(8,128)(2,1)S(1)}, u32[]{:S(2)}, u32[]{:S(2)}) %collective-permute-start.15) | collective-permute-done | bytes 180256 | tf_op jit(solution)/shard_map/ppermute | solution.py:18
  82.0 1.6 %collective-permute-start.19 = (bf16[2,16,16,352]{3,2,1,0:T(8,128)(2,1)S(1)}, bf16[2,16,16,352]{3,2,1,0:T(8,128)(2,1)S(1)}, u32[]{:S(2)}, u32[]{:S(2)}) collective-permute-start(bf16[2,16,16,352]{3,2,1,0:T(8,128)(2,1)S(1)} %pad_maximum_fusion.h0), channel_id=1, source_target_pairs={{0,16},{8,24},{16,0},{24,8},{1,17},{9,25},{17,1},{25,9},{2,18},{10... | collective-permute-start | bytes 1081352 | tf_op jit(solution)/shard_map/ppermute | solution.py:18
  83.6 8.7 %collective-permute-done.19.h2 = bf16[2,16,16,352]{3,2,1,0:T(8,128)(2,1)S(1)} collective-permute-done((bf16[2,16,16,352]{3,2,1,0:T(8,128)(2,1)S(1)}, bf16[2,16,16,352]{3,2,1,0:T(8,128)(2,1)S(1)}, u32[]{:S(2)}, u32[]{:S(2)}) %collective-permute-start.19) | collective-permute-done | bytes 360480 | tf_op jit(solution)/shard_map/ppermute | solution.py:18
  92.3 1.7 %collective-permute-done.20.h3 = bf16[2,16,16,352]{3,2,1,0:T(8,128)(2,1)S(1)} collective-permute-done((bf16[2,16,16,352]{3,2,1,0:T(8,128)(2,1)S(1)}, bf16[2,16,16,352]{3,2,1,0:T(8,128)(2,1)S(1)}, u32[]{:S(2)}, u32[]{:S(2)}) %collective-permute-start.20) | collective-permute-done | bytes 360480 | tf_op jit(solution)/shard_map/ppermute | solution.py:18
  94.0 10.3 %shard_map.89 = (bf16[4,128,256]{2,1,0:T(8,128)(2,1)S(1)}, bf16[4,128,256]{2,1,0:T(8,128)(2,1)S(1)}, bf16[2,2,128,256]{3,2,1,0:T(8,128)(2,1)S(1)}, bf16[2,2,128,256]{3,2,1,0:T(8,128)(2,1)}) custom-call(s32[3]{0:T(128)S(1)} %pad_add_fusion.where, s32[4,8,256]{2,1,0:T(8,128)S(1)} %get-tuple-element.25.refs_8_.lines, ...), custom_call_target="tpu_custom_call" | custom-call | flops 2952790016 | bytes 11534336 | tf_op jit(solution)/shard_map/pallas_call | solution.py:194
  104.3 1.6 %collective-permute-start.23 = (bf16[2,2,128,256]{3,2,1,0:T(8,128)(2,1)}, bf16[2,2,128,256]{3,2,1,0:T(8,128)(2,1)}, u32[]{:S(2)}, u32[]{:S(2)}) collective-permute-start(bf16[2,2,128,256]{3,2,1,0:T(8,128)(2,1)} %get-tuple-element.37), channel_id=1, source_target_pairs={{0,1},{1,0},{2,3},{3,2},{4,5},{5,4},{6,7},{7,6},{8,9},{9,8},{10,11... | collective-permute-start | bytes 786440 | tf_op jit(solution)/shard_map/ppermute | solution.py:18
  107.4 5.8 %shard_map.91 = bf16[16,512,352]{2,1,0:T(8,128)(2,1)} custom-call(bf16[16,64,512]{2,1,0:T(8,128)(2,1)S(1)} %get-tuple-element.38.placed, bf16[2,16,16,352]{3,2,1,0:T(8,128)(2,1)S(1)} %pad_maximum_fusion.h0, bf16[2,16,16,352]{3,2,1,0:T(8,128)(2,1)S(1)} %collective-permute-done.18.h1, bf16[2,16,16,352]{3,2,1,0:T(8,128)(2,1)S(1)} %collective-permute-done.19.h2, ...), custom_call_target="tpu_custom_call" | custom-call | flops 1476395008 | bytes 5767168 | tf_op jit(solution)/shard_map/pallas_call | solution.py:223
  113.2 8.4 %copy.20 = bf16[16,512,352]{1,2,0:T(8,128)(2,1)} copy(bf16[16,512,352]{2,1,0:T(8,128)(2,1)} %shard_map.91) | data formatting | bytes 11534336
  124.8 2.9 %collective-permute-done.24 = bf16[2,128,256]{2,1,0:T(8,128)(2,1)S(1)} collective-permute-done((bf16[2,128,256]{2,1,0:T(8,128)(2,1)S(1)}, bf16[2,128,256]{2,1,0:T(8,128)(2,1)S(1)}, u32[]{:S(2)}, u32[]{:S(2)}) %collective-permute-start.24) | collective-permute-done | bytes 131104 | tf_op jit(solution)/shard_map/ppermute | solution.py:18
  127.7 1.7 %collective-permute-done.22 = bf16[2,128,256]{2,1,0:T(8,128)(2,1)S(1)} collective-permute-done((bf16[2,128,256]{2,1,0:T(8,128)(2,1)S(1)}, bf16[2,128,256]{2,1,0:T(8,128)(2,1)S(1)}, u32[]{:S(2)}, u32[]{:S(2)}) %collective-permute-start.22) | collective-permute-done | bytes 131104 | tf_op jit(solution)/shard_map/ppermute | solution.py:18
  129.8 5.5 %collective-permute-start.25 = (bf16[128,512]{1,0:T(8,128)(2,1)S(1)}, bf16[128,512]{1,0:T(8,128)(2,1)S(1)}, u32[]{:S(2)}, u32[]{:S(2)}) collective-permute-start(bf16[128,512]{1,0:T(8,128)(2,1)S(1)} %pad_maximum_fusion.2), channel_id=1, source_target_pairs={{0,0},{1,8},{2,16},{3,24},{8,1},{9,9},{10,17},{11,25},{16,2},{17,1... | collective-permute-start | bytes 393224 | tf_op jit(solution)/shard_map/ppermute | solution.py:290
  135.2 5.8 %shard_map.90 = bf16[16,512,352]{2,1,0:T(8,128)(2,1)} custom-call(bf16[16,64,512]{2,1,0:T(8,128)(2,1)S(1)} %get-tuple-element.38.placed, bf16[2,16,16,352]{3,2,1,0:T(8,128)(2,1)S(1)} %pad_maximum_fusion.h0, bf16[2,16,16,352]{3,2,1,0:T(8,128)(2,1)S(1)} %collective-permute-done.18.h1, bf16[2,16,16,352]{3,2,1,0:T(8,128)(2,1)S(1)} %collective-permute-done.19.h2, ...), custom_call_target="tpu_custom_call" | custom-call | flops 1476395008 | bytes 5767168 | tf_op jit(solution)/shard_map/pallas_call | solution.py:223
  141.0 8.4 %copy.19 = bf16[16,512,352]{1,2,0:T(8,128)(2,1)} copy(bf16[16,512,352]{2,1,0:T(8,128)(2,1)} %shard_map.90) | data formatting | bytes 11534336
  (64 shorter events, 24.5 us)
Async XLA Ops:
  3.2 3.4 %collective-permute-start.1 = (bf16[144,512]{1,0:T(8,128)(2,1)S(1)}, bf16[144,512]{1,0:T(8,128)(2,1)S(1)}, u32[]{:S(2)}, u32[]{:S(2)}) collective-permute-start(bf16[144,512]{1,0:T(8,128)(2,1)S(1)} %get-tuple-element.22), channel_id=1, source_target_pairs={{0,8},{8,0},{16,24},{24,16},{1,9},{9,1},{17,25},{25,17},{2,10},{10... | collective-permute-start | bytes 442376 | tf_op jit(solution)/shard_map/ppermute | solution.py:18
  3.3 6.7 %collective-permute-start.3 = (bf16[144,512]{1,0:T(8,128)(2,1)S(1)}, bf16[144,512]{1,0:T(8,128)(2,1)S(1)}, u32[]{:S(2)}, u32[]{:S(2)}) collective-permute-start(bf16[144,512]{1,0:T(8,128)(2,1)S(1)} %get-tuple-element.23), channel_id=1, source_target_pairs={{0,16},{8,24},{16,0},{24,8},{1,17},{9,25},{17,1},{25,9},{2,18},{10... | collective-permute-start | bytes 442376 | tf_op jit(solution)/shard_map/ppermute | solution.py:18
  4.8 7.4 %collective-permute-start.5 = (bf16[144,512]{1,0:T(8,128)(2,1)S(1)}, bf16[144,512]{1,0:T(8,128)(2,1)S(1)}, u32[]{:S(2)}, u32[]{:S(2)}) collective-permute-start(bf16[144,512]{1,0:T(8,128)(2,1)S(1)} %get-tuple-element.24), channel_id=1, source_target_pairs={{0,24},{8,16},{16,8},{24,0},{1,25},{9,17},{17,9},{25,1},{2,26},{10... | collective-permute-start | bytes 442376 | tf_op jit(solution)/shard_map/ppermute | solution.py:18
  5.1 25.5 %collective-permute-start = (bf16[144,512]{1,0:T(8,128)(2,1)S(1)}, bf16[144,512]{1,0:T(8,128)(2,1)S(1)}, u32[]{:S(2)}, u32[]{:S(2)}) collective-permute-start(bf16[144,512]{1,0:T(8,128)(2,1)S(1)} %get-tuple-element.21.refs_0_), channel_id=1, source_target_pairs={{0,4},{4,0},{1,5},{5,1},{2,6},{6,2},{3,7},{7,3},{8,12},{12,8},{9,1... | collective-permute-start | bytes 442376 | tf_op jit(solution)/shard_map/ppermute | solution.py:18
  6.6 24.0 %collective-permute-start.2 = (bf16[144,512]{1,0:T(8,128)(2,1)S(1)}, bf16[144,512]{1,0:T(8,128)(2,1)S(1)}, u32[]{:S(2)}, u32[]{:S(2)}) collective-permute-start(bf16[144,512]{1,0:T(8,128)(2,1)S(1)} %collective-permute-done.1.refs_2_), channel_id=1, source_target_pairs={{0,4},{4,0},{1,5},{5,1},{2,6},{6,2},{3,7},{7,3},{8,12},{12,8},{9,1... | collective-permute-start | bytes 442376 | tf_op jit(solution)/shard_map/ppermute | solution.py:18
  10.0 20.6 %collective-permute-start.4 = (bf16[144,512]{1,0:T(8,128)(2,1)S(1)}, bf16[144,512]{1,0:T(8,128)(2,1)S(1)}, u32[]{:S(2)}, u32[]{:S(2)}) collective-permute-start(bf16[144,512]{1,0:T(8,128)(2,1)S(1)} %collective-permute-done.3.refs_4_), channel_id=1, source_target_pairs={{0,4},{4,0},{1,5},{5,1},{2,6},{6,2},{3,7},{7,3},{8,12},{12,8},{9,1... | collective-permute-start | bytes 442376 | tf_op jit(solution)/shard_map/ppermute | solution.py:18
  12.2 18.4 %collective-permute-start.6 = (bf16[144,512]{1,0:T(8,128)(2,1)S(1)}, bf16[144,512]{1,0:T(8,128)(2,1)S(1)}, u32[]{:S(2)}, u32[]{:S(2)}) collective-permute-start(bf16[144,512]{1,0:T(8,128)(2,1)S(1)} %collective-permute-done.5.refs_6_), channel_id=1, source_target_pairs={{0,4},{4,0},{1,5},{5,1},{2,6},{6,2},{3,7},{7,3},{8,12},{12,8},{9,1... | collective-permute-start | bytes 442376 | tf_op jit(solution)/shard_map/ppermute | solution.py:18
  40.1 25.1 %collective-permute-start.16 = (bf16[2,2,16,16,352]{4,3,2,0,1:T(8,128)(2,1)}, bf16[2,2,16,16,352]{4,3,2,0,1:T(8,128)(2,1)}, u32[]{:S(2)}, u32[]{:S(2)}) collective-permute-start(bf16[2,2,16,16,352]{4,3,2,0,1:T(8,128)(2,1)} %copy.15), channel_id=1, source_target_pairs={{0,8},{8,0},{16,24},{24,16},{1,9},{9,1},{17,25},{25,17},{2,10},{10... | collective-permute-start | bytes 2162696 | tf_op jit(solution)/shard_map/ppermute | solution.py:18
  41.3 6.3 %collective-permute-start.10 = (bf16[128,512]{1,0:T(8,128)(2,1)S(1)}, bf16[128,512]{1,0:T(8,128)(2,1)S(1)}, u32[]{:S(2)}, u32[]{:S(2)}) collective-permute-start(bf16[128,512]{1,0:T(8,128)(2,1)S(1)} %get-tuple-element.28), channel_id=1, source_target_pairs={{0,16},{8,24},{16,0},{24,8},{1,17},{9,25},{17,1},{25,9},{2,18},{10... | collective-permute-start | bytes 393224 | tf_op jit(solution)/shard_map/ppermute | solution.py:18
  42.8 6.4 %collective-permute-start.12 = (bf16[128,512]{1,0:T(8,128)(2,1)S(1)}, bf16[128,512]{1,0:T(8,128)(2,1)S(1)}, u32[]{:S(2)}, u32[]{:S(2)}) collective-permute-start(bf16[128,512]{1,0:T(8,128)(2,1)S(1)} %get-tuple-element.29), channel_id=1, source_target_pairs={{0,24},{8,16},{16,8},{24,0},{1,25},{9,17},{17,9},{25,1},{2,26},{10... | collective-permute-start | bytes 393224 | tf_op jit(solution)/shard_map/ppermute | solution.py:18
  42.9 15.1 %collective-permute-start.7 = (bf16[128,512]{1,0:T(8,128)(2,1)S(1)}, bf16[128,512]{1,0:T(8,128)(2,1)S(1)}, u32[]{:S(2)}, u32[]{:S(2)}) collective-permute-start(bf16[128,512]{1,0:T(8,128)(2,1)S(1)} %get-tuple-element.26.refs_0_), channel_id=1, source_target_pairs={{0,4},{4,0},{1,5},{5,1},{2,6},{6,2},{3,7},{7,3},{8,12},{12,8},{9,1... | collective-permute-start | bytes 393224 | tf_op jit(solution)/shard_map/ppermute | solution.py:18
  43.4 14.6 %collective-permute-start.9 = (bf16[128,512]{1,0:T(8,128)(2,1)S(1)}, bf16[128,512]{1,0:T(8,128)(2,1)S(1)}, u32[]{:S(2)}, u32[]{:S(2)}) collective-permute-start(bf16[128,512]{1,0:T(8,128)(2,1)S(1)} %collective-permute-done.8.refs_2_), channel_id=1, source_target_pairs={{0,4},{4,0},{1,5},{5,1},{2,6},{6,2},{3,7},{7,3},{8,12},{12,8},{9,1... | collective-permute-start | bytes 393224 | tf_op jit(solution)/shard_map/ppermute | solution.py:18
  47.6 10.4 %collective-permute-start.11 = (bf16[128,512]{1,0:T(8,128)(2,1)S(1)}, bf16[128,512]{1,0:T(8,128)(2,1)S(1)}, u32[]{:S(2)}, u32[]{:S(2)}) collective-permute-start(bf16[128,512]{1,0:T(8,128)(2,1)S(1)} %collective-permute-done.10.refs_4_), channel_id=1, source_target_pairs={{0,4},{4,0},{1,5},{5,1},{2,6},{6,2},{3,7},{7,3},{8,12},{12,8},{9,1... | collective-permute-start | bytes 393224 | tf_op jit(solution)/shard_map/ppermute | solution.py:18
  49.1 8.9 %collective-permute-start.13 = (bf16[128,512]{1,0:T(8,128)(2,1)S(1)}, bf16[128,512]{1,0:T(8,128)(2,1)S(1)}, u32[]{:S(2)}, u32[]{:S(2)}) collective-permute-start(bf16[128,512]{1,0:T(8,128)(2,1)S(1)} %collective-permute-done.12.refs_6_), channel_id=1, source_target_pairs={{0,4},{4,0},{1,5},{5,1},{2,6},{6,2},{3,7},{7,3},{8,12},{12,8},{9,1... | collective-permute-start | bytes 393224 | tf_op jit(solution)/shard_map/ppermute | solution.py:18
  66.3 12.0 %collective-permute-start.17 = (bf16[2,16,16,352]{3,2,1,0:T(8,128)(2,1)S(1)}, bf16[2,16,16,352]{3,2,1,0:T(8,128)(2,1)S(1)}, u32[]{:S(2)}, u32[]{:S(2)}) collective-permute-start(bf16[2,16,16,352]{3,2,1,0:T(8,128)(2,1)S(1)} %fusion), channel_id=1, source_target_pairs={{0,16},{8,24},{16,0},{24,8},{1,17},{9,25},{17,1},{25,9},{2,18},{10... | collective-permute-start | bytes 1081352 | tf_op jit(solution)/shard_map/ppermute | solution.py:18
  68.0 13.7 %collective-permute-start.15 = (bf16[1,16,16,352]{3,2,1,0:T(8,128)(2,1)S(1)}, bf16[1,16,16,352]{3,2,1,0:T(8,128)(2,1)S(1)}, u32[]{:S(2)}, u32[]{:S(2)}) collective-permute-start(bf16[1,16,16,352]{3,2,1,0:T(8,128)(2,1)S(1)} %fusion.4), channel_id=1, source_target_pairs={{0,16},{8,24},{16,0},{24,8},{1,17},{9,25},{17,1},{25,9},{2,18},{10... | collective-permute-start | bytes 540680 | tf_op jit(solution)/shard_map/ppermute | solution.py:18
  82.0 10.3 %collective-permute-start.19 = (bf16[2,16,16,352]{3,2,1,0:T(8,128)(2,1)S(1)}, bf16[2,16,16,352]{3,2,1,0:T(8,128)(2,1)S(1)}, u32[]{:S(2)}, u32[]{:S(2)}) collective-permute-start(bf16[2,16,16,352]{3,2,1,0:T(8,128)(2,1)S(1)} %pad_maximum_fusion.h0), channel_id=1, source_target_pairs={{0,16},{8,24},{16,0},{24,8},{1,17},{9,25},{17,1},{25,9},{2,18},{10... | collective-permute-start | bytes 1081352 | tf_op jit(solution)/shard_map/ppermute | solution.py:18
  83.6 8.7 %collective-permute-start.18 = (bf16[2,16,16,352]{3,2,1,0:T(8,128)(2,1)S(1)}, bf16[2,16,16,352]{3,2,1,0:T(8,128)(2,1)S(1)}, u32[]{:S(2)}, u32[]{:S(2)}) collective-permute-start(bf16[2,16,16,352]{3,2,1,0:T(8,128)(2,1)S(1)} %pad_maximum_fusion.h0), channel_id=1, source_target_pairs={{0,8},{8,0},{16,24},{24,16},{1,9},{9,1},{17,25},{25,17},{2,10},{10... | collective-permute-start | bytes 1081352 | tf_op jit(solution)/shard_map/ppermute | solution.py:18
  104.3 17.3 %collective-permute-start.23 = (bf16[2,2,128,256]{3,2,1,0:T(8,128)(2,1)}, bf16[2,2,128,256]{3,2,1,0:T(8,128)(2,1)}, u32[]{:S(2)}, u32[]{:S(2)}) collective-permute-start(bf16[2,2,128,256]{3,2,1,0:T(8,128)(2,1)} %get-tuple-element.37), channel_id=1, source_target_pairs={{0,1},{1,0},{2,3},{3,2},{4,5},{5,4},{6,7},{7,6},{8,9},{9,8},{10,11... | collective-permute-start | bytes 786440 | tf_op jit(solution)/shard_map/ppermute | solution.py:18
  105.9 17.3 %collective-permute-start.21 = (bf16[4,128,256]{2,1,0:T(8,128)(2,1)S(1)}, bf16[4,128,256]{2,1,0:T(8,128)(2,1)}, u32[]{:S(2)}, u32[]{:S(2)}) collective-permute-start(bf16[4,128,256]{2,1,0:T(8,128)(2,1)S(1)} %get-tuple-element.35), channel_id=1, source_target_pairs={{0,4},{4,0},{1,5},{5,1},{2,6},{6,2},{3,7},{7,3},{8,12},{12,8},{9,1... | collective-permute-start | bytes 786440 | tf_op jit(solution)/shard_map/ppermute | solution.py:18
  122.6 5.0 %collective-permute-start.24 = (bf16[2,128,256]{2,1,0:T(8,128)(2,1)S(1)}, bf16[2,128,256]{2,1,0:T(8,128)(2,1)S(1)}, u32[]{:S(2)}, u32[]{:S(2)}) collective-permute-start(bf16[2,128,256]{2,1,0:T(8,128)(2,1)S(1)} %fusion.5), channel_id=1, source_target_pairs={{0,4},{4,0},{1,5},{5,1},{2,6},{6,2},{3,7},{7,3},{8,12},{12,8},{9,1... | collective-permute-start | bytes 393224 | tf_op jit(solution)/shard_map/ppermute | solution.py:18
  124.3 5.1 %collective-permute-start.22 = (bf16[2,128,256]{2,1,0:T(8,128)(2,1)S(1)}, bf16[2,128,256]{2,1,0:T(8,128)(2,1)S(1)}, u32[]{:S(2)}, u32[]{:S(2)}) collective-permute-start(bf16[2,128,256]{2,1,0:T(8,128)(2,1)S(1)} %pad_maximum_fusion.1), channel_id=1, source_target_pairs={{0,1},{1,0},{2,3},{3,2},{4,5},{5,4},{6,7},{7,6},{8,9},{9,8},{10,11... | collective-permute-start | bytes 393224 | tf_op jit(solution)/shard_map/ppermute | solution.py:18
  129.4 20.0 %collective-permute-start.26 = (bf16[128,512]{1,0:T(8,128)(2,1)S(1)}, bf16[128,512]{1,0:T(8,128)(2,1)S(1)}, u32[]{:S(2)}, u32[]{:S(2)}) collective-permute-start(bf16[128,512]{1,0:T(8,128)(2,1)S(1)} %pad_maximum_fusion.3), channel_id=1, source_target_pairs={{0,16},{1,24},{2,0},{3,8},{8,17},{9,25},{10,1},{11,9},{16,18},{17,... | collective-permute-start | bytes 393224 | tf_op jit(solution)/shard_map/ppermute | solution.py:291
  129.8 19.7 %collective-permute-start.25 = (bf16[128,512]{1,0:T(8,128)(2,1)S(1)}, bf16[128,512]{1,0:T(8,128)(2,1)S(1)}, u32[]{:S(2)}, u32[]{:S(2)}) collective-permute-start(bf16[128,512]{1,0:T(8,128)(2,1)S(1)} %pad_maximum_fusion.2), channel_id=1, source_target_pairs={{0,0},{1,8},{2,16},{3,24},{8,1},{9,9},{10,17},{11,25},{16,2},{17,1... | collective-permute-start | bytes 393224 | tf_op jit(solution)/shard_map/ppermute | solution.py:290
  (5 other events, 18.2 us)
where the time goes:
time: 152 us; the launch traced here: 150 us
  local copies, waits for them, and re-layouts  44.9 us (30%)
  Pallas kernels  38.3 us (25%)
  waiting for transfers between devices  34.2 us (23%)
  starting transfers between devices  26.5 us (17%)
  other arithmetic  5.47 us (4%)
    unnamed x10, local copies, waits for them, and re-layouts  43.9 us
    ppermute x25, waiting for transfers between devices, swap(): return lax.ppermute(value, axis, [(i, i ^ bit) for i in range(count)])  34.2 us
    ppermute x25, starting transfers between devices, swap(): return lax.ppermute(value, axis, [(i, i ^ bit) for i in range(count)])  20.7 us
    pallas_call x2, Pallas kernels, project(): pl.pallas_call(functools.partial(project_kernel, n_dp, count, first), gri...  15.1 us
    pallas_call x2, Pallas kernels, weight_grad(): pl.pallas_call(functools.partial(weight_kernel, which), grid=(local_exper...  11.5 us
    pallas_call x1, Pallas kernels, back(): pl.pallas_call(functools.partial(back_kernel, n_dp), grid=(local_experts...  10.3 us
    ppermute x1, starting transfers between devices, on_small_slice(): lax.ppermute(near, ('dp', 'tensor'), [(i * n_t + j, j * n_t + i) for i, j...  5.45 us
  transfers between devices with their start and end apart: 27, of which 10 were waited for; matrix products, arithmetic and copies ran while one was open for 31% of the time, Pallas kernels for 12%

commit v1 on v0

--- a/solution.py
+++ b/solution.py
@@ -26,42 +26,41 @@
     return pltpu.CompilerParams(vmem_limit_bytes=VMEM_LIMIT)
 
 
-def split_kernel(width, n_dp, where, ids, rows_ref, *outs):
+def split_kernel(width, n_dp, where, ids, tokens, cotangent, *outs):
     k, x = where[0], where[1]
-    rows = rows_ref.shape[0]
-    for rel in range(n_dp):
-        start = pl.multiple_of((k ^ rel) * width, 128)
-        outs[rel][0:rows, :] = rows_ref[:, pl.ds(start, width)]
-    if outs[0].shape[0] == rows:
-        return
-    column = ids[...]
+    rows = tokens.shape[0]
+    along = ids[...].astype(F32)
     line = lax.broadcasted_iota(jnp.int32, (rows, rows), 0)
     lane = lax.broadcasted_iota(jnp.int32, (rows, rows), 1)
-    named = jnp.broadcast_to(column, (rows, rows)).astype(F32)
-    along = jnp.sum(jnp.where(line == lane, named, 0.0), axis=0, keepdims=True)
-    earlier = jnp.where((named == along) & (line < lane), 1.0, 0.0)
+    named = jnp.broadcast_to(along, (rows, rows))
+    down = jnp.sum(jnp.where(line == lane, named, 0.0), axis=1, keepdims=True)
+    earlier = jnp.where((named == down) & (line < lane), 1.0, 0.0)
     place = jnp.sum(earlier, axis=0, keepdims=True) + (x * CAP).astype(F32)
     at = lax.broadcasted_iota(jnp.int32, (META, rows), 0)
     meta = jnp.where(at == 0, along, jnp.where(at == 1, place, 0.0)).astype(BF16)
     for rel in range(n_dp):
+        start = pl.multiple_of((k ^ rel) * width, 128)
+        outs[rel][0:rows, :] = tokens[:, pl.ds(start, width)]
         outs[rel][rows:, :] = jnp.zeros((META, width), BF16)
         outs[rel][rows:, 0:rows] = meta
-
-
-def split(where, ids, values, width, n_dp, with_meta):
-    rows = values.shape[0]
-    tall = rows + META if with_meta else rows
+        outs[n_dp + rel][...] = cotangent[:, pl.ds(start, width)]
+
+
+def split(where, ids, tokens, cotangent, width, n_dp):
+    rows = tokens.shape[0]
+    tall, low = (rows + META, width), (rows, width)
     return pl.pallas_call(
         functools.partial(split_kernel, width, n_dp),
-        out_shape=[jax.ShapeDtypeStruct((tall, width), BF16)] * n_dp,
+        out_shape=[jax.ShapeDtypeStruct(s, BF16) for s in [tall] * n_dp + [low] * n_dp],
         in_specs=[
             pl.BlockSpec(memory_space=pltpu.SMEM),
             whole_spec(ids.shape),
-            whole_spec(values.shape),
+            whole_spec(tokens.shape),
+            whole_spec(cotangent.shape),
         ],
-        out_specs=[whole_spec((tall, width))] * n_dp,
+        out_specs=[whole_spec(s) for s in [tall] * n_dp + [low] * n_dp],
         compiler_params=params(),
-    )(where, ids, values)
+    )(where, ids, tokens, cotangent)
 
 
 def placer_of(row, slot_count):
@@ -69,8 +68,8 @@
     return (every == row).astype(F32).astype(BF16)
 
 
-def project_kernel(n_dp, weights, first, where, *refs):
-    blocks, refs = refs[: 2 * n_dp], refs[2 * n_dp :]
+def project_kernel(n_dp, weights, first, after, where, *refs):
+    blocks, refs = refs[: 2 * n_dp], refs[2 * n_dp + after :]
     if not first:
         lines, refs = refs[0], refs[1:]
     weight_refs, refs = refs[:weights], refs[weights:]
@@ -105,30 +104,34 @@
     for i in range(per_step):
         mine = placed[step * per_step + i]
         for w in range(weights):
-            act = jnp.dot(mine, weight_refs[w][i], preferred_element_type=F32).astype(BF16)
+            act = lax.dot_general(
+                mine, weight_refs[w][i], (((1,), (1,)), ((), ())), preferred_element_type=F32
+            ).astype(BF16)
             for rel in range(n_dp):
                 out = send if rel & 1 else keep
-                out[w, rel // 2, i] = act[rel * slots : (rel + 1) * slots]
-
-
-def project(where, blocks, lines, weights, n_dp, per_step):
+                out[rel // 2, w, i] = act[rel * slots : (rel + 1) * slots]
+
+
+def project(where, blocks, lines, weights, n_dp, per_step, after=()):
     first = lines is None
-    local_experts, width, hidden = weights[0].shape
+    local_experts, hidden, width = weights[0].shape
     slots = 2 * CAP
     rows = blocks[0].shape[0] - (META if first else 0)
     count = len(weights)
-    act = (count, n_dp // 2, local_experts, slots, hidden)
-    act_block = (count, n_dp // 2, per_step, slots, hidden)
+    act = (n_dp // 2, count, local_experts, slots, hidden)
+    act_block = (n_dp // 2, count, per_step, slots, hidden)
     act_spec = pl.BlockSpec(act_block, lambda e: (0, 0, e, 0, 0))
     placed = (local_experts, n_dp * slots, width)
     line = (n_dp, 8, 2 * rows)
-    weight_spec = pl.BlockSpec((per_step, width, hidden), lambda e: (e, 0, 0))
+    weight_spec = pl.BlockSpec((per_step, hidden, width), lambda e: (e, 0, 0))
     out_shape = [jax.ShapeDtypeStruct(act, BF16), jax.ShapeDtypeStruct(act, BF16)]
     out_specs = [act_spec, act_spec]
     scratch = []
     operands = [where, *blocks]
     in_specs = [pl.BlockSpec(memory_space=pltpu.SMEM)] + [whole_spec(b.shape) for b in blocks]
     if first:
+        operands += after
+        in_specs += [pl.BlockSpec(memory_space=pl.ANY)] * len(after)
         out_shape += [jax.ShapeDtypeStruct(placed, BF16), jax.ShapeDtypeStruct(line, jnp.int32)]
         out_specs += [whole_spec(placed), whole_spec(line)]
     else:
@@ -137,7 +140,7 @@
         scratch.append(pltpu.VMEM(placed, BF16))
     flops = 2 * count * local_experts * n_dp * slots * width * hidden
     return pl.pallas_call(
-        functools.partial(project_kernel, n_dp, count, first),
+        functools.partial(project_kernel, n_dp, count, first, len(after)),
         grid=(local_experts // per_step,),
         out_shape=out_shape,
         in_specs=in_specs + [weight_spec] * count,
@@ -158,9 +161,8 @@
     for i in range(per_step):
         gate_grad = jnp.concatenate([h[0, i] for h in held_hidden], axis=0)
         up_grad = jnp.concatenate([h[1, i] for h in held_hidden], axis=0)
-        dims = (((1,), (1,)), ((), ()))
-        value = lax.dot_general(gate_grad, gate[i], dims, preferred_element_type=F32)
-        value = value + lax.dot_general(up_grad, up[i], dims, preferred_element_type=F32)
+        value = jnp.dot(gate_grad, gate[i], preferred_element_type=F32)
+        value = value + jnp.dot(up_grad, up[i], preferred_element_type=F32)
         value = value.astype(BF16)
         start = pl.multiple_of((step * per_step + i) * slots, 16)
         for rel in range(n_dp):
@@ -184,10 +186,10 @@
 
 def back(where, lines, parts, gate, up, rows, per_step):
     n_dp = len(parts)
-    local_experts, width, hidden = gate.shape
+    local_experts, hidden, width = gate.shape
     slots = parts[0].shape[2]
     part_spec = pl.BlockSpec((2, per_step, slots, hidden), lambda e: (0, e, 0, 0))
-    weight_spec = pl.BlockSpec((per_step, width, hidden), lambda e: (e, 0, 0))
+    weight_spec = pl.BlockSpec((per_step, hidden, width), lambda e: (e, 0, 0))
     shape_x = (n_dp, rows, width // 2)
     shape_z = (2, n_dp // 2, rows, width // 2)
     flops = 4 * local_experts * n_dp * slots * width * hidden
@@ -211,7 +213,7 @@
     for i in range(out.shape[0]):
         grad = jnp.concatenate([h[which, i] for h in (h0, h1, h2, h3)], axis=0)
         out[i] = lax.dot_general(
-            placed[i], grad, (((0,), (0,)), ((), ())), preferred_element_type=F32
+            grad, placed[i], (((0,), (0,)), ((), ())), preferred_element_type=F32
         ).astype(BF16)
 
 
@@ -223,9 +225,9 @@
     return pl.pallas_call(
         functools.partial(weight_kernel, which),
         grid=(local_experts // per_step,),
-        out_shape=jax.ShapeDtypeStruct((local_experts, width, hidden), BF16),
+        out_shape=jax.ShapeDtypeStruct((local_experts, hidden, width), BF16),
         in_specs=[pl.BlockSpec((per_step, slot_rows, width), lambda e: (e, 0, 0))] + [part_spec] * len(parts),
-        out_specs=pl.BlockSpec((per_step, width, hidden), lambda e: (e, 0, 0)),
+        out_specs=pl.BlockSpec((per_step, hidden, width), lambda e: (e, 0, 0)),
         compiler_params=params(),
         cost_estimate=pl.CostEstimate(
             flops=4 * flops, bytes_accessed=local_experts * width * hidden * 2, transcendentals=0
@@ -254,22 +256,28 @@
     half = width // 2
     where = jnp.stack([k, x, k ^ t]).astype(jnp.int32)
 
-    def collect(values, with_meta):
-        chunks = split(where, expert_ids, values, width, n_dp, with_meta)
+    chunks = split(where, expert_ids.reshape(1, rows), tokens, cotangent, width, n_dp)
+
+    def collect(chunks):
         blocks = []
         for rel in range(n_dp):
             mine = chunks[0] if rel == 0 else swap(chunks[rel], "dp", n_dp, rel)
             blocks += [mine, swap(mine, "expert", n_x, 1)]
         return blocks
 
-    token_blocks = collect(tokens, True)
-    grad_blocks = collect(cotangent, False)
-    keep, send, placed, lines = project(where, token_blocks, None, [gate_weight, up_weight], n_dp, 2)
+    token_blocks = collect(chunks[:n_dp])
+    grad_blocks = collect(chunks[n_dp:])
+    gate_weight, up_weight, down_weight = (
+        jnp.swapaxes(weight, 1, 2) for weight in (gate_weight, up_weight, down_weight)
+    )
+    keep, send, placed, lines = project(
+        where, token_blocks, None, [gate_weight, up_weight], n_dp, 2, after=grad_blocks[::2]
+    )
 
     def over_dp(keep, send):
         arrived = swap(send, "dp", n_dp, 1)
-        near = plus(keep[:, 0], arrived[:, 0])
-        far = plus(keep[:, 1], arrived[:, 1]).astype(BF16)
+        near = plus(keep[0], arrived[0])
+        far = plus(keep[1], arrived[1]).astype(BF16)
         return near + swap(far, "dp", n_dp, 2).astype(F32)
 
     acts = over_dp(keep, send)
@@ -291,8 +299,8 @@
     far = lax.ppermute(far, ("dp", "tensor"), [(i * n_t + j, (j ^ 2) * n_t + i) for i, j in pairs])
     grad_tokens = plus(near, far).astype(BF16)
 
-    grad_gate = weight_grad(0, placed, parts, 2)
-    grad_up = weight_grad(1, placed, parts, 2)
+    grad_gate = jnp.swapaxes(weight_grad(0, placed, parts, 2), 1, 2)
+    grad_up = jnp.swapaxes(weight_grad(1, placed, parts, 2), 1, 2)
     return grad_tokens, grad_gate, grad_up
 
 

time: 152 us -> 125 us (0.82)
  the two profiles are of different devices: /device:TPU:16 before, /device:TPU:0 now
where the time goes in v1:
time: 125 us; the launch traced here: 124 us
  waiting for transfers between devices  50.9 us (41%)
  Pallas kernels  35.6 us (28%)
  starting transfers between devices  32.8 us (26%)
  local copies, waits for them, and re-layouts  2.77 us (2%)
  other arithmetic  1.6 us (1%)
    ppermute x25, waiting for transfers between devices, swap(): return lax.ppermute(value, axis, [(i, i ^ bit) for i in range(count)])  45.7 us
    ppermute x25, starting transfers between devices, swap(): return lax.ppermute(value, axis, [(i, i ^ bit) for i in range(count)])  26.7 us
    pallas_call x2, Pallas kernels, project(): pl.pallas_call(functools.partial(project_kernel, n_dp, count, first, len(...  15.8 us
    pallas_call x2, Pallas kernels, weight_grad(): pl.pallas_call(functools.partial(weight_kernel, which), grid=(local_exper...  10.9 us
    pallas_call x1, Pallas kernels, back(): pl.pallas_call(functools.partial(back_kernel, n_dp), grid=(local_experts...  8.31 us
    ppermute x1, starting transfers between devices, on_small_slice(): lax.ppermute(far, ('dp', 'tensor'), [(i * n_t + j, (j ^ 2) * n_t + i) for...  5.35 us
    ppermute x1, waiting for transfers between devices, on_small_slice(): lax.ppermute(far, ('dp', 'tensor'), [(i * n_t + j, (j ^ 2) * n_t + i) for...  5.2 us
    unnamed x6, local copies, waits for them, and re-layouts  2.74 us
  transfers between devices with their start and end apart: 27, of which 17 were waited for; matrix products, arithmetic and copies ran while one was open for 0% of the time, Pallas kernels for 14%

profile of v1, /device:TPU:0, one launch (start us, length us, event | category | flops | bytes accessed | tf_op | source)
XLA Modules:
  0.0 124.5 jit_solution(6228922750711566327)
XLA Ops:
  4.6 2.6 %collective-permute-start.3 = (bf16[144,512]{1,0:T(8,128)(2,1)S(1)}, bf16[144,512]{1,0:T(8,128)(2,1)S(1)}, u32[]{:S(2)}, u32[]{:S(2)}) collective-permute-start(bf16[144,512]{1,0:T(8,128)(2,1)S(1)} %get-tuple-element.23), channel_id=1, source_target_pairs={{0,16},{8,24},{16,0},{24,8},{1,17},{9,25},{17,1},{25,9},{2,18},{10... | collective-permute-start | bytes 442376 | tf_op jit(solution)/shard_map/ppermute | solution.py:18
  7.4 1.9 %collective-permute-start.8 = (bf16[128,512]{1,0:T(8,128)(2,1)S(1)}, bf16[128,512]{1,0:T(8,128)(2,1)S(1)}, u32[]{:S(2)}, u32[]{:S(2)}) collective-permute-start(bf16[128,512]{1,0:T(8,128)(2,1)S(1)} %get-tuple-element.27), channel_id=1, source_target_pairs={{0,16},{8,24},{16,0},{24,8},{1,17},{9,25},{17,1},{25,9},{2,18},{10... | collective-permute-start | bytes 393224 | tf_op jit(solution)/shard_map/ppermute | solution.py:18
  11.9 1.9 %collective-permute-start.4 = (bf16[144,512]{1,0:T(8,128)(2,1)S(1)}, bf16[144,512]{1,0:T(8,128)(2,1)S(1)}, u32[]{:S(2)}, u32[]{:S(2)}) collective-permute-start(bf16[144,512]{1,0:T(8,128)(2,1)S(1)} %collective-permute-done.3.refs_4_), channel_id=1, source_target_pairs={{0,4},{4,0},{1,5},{5,1},{2,6},{6,2},{3,7},{7,3},{8,12},{12,8},{9,1... | collective-permute-start | bytes 442376 | tf_op jit(solution)/shard_map/ppermute | solution.py:18
  14.6 1.5 %collective-permute-start.6 = (bf16[144,512]{1,0:T(8,128)(2,1)S(1)}, bf16[144,512]{1,0:T(8,128)(2,1)S(1)}, u32[]{:S(2)}, u32[]{:S(2)}) collective-permute-start(bf16[144,512]{1,0:T(8,128)(2,1)S(1)} %collective-permute-done.5.refs_6_), channel_id=1, source_target_pairs={{0,4},{4,0},{1,5},{5,1},{2,6},{6,2},{3,7},{7,3},{8,12},{12,8},{9,1... | collective-permute-start | bytes 442376 | tf_op jit(solution)/shard_map/ppermute | solution.py:18
  18.7 4.5 %collective-permute-done.9.refs_11_.refs_6_ = bf16[128,512]{1,0:T(8,128)(2,1)S(1)} collective-permute-done((bf16[128,512]{1,0:T(8,128)(2,1)S(1)}, bf16[128,512]{1,0:T(8,128)(2,1)S(1)}, u32[]{:S(2)}, u32[]{:S(2)}) %collective-permute-start.9) | collective-permute-done | bytes 131104 | tf_op jit(solution)/shard_map/ppermute | solution.py:18
  24.5 8.9 %shard_map.86 = (bf16[2,2,16,16,352]{4,3,2,1,0:T(8,128)(2,1)S(1)}, bf16[2,2,16,16,352]{4,3,2,1,0:T(8,128)(2,1)S(1)}, bf16[16,64,512]{2,1,0:T(8,128)(2,1)S(1)}, s32[4,8,256]{2,1,0:T(8,128)S(1)}) custom-call(s32[3]{0:T(128)S(1)} %pad_add_fusion.where, bf16[144,512]{1,0:T(8,128)(2,1)S(1)} %get-tuple-element.21.refs_0_, ...), custom_call_target="tpu_custom_call" | custom-call | flops 2952790016 | bytes 11534336 | tf_op jit(solution)/shard_map/pallas_call | solution.py:142
  33.5 1.6 %collective-permute-start.10 = (bf16[128,512]{1,0:T(8,128)(2,1)S(1)}, bf16[128,512]{1,0:T(8,128)(2,1)S(1)}, u32[]{:S(2)}, u32[]{:S(2)}) collective-permute-start(bf16[128,512]{1,0:T(8,128)(2,1)S(1)} %get-tuple-element.25.refs_8_.refs_0_), channel_id=1, source_target_pairs={{0,4},{4,0},{1,5},{5,1},{2,6},{6,2},{3,7},{7,3},{8,12},{12,8},{9,1... | collective-permute-start | bytes 393224 | tf_op jit(solution)/shard_map/ppermute | solution.py:18
  37.6 2.2 %collective-permute-done.10.refs_1_ = bf16[128,512]{1,0:T(8,128)(2,1)S(1)} collective-permute-done((bf16[128,512]{1,0:T(8,128)(2,1)S(1)}, bf16[128,512]{1,0:T(8,128)(2,1)S(1)}, u32[]{:S(2)}, u32[]{:S(2)}) %collective-permute-start.10) | collective-permute-done | bytes 131104 | tf_op jit(solution)/shard_map/ppermute | solution.py:18
  39.9 2.8 %collective-permute-done.11.refs_3_ = bf16[128,512]{1,0:T(8,128)(2,1)S(1)} collective-permute-done((bf16[128,512]{1,0:T(8,128)(2,1)S(1)}, bf16[128,512]{1,0:T(8,128)(2,1)S(1)}, u32[]{:S(2)}, u32[]{:S(2)}) %collective-permute-start.11) | collective-permute-done | bytes 131104 | tf_op jit(solution)/shard_map/ppermute | solution.py:18
  42.7 2.8 %collective-permute-done.12.refs_5_ = bf16[128,512]{1,0:T(8,128)(2,1)S(1)} collective-permute-done((bf16[128,512]{1,0:T(8,128)(2,1)S(1)}, bf16[128,512]{1,0:T(8,128)(2,1)S(1)}, u32[]{:S(2)}, u32[]{:S(2)}) %collective-permute-start.12) | collective-permute-done | bytes 131104 | tf_op jit(solution)/shard_map/ppermute | solution.py:18
  45.5 2.4 %collective-permute-done.13.refs_7_ = bf16[128,512]{1,0:T(8,128)(2,1)S(1)} collective-permute-done((bf16[128,512]{1,0:T(8,128)(2,1)S(1)}, bf16[128,512]{1,0:T(8,128)(2,1)S(1)}, u32[]{:S(2)}, u32[]{:S(2)}) %collective-permute-start.13) | collective-permute-done | bytes 131104 | tf_op jit(solution)/shard_map/ppermute | solution.py:18
  47.8 6.8 %shard_map.87 = (bf16[2,1,16,16,352]{4,3,2,1,0:T(8,128)(2,1)S(1)}, bf16[2,1,16,16,352]{4,3,2,1,0:T(8,128)(2,1)S(1)}) custom-call(s32[3]{0:T(128)S(1)} %pad_add_fusion.where, bf16[128,512]{1,0:T(8,128)(2,1)S(1)} %get-tuple-element.25.refs_8_.refs_0_, bf16[128,512]{1,0:T(8,128)(2,1)S(1)} %collective-permute-done.10.refs_1_, ...), custom_call_target="tpu_custom_call" | custom-call | flops 1476395008 | bytes 5767168 | tf_op jit(solution)/shard_map/pallas_call | solution.py:142
  58.0 8.8 %collective-permute-done.17 = bf16[2,16,16,352]{3,2,1,0:T(8,128)(2,1)S(1)} collective-permute-done((bf16[2,16,16,352]{3,2,1,0:T(8,128)(2,1)S(1)}, bf16[2,16,16,352]{3,2,1,0:T(8,128)(2,1)S(1)}, u32[]{:S(2)}, u32[]{:S(2)}) %collective-permute-start.17) | collective-permute-done | bytes 360480 | tf_op jit(solution)/shard_map/ppermute | solution.py:18
  67.0 3.7 %collective-permute-done.15 = bf16[1,16,16,352]{3,2,1,0:T(8,128)(2,1)S(1)} collective-permute-done((bf16[1,16,16,352]{3,2,1,0:T(8,128)(2,1)S(1)}, bf16[1,16,16,352]{3,2,1,0:T(8,128)(2,1)S(1)}, u32[]{:S(2)}, u32[]{:S(2)}) %collective-permute-start.15) | collective-permute-done | bytes 180256 | tf_op jit(solution)/shard_map/ppermute | solution.py:18
  72.5 9.3 %collective-permute-done.19.h2 = bf16[2,16,16,352]{3,2,1,0:T(8,128)(2,1)S(1)} collective-permute-done((bf16[2,16,16,352]{3,2,1,0:T(8,128)(2,1)S(1)}, bf16[2,16,16,352]{3,2,1,0:T(8,128)(2,1)S(1)}, u32[]{:S(2)}, u32[]{:S(2)}) %collective-permute-start.19) | collective-permute-done | bytes 360480 | tf_op jit(solution)/shard_map/ppermute | solution.py:18
  81.8 1.7 %collective-permute-done.20.h3 = bf16[2,16,16,352]{3,2,1,0:T(8,128)(2,1)S(1)} collective-permute-done((bf16[2,16,16,352]{3,2,1,0:T(8,128)(2,1)S(1)}, bf16[2,16,16,352]{3,2,1,0:T(8,128)(2,1)S(1)}, u32[]{:S(2)}, u32[]{:S(2)}) %collective-permute-start.20) | collective-permute-done | bytes 360480 | tf_op jit(solution)/shard_map/ppermute | solution.py:18
  83.5 8.3 %shard_map.88 = (bf16[4,128,256]{2,1,0:T(8,128)(2,1)S(1)}, bf16[4,128,256]{2,1,0:T(8,128)(2,1)S(1)}, bf16[2,2,128,256]{3,2,1,0:T(8,128)(2,1)S(1)}, bf16[2,2,128,256]{3,2,1,0:T(8,128)(2,1)S(1)}) custom-call(s32[3]{0:T(128)S(1)} %pad_add_fusion.where, s32[4,8,256]{2,1,0:T(8,128)S(1)} %get-tuple-element.29.refs_8_.lines, ...), custom_call_target="tpu_custom_call" | custom-call | flops 2952790016 | bytes 11534336 | tf_op jit(solution)/shard_map/pallas_call | solution.py:196
  91.8 1.6 %collective-permute-start.23 = (bf16[2,2,128,256]{3,2,1,0:T(8,128)(2,1)S(1)}, bf16[2,2,128,256]{3,2,1,0:T(8,128)(2,1)S(1)}, u32[]{:S(2)}, u32[]{:S(2)}) collective-permute-start(bf16[2,2,128,256]{3,2,1,0:T(8,128)(2,1)S(1)} %get-tuple-element.37), channel_id=1, source_target_pairs={{0,1},{1,0},{2,3},{3,2},{4,5},{5,4},{6,7},{7,6},{8,9},{9,8},{10,11... | collective-permute-start | bytes 786440 | tf_op jit(solution)/shard_map/ppermute | solution.py:18
  95.0 5.5 %shard_map.90 = bf16[16,352,512]{2,1,0:T(8,128)(2,1)} custom-call(bf16[16,64,512]{2,1,0:T(8,128)(2,1)S(1)} %get-tuple-element.38.placed, bf16[2,16,16,352]{3,2,1,0:T(8,128)(2,1)S(1)} %pad_maximum_fusion.h0, bf16[2,16,16,352]{3,2,1,0:T(8,128)(2,1)S(1)} %collective-permute-done.18.h1, bf16[2,16,16,352]{3,2,1,0:T(8,128)(2,1)S(1)} %collective-permute-done.19.h2, ...), custom_call_target="tpu_custom_call" | custom-call | flops 1476395008 | bytes 5767168 | tf_op jit(solution)/shard_map/pallas_call | solution.py:225
  102.0 1.6 %collective-permute-start.22 = (bf16[2,128,256]{2,1,0:T(8,128)(2,1)S(1)}, bf16[2,128,256]{2,1,0:T(8,128)(2,1)S(1)}, u32[]{:S(2)}, u32[]{:S(2)}) collective-permute-start(bf16[2,128,256]{2,1,0:T(8,128)(2,1)S(1)} %pad_maximum_fusion.1), channel_id=1, source_target_pairs={{0,1},{1,0},{2,3},{3,2},{4,5},{5,4},{6,7},{7,6},{8,9},{9,8},{10,11... | collective-permute-start | bytes 393224 | tf_op jit(solution)/shard_map/ppermute | solution.py:18
  103.6 1.9 %collective-permute-done.24 = bf16[2,128,256]{2,1,0:T(8,128)(2,1)S(1)} collective-permute-done((bf16[2,128,256]{2,1,0:T(8,128)(2,1)S(1)}, bf16[2,128,256]{2,1,0:T(8,128)(2,1)S(1)}, u32[]{:S(2)}, u32[]{:S(2)}) %collective-permute-start.24) | collective-permute-done | bytes 131104 | tf_op jit(solution)/shard_map/ppermute | solution.py:18
  107.8 5.3 %collective-permute-start.26 = (bf16[128,512]{1,0:T(8,128)(2,1)S(1)}, bf16[128,512]{1,0:T(8,128)(2,1)S(1)}, u32[]{:S(2)}, u32[]{:S(2)}) collective-permute-start(bf16[128,512]{1,0:T(8,128)(2,1)S(1)} %pad_maximum_fusion.3), channel_id=1, source_target_pairs={{0,16},{1,24},{2,0},{3,8},{8,17},{9,25},{10,1},{11,9},{16,18},{17,... | collective-permute-start | bytes 393224 | tf_op jit(solution)/shard_map/ppermute | solution.py:299
  113.1 5.5 %shard_map.89 = bf16[16,352,512]{2,1,0:T(8,128)(2,1)} custom-call(bf16[16,64,512]{2,1,0:T(8,128)(2,1)S(1)} %get-tuple-element.38.placed, bf16[2,16,16,352]{3,2,1,0:T(8,128)(2,1)S(1)} %pad_maximum_fusion.h0, bf16[2,16,16,352]{3,2,1,0:T(8,128)(2,1)S(1)} %collective-permute-done.18.h1, bf16[2,16,16,352]{3,2,1,0:T(8,128)(2,1)S(1)} %collective-permute-done.19.h2, ...), custom_call_target="tpu_custom_call" | custom-call | flops 1476395008 | bytes 5767168 | tf_op jit(solution)/shard_map/pallas_call | solution.py:225
  118.6 5.2 %collective-permute-done.26 = bf16[128,512]{1,0:T(8,128)(2,1)S(1)} collective-permute-done((bf16[128,512]{1,0:T(8,128)(2,1)S(1)}, bf16[128,512]{1,0:T(8,128)(2,1)S(1)}, u32[]{:S(2)}, u32[]{:S(2)}) %collective-permute-start.26) | collective-permute-done | bytes 131104 | tf_op jit(solution)/shard_map/ppermute | solution.py:299
  (58 shorter events, 25.3 us)
Async XLA Ops:
  4.1 6.8 %collective-permute-start.1 = (bf16[144,512]{1,0:T(8,128)(2,1)S(1)}, bf16[144,512]{1,0:T(8,128)(2,1)S(1)}, u32[]{:S(2)}, u32[]{:S(2)}) collective-permute-start(bf16[144,512]{1,0:T(8,128)(2,1)S(1)} %get-tuple-element.22), channel_id=1, source_target_pairs={{0,8},{8,0},{16,24},{24,16},{1,9},{9,1},{17,25},{25,17},{2,10},{10... | collective-permute-start | bytes 442376 | tf_op jit(solution)/shard_map/ppermute | solution.py:18
  4.6 7.3 %collective-permute-start.3 = (bf16[144,512]{1,0:T(8,128)(2,1)S(1)}, bf16[144,512]{1,0:T(8,128)(2,1)S(1)}, u32[]{:S(2)}, u32[]{:S(2)}) collective-permute-start(bf16[144,512]{1,0:T(8,128)(2,1)S(1)} %get-tuple-element.23), channel_id=1, source_target_pairs={{0,16},{8,24},{16,0},{24,8},{1,17},{9,25},{17,1},{25,9},{2,18},{10... | collective-permute-start | bytes 442376 | tf_op jit(solution)/shard_map/ppermute | solution.py:18
  7.2 7.3 %collective-permute-start.5 = (bf16[144,512]{1,0:T(8,128)(2,1)S(1)}, bf16[144,512]{1,0:T(8,128)(2,1)S(1)}, u32[]{:S(2)}, u32[]{:S(2)}) collective-permute-start(bf16[144,512]{1,0:T(8,128)(2,1)S(1)} %get-tuple-element.24), channel_id=1, source_target_pairs={{0,24},{8,16},{16,8},{24,0},{1,25},{9,17},{17,9},{25,1},{2,26},{10... | collective-permute-start | bytes 442376 | tf_op jit(solution)/shard_map/ppermute | solution.py:18
  7.4 10.2 %collective-permute-start.8 = (bf16[128,512]{1,0:T(8,128)(2,1)S(1)}, bf16[128,512]{1,0:T(8,128)(2,1)S(1)}, u32[]{:S(2)}, u32[]{:S(2)}) collective-permute-start(bf16[128,512]{1,0:T(8,128)(2,1)S(1)} %get-tuple-element.27), channel_id=1, source_target_pairs={{0,16},{8,24},{16,0},{24,8},{1,17},{9,25},{17,1},{25,9},{2,18},{10... | collective-permute-start | bytes 393224 | tf_op jit(solution)/shard_map/ppermute | solution.py:18
  9.4 13.8 %collective-permute-start = (bf16[144,512]{1,0:T(8,128)(2,1)S(1)}, bf16[144,512]{1,0:T(8,128)(2,1)S(1)}, u32[]{:S(2)}, u32[]{:S(2)}) collective-permute-start(bf16[144,512]{1,0:T(8,128)(2,1)S(1)} %get-tuple-element.21.refs_0_), channel_id=1, source_target_pairs={{0,4},{4,0},{1,5},{5,1},{2,6},{6,2},{3,7},{7,3},{8,12},{12,8},{9,1... | collective-permute-start | bytes 442376 | tf_op jit(solution)/shard_map/ppermute | solution.py:18
  10.9 12.3 %collective-permute-start.2 = (bf16[144,512]{1,0:T(8,128)(2,1)S(1)}, bf16[144,512]{1,0:T(8,128)(2,1)S(1)}, u32[]{:S(2)}, u32[]{:S(2)}) collective-permute-start(bf16[144,512]{1,0:T(8,128)(2,1)S(1)} %collective-permute-done.1.refs_2_), channel_id=1, source_target_pairs={{0,4},{4,0},{1,5},{5,1},{2,6},{6,2},{3,7},{7,3},{8,12},{12,8},{9,1... | collective-permute-start | bytes 442376 | tf_op jit(solution)/shard_map/ppermute | solution.py:18
  11.9 11.2 %collective-permute-start.4 = (bf16[144,512]{1,0:T(8,128)(2,1)S(1)}, bf16[144,512]{1,0:T(8,128)(2,1)S(1)}, u32[]{:S(2)}, u32[]{:S(2)}) collective-permute-start(bf16[144,512]{1,0:T(8,128)(2,1)S(1)} %collective-permute-done.3.refs_4_), channel_id=1, source_target_pairs={{0,4},{4,0},{1,5},{5,1},{2,6},{6,2},{3,7},{7,3},{8,12},{12,8},{9,1... | collective-permute-start | bytes 442376 | tf_op jit(solution)/shard_map/ppermute | solution.py:18
  14.6 9.9 %collective-permute-start.6 = (bf16[144,512]{1,0:T(8,128)(2,1)S(1)}, bf16[144,512]{1,0:T(8,128)(2,1)S(1)}, u32[]{:S(2)}, u32[]{:S(2)}) collective-permute-start(bf16[144,512]{1,0:T(8,128)(2,1)S(1)} %collective-permute-done.5.refs_6_), channel_id=1, source_target_pairs={{0,4},{4,0},{1,5},{5,1},{2,6},{6,2},{3,7},{7,3},{8,12},{12,8},{9,1... | collective-permute-start | bytes 442376 | tf_op jit(solution)/shard_map/ppermute | solution.py:18
  17.6 5.5 %collective-permute-start.9 = (bf16[128,512]{1,0:T(8,128)(2,1)S(1)}, bf16[128,512]{1,0:T(8,128)(2,1)S(1)}, u32[]{:S(2)}, u32[]{:S(2)}) collective-permute-start(bf16[128,512]{1,0:T(8,128)(2,1)S(1)} %get-tuple-element.28), channel_id=1, source_target_pairs={{0,24},{8,16},{16,8},{24,0},{1,25},{9,17},{17,9},{25,1},{2,26},{10... | collective-permute-start | bytes 393224 | tf_op jit(solution)/shard_map/ppermute | solution.py:18
  33.4 21.3 %collective-permute-start.16 = (bf16[2,2,16,16,352]{4,3,2,1,0:T(8,128)(2,1)S(1)}, bf16[2,2,16,16,352]{4,3,2,1,0:T(8,128)(2,1)S(1)}, u32[]{:S(2)}, u32[]{:S(2)}) collective-permute-start(bf16[2,2,16,16,352]{4,3,2,1,0:T(8,128)(2,1)S(1)} %get-tuple-element.33), channel_id=1, source_target_pairs={{0,8},{8,0},{16,24},{24,16},{1,9},{9,1},{17,25},{25,17},{2,10},{10... | collective-permute-start | bytes 2162696 | tf_op jit(solution)/shard_map/ppermute | solution.py:18
  33.5 6.4 %collective-permute-start.10 = (bf16[128,512]{1,0:T(8,128)(2,1)S(1)}, bf16[128,512]{1,0:T(8,128)(2,1)S(1)}, u32[]{:S(2)}, u32[]{:S(2)}) collective-permute-start(bf16[128,512]{1,0:T(8,128)(2,1)S(1)} %get-tuple-element.25.refs_8_.refs_0_), channel_id=1, source_target_pairs={{0,4},{4,0},{1,5},{5,1},{2,6},{6,2},{3,7},{7,3},{8,12},{12,8},{9,1... | collective-permute-start | bytes 393224 | tf_op jit(solution)/shard_map/ppermute | solution.py:18
  35.0 7.6 %collective-permute-start.11 = (bf16[128,512]{1,0:T(8,128)(2,1)S(1)}, bf16[128,512]{1,0:T(8,128)(2,1)S(1)}, u32[]{:S(2)}, u32[]{:S(2)}) collective-permute-start(bf16[128,512]{1,0:T(8,128)(2,1)S(1)} %collective-permute-done.7.refs_9_.refs_2_), channel_id=1, source_target_pairs={{0,4},{4,0},{1,5},{5,1},{2,6},{6,2},{3,7},{7,3},{8,12},{12,8},{9,1... | collective-permute-start | bytes 393224 | tf_op jit(solution)/shard_map/ppermute | solution.py:18
  35.6 9.9 %collective-permute-start.12 = (bf16[128,512]{1,0:T(8,128)(2,1)S(1)}, bf16[128,512]{1,0:T(8,128)(2,1)S(1)}, u32[]{:S(2)}, u32[]{:S(2)}) collective-permute-start(bf16[128,512]{1,0:T(8,128)(2,1)S(1)} %collective-permute-done.8.refs_10_.refs_4_), channel_id=1, source_target_pairs={{0,4},{4,0},{1,5},{5,1},{2,6},{6,2},{3,7},{7,3},{8,12},{12,8},{9,1... | collective-permute-start | bytes 393224 | tf_op jit(solution)/shard_map/ppermute | solution.py:18
  37.1 10.8 %collective-permute-start.13 = (bf16[128,512]{1,0:T(8,128)(2,1)S(1)}, bf16[128,512]{1,0:T(8,128)(2,1)S(1)}, u32[]{:S(2)}, u32[]{:S(2)}) collective-permute-start(bf16[128,512]{1,0:T(8,128)(2,1)S(1)} %collective-permute-done.9.refs_11_.refs_6_), channel_id=1, source_target_pairs={{0,4},{4,0},{1,5},{5,1},{2,6},{6,2},{3,7},{7,3},{8,12},{12,8},{9,1... | collective-permute-start | bytes 393224 | tf_op jit(solution)/shard_map/ppermute | solution.py:18
  54.9 12.0 %collective-permute-start.17 = (bf16[2,16,16,352]{3,2,1,0:T(8,128)(2,1)S(1)}, bf16[2,16,16,352]{3,2,1,0:T(8,128)(2,1)S(1)}, u32[]{:S(2)}, u32[]{:S(2)}) collective-permute-start(bf16[2,16,16,352]{3,2,1,0:T(8,128)(2,1)S(1)} %fusion), channel_id=1, source_target_pairs={{0,16},{8,24},{16,0},{24,8},{1,17},{9,25},{17,1},{25,9},{2,18},{10... | collective-permute-start | bytes 1081352 | tf_op jit(solution)/shard_map/ppermute | solution.py:18
  56.5 14.1 %collective-permute-start.15 = (bf16[1,16,16,352]{3,2,1,0:T(8,128)(2,1)S(1)}, bf16[1,16,16,352]{3,2,1,0:T(8,128)(2,1)S(1)}, u32[]{:S(2)}, u32[]{:S(2)}) collective-permute-start(bf16[1,16,16,352]{3,2,1,0:T(8,128)(2,1)S(1)} %fusion.4), channel_id=1, source_target_pairs={{0,16},{8,24},{16,0},{24,8},{1,17},{9,25},{17,1},{25,9},{2,18},{10... | collective-permute-start | bytes 540680 | tf_op jit(solution)/shard_map/ppermute | solution.py:18
  71.0 10.8 %collective-permute-start.19 = (bf16[2,16,16,352]{3,2,1,0:T(8,128)(2,1)S(1)}, bf16[2,16,16,352]{3,2,1,0:T(8,128)(2,1)S(1)}, u32[]{:S(2)}, u32[]{:S(2)}) collective-permute-start(bf16[2,16,16,352]{3,2,1,0:T(8,128)(2,1)S(1)} %pad_maximum_fusion.h0), channel_id=1, source_target_pairs={{0,16},{8,24},{16,0},{24,8},{1,17},{9,25},{17,1},{25,9},{2,18},{10... | collective-permute-start | bytes 1081352 | tf_op jit(solution)/shard_map/ppermute | solution.py:18
  72.5 9.3 %collective-permute-start.18 = (bf16[2,16,16,352]{3,2,1,0:T(8,128)(2,1)S(1)}, bf16[2,16,16,352]{3,2,1,0:T(8,128)(2,1)S(1)}, u32[]{:S(2)}, u32[]{:S(2)}) collective-permute-start(bf16[2,16,16,352]{3,2,1,0:T(8,128)(2,1)S(1)} %pad_maximum_fusion.h0), channel_id=1, source_target_pairs={{0,8},{8,0},{16,24},{24,16},{1,9},{9,1},{17,25},{25,17},{2,10},{10... | collective-permute-start | bytes 1081352 | tf_op jit(solution)/shard_map/ppermute | solution.py:18
  91.8 8.6 %collective-permute-start.23 = (bf16[2,2,128,256]{3,2,1,0:T(8,128)(2,1)S(1)}, bf16[2,2,128,256]{3,2,1,0:T(8,128)(2,1)S(1)}, u32[]{:S(2)}, u32[]{:S(2)}) collective-permute-start(bf16[2,2,128,256]{3,2,1,0:T(8,128)(2,1)S(1)} %get-tuple-element.37), channel_id=1, source_target_pairs={{0,1},{1,0},{2,3},{3,2},{4,5},{5,4},{6,7},{7,6},{8,9},{9,8},{10,11... | collective-permute-start | bytes 786440 | tf_op jit(solution)/shard_map/ppermute | solution.py:18
  93.5 8.4 %collective-permute-start.21 = (bf16[4,128,256]{2,1,0:T(8,128)(2,1)S(1)}, bf16[4,128,256]{2,1,0:T(8,128)(2,1)S(1)}, u32[]{:S(2)}, u32[]{:S(2)}) collective-permute-start(bf16[4,128,256]{2,1,0:T(8,128)(2,1)S(1)} %get-tuple-element.35), channel_id=1, source_target_pairs={{0,4},{4,0},{1,5},{5,1},{2,6},{6,2},{3,7},{7,3},{8,12},{12,8},{9,1... | collective-permute-start | bytes 786440 | tf_op jit(solution)/shard_map/ppermute | solution.py:18
  100.5 5.0 %collective-permute-start.24 = (bf16[2,128,256]{2,1,0:T(8,128)(2,1)S(1)}, bf16[2,128,256]{2,1,0:T(8,128)(2,1)S(1)}, u32[]{:S(2)}, u32[]{:S(2)}) collective-permute-start(bf16[2,128,256]{2,1,0:T(8,128)(2,1)S(1)} %fusion.5), channel_id=1, source_target_pairs={{0,4},{4,0},{1,5},{5,1},{2,6},{6,2},{3,7},{7,3},{8,12},{12,8},{9,1... | collective-permute-start | bytes 393224 | tf_op jit(solution)/shard_map/ppermute | solution.py:18
  102.0 5.0 %collective-permute-start.22 = (bf16[2,128,256]{2,1,0:T(8,128)(2,1)S(1)}, bf16[2,128,256]{2,1,0:T(8,128)(2,1)S(1)}, u32[]{:S(2)}, u32[]{:S(2)}) collective-permute-start(bf16[2,128,256]{2,1,0:T(8,128)(2,1)S(1)} %pad_maximum_fusion.1), channel_id=1, source_target_pairs={{0,1},{1,0},{2,3},{3,2},{4,5},{5,4},{6,7},{7,6},{8,9},{9,8},{10,11... | collective-permute-start | bytes 393224 | tf_op jit(solution)/shard_map/ppermute | solution.py:18
  107.1 11.5 %collective-permute-start.25 = (bf16[128,512]{1,0:T(8,128)(2,1)S(1)}, bf16[128,512]{1,0:T(8,128)(2,1)S(1)}, u32[]{:S(2)}, u32[]{:S(2)}) collective-permute-start(bf16[128,512]{1,0:T(8,128)(2,1)S(1)} %pad_maximum_fusion.2), channel_id=1, source_target_pairs={{0,0},{1,8},{2,16},{3,24},{8,1},{9,9},{10,17},{11,25},{16,2},{17,1... | collective-permute-start | bytes 393224 | tf_op jit(solution)/shard_map/ppermute | solution.py:298
  107.8 16.0 %collective-permute-start.26 = (bf16[128,512]{1,0:T(8,128)(2,1)S(1)}, bf16[128,512]{1,0:T(8,128)(2,1)S(1)}, u32[]{:S(2)}, u32[]{:S(2)}) collective-permute-start(bf16[128,512]{1,0:T(8,128)(2,1)S(1)} %pad_maximum_fusion.3), channel_id=1, source_target_pairs={{0,16},{1,24},{2,0},{3,8},{8,17},{9,25},{10,1},{11,9},{16,18},{17,... | collective-permute-start | bytes 393224 | tf_op jit(solution)/shard_map/ppermute | solution.py:299
  (6 other events, 8.3 us)

commit v2 on v1

v2 whole, which is shorter than its diff:
```python
import functools

import jax
import jax.numpy as jnp
from jax import lax
from jax.experimental import pallas as pl
from jax.experimental.pallas import tpu as pltpu
from jax.sharding import PartitionSpec as P

CAP = 8
META = 16
F32 = jnp.float32
BF16 = jnp.bfloat16
VMEM_LIMIT = 48 * 1024 * 1024


def swap(value, axis, count, bit):
    return lax.ppermute(value, axis, [(i, i ^ bit) for i in range(count)])


def whole_spec(shape):
    return pl.BlockSpec(shape, lambda *_: (0,) * len(shape))


def params():
    return pltpu.CompilerParams(vmem_limit_bytes=VMEM_LIMIT)


def split_kernel(width, n_dp, where, ids, tokens, cotangent, *refs):
    outs, (meta, sems) = refs[:-2], refs[-2:]
    k, x = where[0], where[1]
    rows = tokens.shape[0]
    copies = []
    for rel in range(n_dp):
        start = pl.multiple_of((k ^ rel) * width, 128)
        for which, source in enumerate((tokens, cotangent)):
            out = outs[which * n_dp + rel]
            copy = pltpu.make_async_copy(
                source.at[:, pl.ds(start, width)], out.at[pl.ds(0, rows), :], sems.at[which * n_dp + rel]
            )
            copy.start()
            copies.append(copy)
    along = ids[...].astype(F32)
    line = lax.broadcasted_iota(jnp.int32, (rows, rows), 0)
    lane = lax.broadcasted_iota(jnp.int32, (rows, rows), 1)
    named = jnp.broadcast_to(along, (rows, rows))
    down = jnp.sum(jnp.where(line == lane, named, 0.0), axis=1, keepdims=True)
    earlier = jnp.where((named == down) & (line < lane), 1.0, 0.0)
    place = jnp.sum(earlier, axis=0, keepdims=True) + (x * CAP).astype(F32)
    at = lax.broadcasted_iota(jnp.int32, (META, rows), 0)
    meta[...] = jnp.zeros(meta.shape, BF16)
    meta[:, 0:rows] = jnp.where(at == 0, along, jnp.where(at == 1, place, 0.0)).astype(BF16)
    for rel in range(n_dp):
        copy = pltpu.make_async_copy(meta, outs[rel].at[pl.ds(rows, META), :], sems.at[2 * n_dp + rel])
        copy.start()
        copies.append(copy)
    for copy in copies:
        copy.wait()


def split(where, ids, tokens, cotangent, width, n_dp):
    rows = tokens.shape[0]
    tall, low = (rows + META, width), (rows, width)
    anywhere = pl.BlockSpec(memory_space=pl.ANY)
    return pl.pallas_call(
        functools.partial(split_kernel, width, n_dp),
        out_shape=[jax.ShapeDtypeStruct(s, BF16) for s in [tall] * n_dp + [low] * n_dp],
        in_specs=[
            pl.BlockSpec(memory_space=pltpu.SMEM),
            pl.BlockSpec(memory_space=pltpu.VMEM),
            anywhere,
            anywhere,
        ],
        out_specs=[anywhere] * (2 * n_dp),
        scratch_shapes=[pltpu.VMEM((META, width), BF16), pltpu.SemaphoreType.DMA((3 * n_dp,))],
        compiler_params=params(),
    )(where, ids, tokens, cotangent)


def placer_of(row, slot_count):
    every = lax.broadcasted_iota(jnp.int32, (slot_count, row.shape[1]), 0)
    return (every == row).astype(F32).astype(BF16)


def place_kernel(order, first, after, where, *refs):
    n_dp = len(order)
    if first:
        mine, other, refs = refs[:n_dp], refs[n_dp : 2 * n_dp], refs[2 * n_dp + after :]
        placed, lines = refs
    else:
        mine, lines, refs = refs[:n_dp], refs[n_dp], refs[n_dp + 1 :]
        halves, (placed,) = refs[: len(refs) - after - 1], refs[-1:]
        other = [half.at[i] for half in halves for i in range(half.shape[0])]
    local_experts, slot_rows, width = placed.shape
    slots = slot_rows // n_dp
    rows = mine[0].shape[0] - (META if first else 0)
    for at, rel in enumerate(order):
        pair = mine[rel], other[rel]
        if first:
            metas = [b[rows:, 0:rows].astype(F32) for b in pair]
            ids = jnp.concatenate([m[0:1] for m in metas], axis=1)
            place = jnp.concatenate([m[1:2] for m in metas], axis=1)
            low = (where[1] * local_experts).astype(F32)
            row = ((ids - low) * slots + place).astype(jnp.int32)
            lines[rel] = jnp.broadcast_to(row, (8, row.shape[1]))
        else:
            row = lines[rel][0:1]
        placer = placer_of(row, local_experts * slots)
        values = jnp.concatenate([b[0:rows, :] for b in pair], axis=0)
        found = jnp.dot(placer, values, preferred_element_type=F32).astype(BF16)
        placed[:, at * slots : (at + 1) * slots, :] = found.reshape(local_experts, slots, width)


def place(order, where, mine, other, lines, local_experts, after, cost):
    first = lines is None
    n_dp, slots = len(order), 2 * CAP
    width = mine[0].shape[1]
    rows = mine[0].shape[0] - (META if first else 0)
    placed = jax.ShapeDtypeStruct((local_experts, n_dp * slots, width), BF16)
    line = jax.ShapeDtypeStruct((n_dp, 8, 2 * rows), jnp.int32)
    near = pl.BlockSpec(memory_space=pltpu.VMEM)
    operands = [*mine] + ([] if first else [lines]) + [*other]
    return pl.pallas_call(
        functools.partial(place_kernel, order, first, len(after)),
        out_shape=[placed, line] if first else placed,
        in_specs=[pl.BlockSpec(memory_space=pltpu.SMEM)]
        + [near] * len(operands)
        + [pl.BlockSpec(memory_space=pl.ANY)] * len(after),
        out_specs=[near, near] if first else near,
        compiler_params=params(),
        cost_estimate=pl.CostEstimate(flops=cost, bytes_accessed=4 * rows * width * n_dp, transcendentals=0),
    )(where, *operands, *after)


def back_kernel(n_dp, where, lines, h0, h1, h2, h3, gate, up, keep_x, send_x, keep_z, send_z, near, held, sems):
    parts = (h0, h1, h2, h3)
    local_experts, slots = h0.shape[1], h0.shape[2]
    per_copy = local_experts // sems.shape[1]

    def copy_of(which, at):
        group = pl.ds(at * per_copy, per_copy)
        return pltpu.make_async_copy((gate, up)[which].at[group], near.at[which, group], sems.at[which, at])

    for at in range(sems.shape[1]):
        for which in range(2):
            copy_of(which, at).start()
    for at in range(sems.shape[1]):
        for which in range(2):
            copy_of(which, at).wait()
        for e in range(at * per_copy, (at + 1) * per_copy):
            gate_grad = jnp.concatenate([h[0, e] for h in parts], axis=0)
            up_grad = jnp.concatenate([h[1, e] for h in parts], axis=0)
            value = jnp.dot(gate_grad, near[0, e], preferred_element_type=F32)
            value = value + jnp.dot(up_grad, near[1, e], preferred_element_type=F32)
            value = value.astype(BF16)
            for rel in range(n_dp):
                held[rel, e * slots : (e + 1) * slots, :] = value[rel * slots : (rel + 1) * slots]

    rows, half = keep_x.shape[1], keep_x.shape[2]
    for r in range(n_dp):
        rel = where[2] ^ r
        placer = placer_of(lines[rel][0:1], held.shape[1])
        token_rows = lax.dot_general(
            placer, held[rel], (((0,), (0,)), ((), ())), preferred_element_type=F32
        ).astype(BF16)
        keep_x[r] = token_rows[0:rows, 0:half]
        send_x[r] = token_rows[rows:, 0:half]
        out = send_z if r & 1 else keep_z
        out[0, r // 2] = token_rows[0:rows, half:]
        out[1, r // 2] = token_rows[rows:, half:]


def back(where, lines, parts, gate, up, rows):
    n_dp = len(parts)
    local_experts, hidden, width = gate.shape
    slots = parts[0].shape[2]
    shape_x = (n_dp, rows, width // 2)
    shape_z = (2, n_dp // 2, rows, width // 2)
    near = pl.BlockSpec(memory_space=pltpu.VMEM)
    flops = 4 * local_experts * n_dp * slots * width * hidden
    return pl.pallas_call(
        functools.partial(back_kernel, n_dp),
        out_shape=[jax.ShapeDtypeStruct(s, BF16) for s in (shape_x, shape_x, shape_z, shape_z)],
        in_specs=[pl.BlockSpec(memory_space=pltpu.SMEM)]
        + [near] * (1 + n_dp)
        + [pl.BlockSpec(memory_space=pl.ANY)] * 2,
        out_specs=[near] * 4,
        scratch_shapes=[
            pltpu.VMEM((2, local_experts, hidden, width), BF16),
            pltpu.VMEM((n_dp, local_experts * slots, width), BF16),
            pltpu.SemaphoreType.DMA((2, 8 if local_experts % 8 == 0 else 1)),
        ],
        compiler_params=params(),
        cost_estimate=pl.CostEstimate(
            flops=4 * flops, bytes_accessed=2 * local_experts * width * hidden * 2, transcendentals=0
        ),
    )(where, lines, *parts, gate, up)


def weight_kernel(which, order, placed, h0, h1, h2, h3, out):
    parts = (h0, h1, h2, h3)
    for i in range(out.shape[0]):
        grad = jnp.concatenate([parts[rel][which, i] for rel in order], axis=0)
        out[i] = lax.dot_general(
            grad, placed[i], (((0,), (0,)), ((), ())), preferred_element_type=F32
        ).astype(BF16)


def weight_grad(which, order, placed, parts, per_step):
    local_experts, slot_rows, width = placed.shape
    _, _, slots, hidden = parts[0].shape
    part_spec = pl.BlockSpec((2, per_step, slots, hidden), lambda e: (0, e, 0, 0))
    flops = 2 * local_experts * slot_rows * width * hidden
    return pl.pallas_call(
        functools.partial(weight_kernel, which, order),
        grid=(local_experts // per_step,),
        out_shape=jax.ShapeDtypeStruct((local_experts, hidden, width), BF16),
        in_specs=[pl.BlockSpec((per_step, slot_rows, width), lambda e: (e, 0, 0))] + [part_spec] * len(parts),
        out_specs=pl.BlockSpec((per_step, hidden, width), lambda e: (e, 0, 0)),
        compiler_params=params(),
        cost_estimate=pl.CostEstimate(
            flops=4 * flops, bytes_accessed=local_experts * width * hidden * 2, transcendentals=0
        ),
    )(placed, *parts)


def plus(first, second):
    return first.astype(F32) + second.astype(F32)


def swiglu_grads(gate_act, up_act, hidden_grad):
    sigmoid_gate = jax.nn.sigmoid(gate_act)
    up_grad = (hidden_grad * gate_act * sigmoid_gate).astype(BF16)
    gate_grad = (
        hidden_grad * up_act * sigmoid_gate * (1.0 + gate_act * (1.0 - sigmoid_gate))
    ).astype(BF16)
    return gate_grad, up_grad


def on_small_slice(tokens, cotangent, expert_ids, gate_weight, up_weight, down_weight):
    n_dp, n_x, n_t = 4, 2, 4
    k, x, t = lax.axis_index("dp"), lax.axis_index("expert"), lax.axis_index("tensor")
    width = gate_weight.shape[1]
    rows = tokens.shape[0]
    half = width // 2
    where = jnp.stack([k, x, k ^ t]).astype(jnp.int32)

    chunks = split(where, expert_ids.reshape(1, rows), tokens, cotangent, width, n_dp)

    own = [c if i % n_dp == 0 else swap(c, "dp", n_dp, i % n_dp) for i, c in enumerate(chunks)]
    own_tokens, own_grads = own[:n_dp], own[n_dp:]
    other_tokens = [swap(c, "expert", n_x, 1) for c in own_tokens]
    all_grads = jnp.stack(own_grads)
    other_grads = swap(all_grads, "expert", n_x, 1)
    gate_weight, up_weight, down_weight = (
        jnp.swapaxes(weight, 1, 2) for weight in (gate_weight, up_weight, down_weight)
    )
    local_experts = gate_weight.shape[0]
    order = (0, 1, 2, 3)

    def project(values, weight):
        act = jnp.einsum("esd,ehd->esh", values, weight, preferred_element_type=F32).astype(BF16)
        return jnp.split(act, n_dp, axis=1)

    def near_and_far(act):
        near, far = swap(act[1], "dp", n_dp, 1), swap(act[3], "dp", n_dp, 1)
        return plus(act[0], near), plus(act[2], far).astype(BF16)

    placed, lines = place(order, where, own_tokens, other_tokens, None, local_experts, [all_grads], 1 << 34)
    gate_near, gate_far = near_and_far(project(placed, gate_weight))
    up_near, up_far = near_and_far(project(placed, up_weight))
    far = jnp.stack([gate_far, up_far])
    there = swap(far, "dp", n_dp, 2)
    placed_grads = place(order, where, own_grads, [other_grads], lines, local_experts, [far], 1 << 34)
    hidden_act = project(placed_grads, down_weight)
    hidden_grad = hidden_act[0].astype(F32)
    for rel in range(1, n_dp):
        hidden_grad = hidden_grad + swap(hidden_act[rel], "dp", n_dp, rel).astype(F32)
    acts = plus(gate_near, there[0]), plus(up_near, there[1])
    part = jnp.stack(swiglu_grads(acts[0], acts[1], hidden_grad))
    far = swap(part, "dp", n_dp, 2)
    parts = [part, swap(part, "dp", n_dp, 1), far, swap(far, "dp", n_dp, 1)]

    keep_x, send_x, keep_z, send_z = back(where, lines, parts, gate_weight, up_weight, rows)
    sum_x = plus(keep_x, swap(send_x, "expert", n_x, 1))
    sum_z = plus(keep_z, swap(send_z, "tensor", n_t, 1))
    from_z = swap(jnp.stack([sum_x[1], sum_x[3]]).astype(BF16), "tensor", n_t, 1)
    from_x = swap(sum_z[1].astype(BF16), "expert", n_x, 1)
    near = jnp.concatenate([plus(sum_x[0], from_z[0]), plus(sum_z[0, 0], from_x[0])], axis=1).astype(BF16)
    far = jnp.concatenate([plus(sum_x[2], from_z[1]), plus(sum_z[0, 1], from_x[1])], axis=1).astype(BF16)
    pairs = [(i, j) for i in range(n_dp) for j in range(n_t)]
    near = lax.ppermute(near, ("dp", "tensor"), [(i * n_t + j, j * n_t + i) for i, j in pairs])
    far = lax.ppermute(far, ("dp", "tensor"), [(i * n_t + j, (j ^ 2) * n_t + i) for i, j in pairs])
    grad_tokens = plus(near, far).astype(BF16)

    grad_gate = jnp.swapaxes(weight_grad(0, order, placed, parts, 4), 1, 2)
    grad_up = jnp.swapaxes(weight_grad(1, order, placed, parts, 4), 1, 2)
    return grad_tokens, grad_gate, grad_up


def bits_of(count):
    bits = []
    bit = 1
    while bit < count:
        bits.append(bit)
        bit *= 2
    return bits


def halving_sum(parts, axis, count):
    parts = dict(parts)
    for bit in bits_of(count):
        leaving = sorted(r for r in parts if r & bit)
        arrived = swap(jnp.stack([parts[r].astype(BF16) for r in leaving]), axis, count, bit)
        for at, r in enumerate(leaving):
            parts[r ^ bit] = plus(parts[r ^ bit], arrived[at])
            del parts[r]
    return parts[0]


def doubling_gather(value, axis, count):
    held = {0: value}
    for bit in reversed(bits_of(count)):
        known = sorted(held)
        arrived = swap(jnp.stack([held[r] for r in known]), axis, count, bit)
        for at, r in enumerate(known):
            held[r ^ bit] = arrived[at]
    return [held[r] for r in range(count)]


def on_any_slice(tokens, cotangent, expert_ids, gate_weight, up_weight, down_weight):
    n_dp, n_x, n_t = lax.axis_size("dp"), lax.axis_size("expert"), lax.axis_size("tensor")
    k, x, t = lax.axis_index("dp"), lax.axis_index("expert"), lax.axis_index("tensor")
    local_experts, width, hidden = gate_weight.shape
    rows = tokens.shape[0]
    slots = n_x * CAP
    ids_row = expert_ids.reshape(1, rows)
    order = jnp.arange(rows, dtype=jnp.int32)
    earlier = (expert_ids == ids_row) & (order[:, None] < order[None, :])
    position = jnp.sum(earlier.astype(jnp.int32), axis=0)
    target = ids_row[0] * CAP + position
    targets = lax.all_gather(target, ("dp", "expert"), axis=0, tiled=False).reshape(n_dp, n_x, rows)
    pair = jnp.stack([tokens, cotangent])
    placers, slot_rows = [], []
    for rel in range(n_dp):
        columns = lax.dynamic_slice_in_dim(pair, (k ^ rel) * width, width, axis=2)
        mine = columns if rel == 0 else swap(columns, "dp", n_dp, rel)
        blocks = lax.all_gather(mine, "expert", axis=1, tiled=True)
        goal = lax.dynamic_index_in_dim(targets, k ^ rel, axis=0, keepdims=False)
        expert = goal // CAP - x * local_experts
        place = jnp.arange(n_x, dtype=jnp.int32)[:, None] * CAP + goal % CAP
        row = jnp.where((expert >= 0) & (expert < local_experts), expert * slots + place, -1)
        row = row.reshape(1, n_x * rows)
        every = jnp.arange(local_experts * slots, dtype=jnp.int32)[:, None]
        placer = (every == row).astype(BF16)
        placers.append(placer)
        slot_rows.append(
            jnp.einsum("sn,and->asd", placer, blocks, preferred_element_type=F32)
            .astype(BF16)
            .reshape(2, local_experts, slots, width)
        )
    slot_rows = jnp.concatenate(slot_rows, axis=2)
    inputs, grads_in = slot_rows[0], slot_rows[1]

    def act(values, weight):
        return jnp.einsum("esd,edf->esf", values, weight, preferred_element_type=F32).astype(BF16)

    acts = jnp.stack([act(inputs, gate_weight), act(inputs, up_weight), act(grads_in, down_weight)])
    acts = acts.reshape(3, local_experts, n_dp, slots, hidden)
    acts = halving_sum({r: acts[:, :, r] for r in range(n_dp)}, "dp", n_dp)
    grads = doubling_gather(jnp.stack(swiglu_grads(acts[0], acts[1], acts[2])), "dp", n_dp)
    grads = jnp.concatenate(grads, axis=2)
    gate_grad, up_grad = grads[0], grads[1]
    partial_value = jnp.einsum("esf,edf->esd", gate_grad, gate_weight, preferred_element_type=F32)
    partial_value = partial_value + jnp.einsum("esf,edf->esd", up_grad, up_weight, preferred_element_type=F32)
    partial_value = partial_value.astype(BF16).reshape(local_experts, n_dp, slots, width)
    per_token = []
    for rel in range(n_dp):
        flat = partial_value[:, rel].reshape(local_experts * slots, width)
        spread = lax.dot_general(placers[rel], flat, (((0,), (0,)), ((), ())), preferred_element_type=F32)
        spread = spread.astype(BF16).reshape(n_x, rows, width)
        per_token.append(lax.psum_scatter(spread, "expert", scatter_dimension=0, tiled=False))
    per_token = jnp.stack(per_token)
    terms = {r: lax.dynamic_index_in_dim(per_token, k ^ t ^ r, axis=0, keepdims=False) for r in range(n_t)}
    summed = halving_sum(terms, "tensor", n_t).astype(BF16)
    summed = lax.ppermute(
        summed, ("dp", "tensor"), [(i * n_t + j, j * n_t + i) for i in range(n_dp) for j in range(n_t)]
    )
    grad_gate = jnp.einsum("esd,esf->edf", inputs, gate_grad, preferred_element_type=F32).astype(BF16)
    grad_up = jnp.einsum("esd,esf->edf", inputs, up_grad, preferred_element_type=F32).astype(BF16)
    return summed, grad_gate, grad_up


def solution(mesh):
    placed = (
        P(("dp", "expert"), None),
        P(("dp", "expert"), None),
        P(("dp", "expert"), None),
        P("expert", "dp", "tensor"),
        P("expert", "dp", "tensor"),
        P("expert", "dp", "tensor"),
    )
    sizes = tuple(mesh.shape[name] for name in ("dp", "expert", "tensor"))
    return jax.shard_map(
        on_small_slice if sizes == (4, 2, 4) else on_any_slice,
        mesh=mesh,
        in_specs=placed,
        out_specs=(
            P(("dp", "expert"), "tensor"),
            P("expert", "dp", "tensor"),
            P("expert", "dp", "tensor"),
        ),
        check_vma=False,
    )
```

time: 125 us -> 114 us (0.912)
  Pallas kernels: 35.6 us -> 16.8 us
  matrix products: 0 us -> 4.95 us
  waiting for transfers between devices: 50.9 us -> 54.4 us
  starting transfers between devices: 32.8 us -> 31.1 us
    pallas_call x5, Pallas kernels: 35 us -> 15.8 us  [the longest x2 8.09 us: weight_grad(): pl.pallas_call(functools.partial(weight_kernel, which, order), grid=(loca...]
    dot_general x0 -> x3, matrix products: none -> 4.95 us  [project(): jnp.einsum('esd,ehd->esh', values, weight, preferred_element_type=F32)]
    ppermute x25 -> x26, waiting for transfers between devices: 45.7 us -> 47.7 us  [swap(): return lax.ppermute(value, axis, [(i, i ^ bit) for i in range(count)])]
    ppermute x25 -> x26, starting transfers between devices: 26.7 us -> 25 us  [swap(): return lax.ppermute(value, axis, [(i, i ^ bit) for i in range(count)])]
    ppermute x1, waiting for transfers between devices: 5.2 us -> 6.65 us  [on_small_slice(): lax.ppermute(far, ('dp', 'tensor'), [(i * n_t + j, (j ^ 2) * n_t + i) for...]
    another operation x1 -> x2, other arithmetic: 0.07 us -> 1.41 us  [on_small_slice(): part = jnp.stack(swiglu_grads(acts[0], acts[1], hidden_grad))]
    unnamed x6 -> x20, local copies, waits for them, and re-layouts: 2.74 us -> 3.19 us
  transfers between devices with their start and end apart: 27 -> 28, of which waited for: 17 -> 15; matrix products, arithmetic and copies ran while one was open for 0% -> 5% of each run, Pallas kernels for 14% -> 9%
where the time goes in v2:
time: 114 us
  waiting for transfers between devices  54.4 us (48%)
  starting transfers between devices  31.1 us (27%)
  Pallas kernels  16.8 us (15%)
  matrix products  4.95 us (4%)
  local copies, waits for them, and re-layouts  3.36 us (3%)
  other arithmetic  2.65 us (2%)
    ppermute x26, waiting for transfers between devices, swap(): return lax.ppermute(value, axis, [(i, i ^ bit) for i in range(count)])  47.7 us
    ppermute x26, starting transfers between devices, swap(): return lax.ppermute(value, axis, [(i, i ^ bit) for i in range(count)])  25 us
    pallas_call x2, Pallas kernels, weight_grad(): pl.pallas_call(functools.partial(weight_kernel, which, order), grid=(loca...  8.09 us
    ppermute x1, waiting for transfers between devices, on_small_slice(): lax.ppermute(far, ('dp', 'tensor'), [(i * n_t + j, (j ^ 2) * n_t + i) for...  6.65 us
    pallas_call x1, Pallas kernels, back(): pl.pallas_call(functools.partial(back_kernel, n_dp), out_shape=[jax.Shape...  5.79 us
    ppermute x1, starting transfers between devices, on_small_slice(): lax.ppermute(far, ('dp', 'tensor'), [(i * n_t + j, (j ^ 2) * n_t + i) for...  5.35 us
    dot_general x3, matrix products, project(): jnp.einsum('esd,ehd->esh', values, weight, preferred_element_type=F32)  4.95 us
    unnamed x20, local copies, waits for them, and re-layouts  3.19 us
  transfers between devices with their start and end apart: 28, of which 15 were waited for; matrix products, arithmetic and copies ran while one was open for 5% of the time, Pallas kernels for 9%

profile of v2, /device:TPU:0, one launch (start us, length us, event | category | flops | bytes accessed | tf_op | source)
XLA Modules:
  0.0 114.2 jit_solution(6229927235268506788)
XLA Ops:
  5.1 2.9 %collective-permute-start.1 = (bf16[144,512]{1,0:T(8,128)(2,1)S(1)}, bf16[144,512]{1,0:T(8,128)(2,1)S(1)}, u32[]{:S(2)}, u32[]{:S(2)}) collective-permute-start(bf16[144,512]{1,0:T(8,128)(2,1)S(1)} %get-tuple-element.19), channel_id=1, source_target_pairs={{0,16},{8,24},{16,0},{24,8},{1,17},{9,25},{17,1},{25,9},{2,18},{10... | collective-permute-start | bytes 442376 | tf_op jit(solution)/shard_map/ppermute | solution.py:18
  9.8 8.8 %collective-permute-done.8.refs_2_ = bf16[128,512]{1,0:T(8,128)(2,1)S(1)} collective-permute-done((bf16[128,512]{1,0:T(8,128)(2,1)S(1)}, bf16[128,512]{1,0:T(8,128)(2,1)S(1)}, u32[]{:S(2)}, u32[]{:S(2)}) %collective-permute-start.8) | collective-permute-done | bytes 131104 | tf_op jit(solution)/shard_map/ppermute | solution.py:18
  18.6 2.0 %collective-permute-start.3 = (bf16[144,512]{1,0:T(8,128)(2,1)S(1)}, bf16[144,512]{1,0:T(8,128)(2,1)S(1)}, u32[]{:S(2)}, u32[]{:S(2)}) collective-permute-start(bf16[144,512]{1,0:T(8,128)(2,1)S(1)} %get-tuple-element.17.refs_0_), channel_id=1, source_target_pairs={{0,4},{4,0},{1,5},{5,1},{2,6},{6,2},{3,7},{7,3},{8,12},{12,8},{9,1... | collective-permute-start | bytes 442376 | tf_op jit(solution)/shard_map/ppermute | solution.py:18
  20.7 2.0 %collective-permute-start.5 = (bf16[144,512]{1,0:T(8,128)(2,1)S(1)}, bf16[144,512]{1,0:T(8,128)(2,1)S(1)}, u32[]{:S(2)}, u32[]{:S(2)}) collective-permute-start(bf16[144,512]{1,0:T(8,128)(2,1)S(1)} %collective-permute-done.1.refs_2_), channel_id=1, source_target_pairs={{0,4},{4,0},{1,5},{5,1},{2,6},{6,2},{3,7},{7,3},{8,12},{12,8},{9,1... | collective-permute-start | bytes 442376 | tf_op jit(solution)/shard_map/ppermute | solution.py:18
  22.9 2.0 %collective-permute-start.10 = (bf16[4,128,512]{2,1,0:T(8,128)(2,1)S(1)}, bf16[4,128,512]{2,1,0:T(8,128)(2,1)S(1)}, u32[]{:S(2)}, u32[]{:S(2)}) collective-permute-start(bf16[4,128,512]{2,1,0:T(8,128)(2,1)S(1)} %pad_maximum_fusion.refs_8_), channel_id=1, source_target_pairs={{0,4},{4,0},{1,5},{5,1},{2,6},{6,2},{3,7},{7,3},{8,12},{12,8},{9,1... | collective-permute-start | bytes 1572872 | tf_op jit(solution)/shard_map/ppermute | solution.py:18
  25.4 3.2 %collective-permute-done.4.refs_5_ = bf16[144,512]{1,0:T(8,128)(2,1)S(1)} collective-permute-done((bf16[144,512]{1,0:T(8,128)(2,1)S(1)}, bf16[144,512]{1,0:T(8,128)(2,1)S(1)}, u32[]{:S(2)}, u32[]{:S(2)}) %collective-permute-start.4) | collective-permute-done | bytes 147488 | tf_op jit(solution)/shard_map/ppermute | solution.py:18
  28.6 3.2 %collective-permute-done.5.refs_6_ = bf16[144,512]{1,0:T(8,128)(2,1)S(1)} collective-permute-done((bf16[144,512]{1,0:T(8,128)(2,1)S(1)}, bf16[144,512]{1,0:T(8,128)(2,1)S(1)}, u32[]{:S(2)}, u32[]{:S(2)}) %collective-permute-start.5) | collective-permute-done | bytes 147488 | tf_op jit(solution)/shard_map/ppermute | solution.py:18
  31.7 3.2 %collective-permute-done.6.refs_7_ = bf16[144,512]{1,0:T(8,128)(2,1)S(1)} collective-permute-done((bf16[144,512]{1,0:T(8,128)(2,1)S(1)}, bf16[144,512]{1,0:T(8,128)(2,1)S(1)}, u32[]{:S(2)}, u32[]{:S(2)}) %collective-permute-start.6) | collective-permute-done | bytes 147488 | tf_op jit(solution)/shard_map/ppermute | solution.py:18
  35.9 1.7 %convolution_convert_fusion.2 = bf16[16,64,352]{2,1,0:T(8,128)(2,1)S(1)} fusion(bf16[16,64,512]{2,1,0:T(8,128)(2,1)S(1)} %get-tuple-element.26.placed, bf16[16,512,352]{1,2,0:T(8,128)(2,1)S(1)} %bitcast.75), kind=kOutput, calls=%fused_computation.2 | convolution fusion | flops 369459200 | bytes 7536640 | tf_op jit(solution)/shard_map/esd,ehd->esh/dot_general | solution.py:262
  37.7 1.7 %convolution_convert_fusion.1 = bf16[16,64,352]{2,1,0:T(8,128)(2,1)S(1)} fusion(bf16[16,64,512]{2,1,0:T(8,128)(2,1)S(1)} %get-tuple-element.26.placed, bf16[16,512,352]{1,2,0:T(8,128)(2,1)S(1)} %bitcast.78), kind=kOutput, calls=%fused_computation.1 | convolution fusion | flops 369459200 | bytes 7536640 | tf_op jit(solution)/shard_map/esd,ehd->esh/dot_general | solution.py:262
  41.2 2.1 %collective-permute-start.17 = (bf16[2,16,16,352]{3,2,1,0:T(8,128)(2,1)S(1)}, bf16[2,16,16,352]{3,2,1,0:T(8,128)(2,1)S(1)}, u32[]{:S(2)}, u32[]{:S(2)}) collective-permute-start(bf16[2,16,16,352]{3,2,1,0:T(8,128)(2,1)S(1)} %pad_maximum_fusion.1.refs_6_), channel_id=1, source_target_pairs={{0,16},{8,24},{16,0},{24,8},{1,17},{9,25},{17,1},{25,9},{2,18},{10... | collective-permute-start | bytes 1081352 | tf_op jit(solution)/shard_map/ppermute | solution.py:18
  45.5 1.6 %convolution_convert_fusion = bf16[16,64,352]{2,1,0:T(8,128)(2,1)S(1)} fusion(bf16[16,64,512]{2,1,0:T(8,128)(2,1)S(1)} %shard_map.87, bf16[16,512,352]{1,2,0:T(8,128)(2,1)S(1)} %bitcast.82), kind=kOutput, calls=%fused_computation | convolution fusion | flops 369459200 | bytes 7536640 | tf_op jit(solution)/shard_map/esd,ehd->esh/dot_general | solution.py:262
  49.2 8.3 %collective-permute-done.14 = bf16[16,16,352]{2,1,0:T(8,128)(2,1)S(1)} collective-permute-done((bf16[16,16,352]{2,1,0:T(8,128)(2,1)S(1)}, bf16[16,16,352]{2,1,0:T(8,128)(2,1)S(1)}, u32[]{:S(2)}, u32[]{:S(2)}) %collective-permute-start.14) | collective-permute-done | bytes 180256 | tf_op jit(solution)/shard_map/ppermute | solution.py:18
  57.5 3.6 %collective-permute-done.15 = bf16[16,16,352]{2,1,0:T(8,128)(2,1)S(1)} collective-permute-done((bf16[16,16,352]{2,1,0:T(8,128)(2,1)S(1)}, bf16[16,16,352]{2,1,0:T(8,128)(2,1)S(1)}, u32[]{:S(2)}, u32[]{:S(2)}) %collective-permute-start.15) | collective-permute-done | bytes 180256 | tf_op jit(solution)/shard_map/ppermute | solution.py:18
  64.2 9.6 %collective-permute-done.20.h2 = bf16[2,16,16,352]{3,2,1,0:T(8,128)(2,1)S(1)} collective-permute-done((bf16[2,16,16,352]{3,2,1,0:T(8,128)(2,1)S(1)}, bf16[2,16,16,352]{3,2,1,0:T(8,128)(2,1)S(1)}, u32[]{:S(2)}, u32[]{:S(2)}) %collective-permute-start.20) | collective-permute-done | bytes 360480 | tf_op jit(solution)/shard_map/ppermute | solution.py:18
  73.7 1.7 %collective-permute-done.21.h3 = bf16[2,16,16,352]{3,2,1,0:T(8,128)(2,1)S(1)} collective-permute-done((bf16[2,16,16,352]{3,2,1,0:T(8,128)(2,1)S(1)}, bf16[2,16,16,352]{3,2,1,0:T(8,128)(2,1)S(1)}, u32[]{:S(2)}, u32[]{:S(2)}) %collective-permute-start.21) | collective-permute-done | bytes 360480 | tf_op jit(solution)/shard_map/ppermute | solution.py:18
  75.5 5.8 %shard_map.88 = (bf16[4,128,256]{2,1,0:T(8,128)(2,1)S(1)}, bf16[4,128,256]{2,1,0:T(8,128)(2,1)S(1)}, bf16[2,2,128,256]{3,2,1,0:T(8,128)(2,1)S(1)}, bf16[2,2,128,256]{3,2,1,0:T(8,128)(2,1)S(1)}) custom-call(s32[3]{0:T(128)S(1)} %pad_add_fusion.where, s32[4,8,256]{2,1,0:T(8,128)S(1)} %get-tuple-element.25.refs_4_.lines, ...), custom_call_target="tpu_custom_call" | custom-call | flops 2952790016 | bytes 11534336 | tf_op jit(solution)/shard_map/pallas_call | solution.py:181
  81.3 1.9 %collective-permute-start.24 = (bf16[2,2,128,256]{3,2,1,0:T(8,128)(2,1)S(1)}, bf16[2,2,128,256]{3,2,1,0:T(8,128)(2,1)S(1)}, u32[]{:S(2)}, u32[]{:S(2)}) collective-permute-start(bf16[2,2,128,256]{3,2,1,0:T(8,128)(2,1)S(1)} %get-tuple-element.30), channel_id=1, source_target_pairs={{0,1},{1,0},{2,3},{3,2},{4,5},{5,4},{6,7},{7,6},{8,9},{9,8},{10,11... | collective-permute-start | bytes 786440 | tf_op jit(solution)/shard_map/ppermute | solution.py:18
  84.6 4.0 %shard_map.90 = bf16[16,352,512]{2,1,0:T(8,128)(2,1)} custom-call(bf16[16,64,512]{2,1,0:T(8,128)(2,1)S(1)} %get-tuple-element.26.placed, bf16[2,16,16,352]{3,2,1,0:T(8,128)(2,1)S(1)} %pad_maximum_fusion.2.h0, bf16[2,16,16,352]{3,2,1,0:T(8,128)(2,1)S(1)} %collective-permute-done.19.h1, bf16[2,16,16,352]{3,2,1,0:T(8,128)(2,1)S(1)} %collective-permute-done.20.h2, ...), custom_call_target="tpu_custom_call" | custom-call | flops 1476395008 | bytes 5767168 | tf_op jit(solution)/shard_map/pallas_call | solution.py:214
  89.8 1.7 %collective-permute-start.25 = (bf16[2,128,256]{2,1,0:T(8,128)(2,1)S(1)}, bf16[2,128,256]{2,1,0:T(8,128)(2,1)S(1)}, u32[]{:S(2)}, u32[]{:S(2)}) collective-permute-start(bf16[2,128,256]{2,1,0:T(8,128)(2,1)S(1)} %fusion.8), channel_id=1, source_target_pairs={{0,4},{4,0},{1,5},{5,1},{2,6},{6,2},{3,7},{7,3},{8,12},{12,8},{9,1... | collective-permute-start | bytes 393224 | tf_op jit(solution)/shard_map/ppermute | solution.py:18
  94.9 1.8 %collective-permute-done.23 = bf16[2,128,256]{2,1,0:T(8,128)(2,1)S(1)} collective-permute-done((bf16[2,128,256]{2,1,0:T(8,128)(2,1)S(1)}, bf16[2,128,256]{2,1,0:T(8,128)(2,1)S(1)}, u32[]{:S(2)}, u32[]{:S(2)}) %collective-permute-start.23) | collective-permute-done | bytes 131104 | tf_op jit(solution)/shard_map/ppermute | solution.py:18
  97.4 5.3 %collective-permute-start.27 = (bf16[128,512]{1,0:T(8,128)(2,1)S(1)}, bf16[128,512]{1,0:T(8,128)(2,1)S(1)}, u32[]{:S(2)}, u32[]{:S(2)}) collective-permute-start(bf16[128,512]{1,0:T(8,128)(2,1)S(1)} %pad_maximum_fusion.5), channel_id=1, source_target_pairs={{0,16},{1,24},{2,0},{3,8},{8,17},{9,25},{10,1},{11,9},{16,18},{17,... | collective-permute-start | bytes 393224 | tf_op jit(solution)/shard_map/ppermute | solution.py:293
  102.8 4.0 %shard_map.89 = bf16[16,352,512]{2,1,0:T(8,128)(2,1)} custom-call(bf16[16,64,512]{2,1,0:T(8,128)(2,1)S(1)} %get-tuple-element.26.placed, bf16[2,16,16,352]{3,2,1,0:T(8,128)(2,1)S(1)} %pad_maximum_fusion.2.h0, bf16[2,16,16,352]{3,2,1,0:T(8,128)(2,1)S(1)} %collective-permute-done.19.h1, bf16[2,16,16,352]{3,2,1,0:T(8,128)(2,1)S(1)} %collective-permute-done.20.h2, ...), custom_call_target="tpu_custom_call" | custom-call | flops 1476395008 | bytes 5767168 | tf_op jit(solution)/shard_map/pallas_call | solution.py:214
  106.8 6.7 %collective-permute-done.27 = bf16[128,512]{1,0:T(8,128)(2,1)S(1)} collective-permute-done((bf16[128,512]{1,0:T(8,128)(2,1)S(1)}, bf16[128,512]{1,0:T(8,128)(2,1)S(1)}, u32[]{:S(2)}, u32[]{:S(2)}) %collective-permute-start.27) | collective-permute-done | bytes 131104 | tf_op jit(solution)/shard_map/ppermute | solution.py:293
  (84 shorter events, 24.4 us)
Async XLA Ops:
  4.5 5.0 %collective-permute-start.7 = (bf16[128,512]{1,0:T(8,128)(2,1)S(1)}, bf16[128,512]{1,0:T(8,128)(2,1)S(1)}, u32[]{:S(2)}, u32[]{:S(2)}) collective-permute-start(bf16[128,512]{1,0:T(8,128)(2,1)S(1)} %get-tuple-element.22), channel_id=1, source_target_pairs={{0,8},{8,0},{16,24},{24,16},{1,9},{9,1},{17,25},{25,17},{2,10},{10... | collective-permute-start | bytes 393224 | tf_op jit(solution)/shard_map/ppermute | solution.py:18
  5.0 15.7 %collective-permute-start = (bf16[144,512]{1,0:T(8,128)(2,1)S(1)}, bf16[144,512]{1,0:T(8,128)(2,1)S(1)}, u32[]{:S(2)}, u32[]{:S(2)}) collective-permute-start(bf16[144,512]{1,0:T(8,128)(2,1)S(1)} %get-tuple-element.18), channel_id=1, source_target_pairs={{0,8},{8,0},{16,24},{24,16},{1,9},{9,1},{17,25},{25,17},{2,10},{10... | collective-permute-start | bytes 442376 | tf_op jit(solution)/shard_map/ppermute | solution.py:18
  5.1 15.6 %collective-permute-start.1 = (bf16[144,512]{1,0:T(8,128)(2,1)S(1)}, bf16[144,512]{1,0:T(8,128)(2,1)S(1)}, u32[]{:S(2)}, u32[]{:S(2)}) collective-permute-start(bf16[144,512]{1,0:T(8,128)(2,1)S(1)} %get-tuple-element.19), channel_id=1, source_target_pairs={{0,16},{8,24},{16,0},{24,8},{1,17},{9,25},{17,1},{25,9},{2,18},{10... | collective-permute-start | bytes 442376 | tf_op jit(solution)/shard_map/ppermute | solution.py:18
  8.0 14.7 %collective-permute-start.2 = (bf16[144,512]{1,0:T(8,128)(2,1)S(1)}, bf16[144,512]{1,0:T(8,128)(2,1)S(1)}, u32[]{:S(2)}, u32[]{:S(2)}) collective-permute-start(bf16[144,512]{1,0:T(8,128)(2,1)S(1)} %get-tuple-element.20), channel_id=1, source_target_pairs={{0,24},{8,16},{16,8},{24,0},{1,25},{9,17},{17,9},{25,1},{2,26},{10... | collective-permute-start | bytes 442376 | tf_op jit(solution)/shard_map/ppermute | solution.py:18
  8.0 10.6 %collective-permute-start.8 = (bf16[128,512]{1,0:T(8,128)(2,1)S(1)}, bf16[128,512]{1,0:T(8,128)(2,1)S(1)}, u32[]{:S(2)}, u32[]{:S(2)}) collective-permute-start(bf16[128,512]{1,0:T(8,128)(2,1)S(1)} %get-tuple-element.23), channel_id=1, source_target_pairs={{0,16},{8,24},{16,0},{24,8},{1,17},{9,25},{17,1},{25,9},{2,18},{10... | collective-permute-start | bytes 393224 | tf_op jit(solution)/shard_map/ppermute | solution.py:18
  9.5 13.3 %collective-permute-start.9 = (bf16[128,512]{1,0:T(8,128)(2,1)S(1)}, bf16[128,512]{1,0:T(8,128)(2,1)S(1)}, u32[]{:S(2)}, u32[]{:S(2)}) collective-permute-start(bf16[128,512]{1,0:T(8,128)(2,1)S(1)} %get-tuple-element.24), channel_id=1, source_target_pairs={{0,24},{8,16},{16,8},{24,0},{1,25},{9,17},{17,9},{25,1},{2,26},{10... | collective-permute-start | bytes 393224 | tf_op jit(solution)/shard_map/ppermute | solution.py:18
  18.6 6.8 %collective-permute-start.3 = (bf16[144,512]{1,0:T(8,128)(2,1)S(1)}, bf16[144,512]{1,0:T(8,128)(2,1)S(1)}, u32[]{:S(2)}, u32[]{:S(2)}) collective-permute-start(bf16[144,512]{1,0:T(8,128)(2,1)S(1)} %get-tuple-element.17.refs_0_), channel_id=1, source_target_pairs={{0,4},{4,0},{1,5},{5,1},{2,6},{6,2},{3,7},{7,3},{8,12},{12,8},{9,1... | collective-permute-start | bytes 442376 | tf_op jit(solution)/shard_map/ppermute | solution.py:18
  20.7 7.9 %collective-permute-start.4 = (bf16[144,512]{1,0:T(8,128)(2,1)S(1)}, bf16[144,512]{1,0:T(8,128)(2,1)S(1)}, u32[]{:S(2)}, u32[]{:S(2)}) collective-permute-start(bf16[144,512]{1,0:T(8,128)(2,1)S(1)} %collective-permute-done.refs_1_), channel_id=1, source_target_pairs={{0,4},{4,0},{1,5},{5,1},{2,6},{6,2},{3,7},{7,3},{8,12},{12,8},{9,1... | collective-permute-start | bytes 442376 | tf_op jit(solution)/shard_map/ppermute | solution.py:18
  20.7 11.0 %collective-permute-start.5 = (bf16[144,512]{1,0:T(8,128)(2,1)S(1)}, bf16[144,512]{1,0:T(8,128)(2,1)S(1)}, u32[]{:S(2)}, u32[]{:S(2)}) collective-permute-start(bf16[144,512]{1,0:T(8,128)(2,1)S(1)} %collective-permute-done.1.refs_2_), channel_id=1, source_target_pairs={{0,4},{4,0},{1,5},{5,1},{2,6},{6,2},{3,7},{7,3},{8,12},{12,8},{9,1... | collective-permute-start | bytes 442376 | tf_op jit(solution)/shard_map/ppermute | solution.py:18
  22.7 12.2 %collective-permute-start.6 = (bf16[144,512]{1,0:T(8,128)(2,1)S(1)}, bf16[144,512]{1,0:T(8,128)(2,1)S(1)}, u32[]{:S(2)}, u32[]{:S(2)}) collective-permute-start(bf16[144,512]{1,0:T(8,128)(2,1)S(1)} %collective-permute-done.2.refs_3_), channel_id=1, source_target_pairs={{0,4},{4,0},{1,5},{5,1},{2,6},{6,2},{3,7},{7,3},{8,12},{12,8},{9,1... | collective-permute-start | bytes 442376 | tf_op jit(solution)/shard_map/ppermute | solution.py:18
  22.9 21.2 %collective-permute-start.10 = (bf16[4,128,512]{2,1,0:T(8,128)(2,1)S(1)}, bf16[4,128,512]{2,1,0:T(8,128)(2,1)S(1)}, u32[]{:S(2)}, u32[]{:S(2)}) collective-permute-start(bf16[4,128,512]{2,1,0:T(8,128)(2,1)S(1)} %pad_maximum_fusion.refs_8_), channel_id=1, source_target_pairs={{0,4},{4,0},{1,5},{5,1},{2,6},{6,2},{3,7},{7,3},{8,12},{12,8},{9,1... | collective-permute-start | bytes 1572872 | tf_op jit(solution)/shard_map/ppermute | solution.py:18
  40.0 8.8 %collective-permute-start.16 = (bf16[16,16,352]{2,1,0:T(8,128)(2,1)S(1)}, bf16[16,16,352]{2,1,0:T(8,128)(2,1)S(1)}, u32[]{:S(2)}, u32[]{:S(2)}) collective-permute-start(bf16[16,16,352]{2,1,0:T(8,128)(2,1)S(1)} %get-tuple-element.33), channel_id=1, source_target_pairs={{0,8},{8,0},{16,24},{24,16},{1,9},{9,1},{17,25},{25,17},{2,10},{10... | collective-permute-start | bytes 540680 | tf_op jit(solution)/shard_map/ppermute | solution.py:18
  40.1 9.1 %collective-permute-start.18 = (bf16[16,16,352]{2,1,0:T(8,128)(2,1)S(1)}, bf16[16,16,352]{2,1,0:T(8,128)(2,1)S(1)}, u32[]{:S(2)}, u32[]{:S(2)}) collective-permute-start(bf16[16,16,352]{2,1,0:T(8,128)(2,1)S(1)} %get-tuple-element.39), channel_id=1, source_target_pairs={{0,8},{8,0},{16,24},{24,16},{1,9},{9,1},{17,25},{25,17},{2,10},{10... | collective-permute-start | bytes 540680 | tf_op jit(solution)/shard_map/ppermute | solution.py:18
  41.2 19.9 %collective-permute-start.17 = (bf16[2,16,16,352]{3,2,1,0:T(8,128)(2,1)S(1)}, bf16[2,16,16,352]{3,2,1,0:T(8,128)(2,1)S(1)}, u32[]{:S(2)}, u32[]{:S(2)}) collective-permute-start(bf16[2,16,16,352]{3,2,1,0:T(8,128)(2,1)S(1)} %pad_maximum_fusion.1.refs_6_), channel_id=1, source_target_pairs={{0,16},{8,24},{16,0},{24,8},{1,17},{9,25},{17,1},{25,9},{2,18},{10... | collective-permute-start | bytes 1081352 | tf_op jit(solution)/shard_map/ppermute | solution.py:18
  47.3 10.2 %collective-permute-start.14 = (bf16[16,16,352]{2,1,0:T(8,128)(2,1)S(1)}, bf16[16,16,352]{2,1,0:T(8,128)(2,1)S(1)}, u32[]{:S(2)}, u32[]{:S(2)}) collective-permute-start(bf16[16,16,352]{2,1,0:T(8,128)(2,1)S(1)} %get-tuple-element.37), channel_id=1, source_target_pairs={{0,16},{8,24},{16,0},{24,8},{1,17},{9,25},{17,1},{25,9},{2,18},{10... | collective-permute-start | bytes 540680 | tf_op jit(solution)/shard_map/ppermute | solution.py:18
  48.8 12.3 %collective-permute-start.15 = (bf16[16,16,352]{2,1,0:T(8,128)(2,1)S(1)}, bf16[16,16,352]{2,1,0:T(8,128)(2,1)S(1)}, u32[]{:S(2)}, u32[]{:S(2)}) collective-permute-start(bf16[16,16,352]{2,1,0:T(8,128)(2,1)S(1)} %get-tuple-element.36), channel_id=1, source_target_pairs={{0,24},{8,16},{16,8},{24,0},{1,25},{9,17},{17,9},{25,1},{2,26},{10... | collective-permute-start | bytes 540680 | tf_op jit(solution)/shard_map/ppermute | solution.py:18
  62.5 11.2 %collective-permute-start.20 = (bf16[2,16,16,352]{3,2,1,0:T(8,128)(2,1)S(1)}, bf16[2,16,16,352]{3,2,1,0:T(8,128)(2,1)S(1)}, u32[]{:S(2)}, u32[]{:S(2)}) collective-permute-start(bf16[2,16,16,352]{3,2,1,0:T(8,128)(2,1)S(1)} %pad_maximum_fusion.2.h0), channel_id=1, source_target_pairs={{0,16},{8,24},{16,0},{24,8},{1,17},{9,25},{17,1},{25,9},{2,18},{10... | collective-permute-start | bytes 1081352 | tf_op jit(solution)/shard_map/ppermute | solution.py:18
  64.1 9.6 %collective-permute-start.19 = (bf16[2,16,16,352]{3,2,1,0:T(8,128)(2,1)S(1)}, bf16[2,16,16,352]{3,2,1,0:T(8,128)(2,1)S(1)}, u32[]{:S(2)}, u32[]{:S(2)}) collective-permute-start(bf16[2,16,16,352]{3,2,1,0:T(8,128)(2,1)S(1)} %pad_maximum_fusion.2.h0), channel_id=1, source_target_pairs={{0,8},{8,0},{16,24},{24,16},{1,9},{9,1},{17,25},{25,17},{2,10},{10... | collective-permute-start | bytes 1081352 | tf_op jit(solution)/shard_map/ppermute | solution.py:18
  81.3 8.5 %collective-permute-start.24 = (bf16[2,2,128,256]{3,2,1,0:T(8,128)(2,1)S(1)}, bf16[2,2,128,256]{3,2,1,0:T(8,128)(2,1)S(1)}, u32[]{:S(2)}, u32[]{:S(2)}) collective-permute-start(bf16[2,2,128,256]{3,2,1,0:T(8,128)(2,1)S(1)} %get-tuple-element.30), channel_id=1, source_target_pairs={{0,1},{1,0},{2,3},{3,2},{4,5},{5,4},{6,7},{7,6},{8,9},{9,8},{10,11... | collective-permute-start | bytes 786440 | tf_op jit(solution)/shard_map/ppermute | solution.py:18
  83.1 8.4 %collective-permute-start.22 = (bf16[4,128,256]{2,1,0:T(8,128)(2,1)S(1)}, bf16[4,128,256]{2,1,0:T(8,128)(2,1)S(1)}, u32[]{:S(2)}, u32[]{:S(2)}) collective-permute-start(bf16[4,128,256]{2,1,0:T(8,128)(2,1)S(1)} %get-tuple-element.28), channel_id=1, source_target_pairs={{0,4},{4,0},{1,5},{5,1},{2,6},{6,2},{3,7},{7,3},{8,12},{12,8},{9,1... | collective-permute-start | bytes 786440 | tf_op jit(solution)/shard_map/ppermute | solution.py:18
  89.8 5.0 %collective-permute-start.25 = (bf16[2,128,256]{2,1,0:T(8,128)(2,1)S(1)}, bf16[2,128,256]{2,1,0:T(8,128)(2,1)S(1)}, u32[]{:S(2)}, u32[]{:S(2)}) collective-permute-start(bf16[2,128,256]{2,1,0:T(8,128)(2,1)S(1)} %fusion.8), channel_id=1, source_target_pairs={{0,4},{4,0},{1,5},{5,1},{2,6},{6,2},{3,7},{7,3},{8,12},{12,8},{9,1... | collective-permute-start | bytes 393224 | tf_op jit(solution)/shard_map/ppermute | solution.py:18
  91.6 5.0 %collective-permute-start.23 = (bf16[2,128,256]{2,1,0:T(8,128)(2,1)S(1)}, bf16[2,128,256]{2,1,0:T(8,128)(2,1)S(1)}, u32[]{:S(2)}, u32[]{:S(2)}) collective-permute-start(bf16[2,128,256]{2,1,0:T(8,128)(2,1)S(1)} %pad_maximum_fusion.3), channel_id=1, source_target_pairs={{0,1},{1,0},{2,3},{3,2},{4,5},{5,4},{6,7},{7,6},{8,9},{9,8},{10,11... | collective-permute-start | bytes 393224 | tf_op jit(solution)/shard_map/ppermute | solution.py:18
  96.7 10.1 %collective-permute-start.26 = (bf16[128,512]{1,0:T(8,128)(2,1)S(1)}, bf16[128,512]{1,0:T(8,128)(2,1)S(1)}, u32[]{:S(2)}, u32[]{:S(2)}) collective-permute-start(bf16[128,512]{1,0:T(8,128)(2,1)S(1)} %pad_maximum_fusion.4), channel_id=1, source_target_pairs={{0,0},{1,8},{2,16},{3,24},{8,1},{9,9},{10,17},{11,25},{16,2},{17,1... | collective-permute-start | bytes 393224 | tf_op jit(solution)/shard_map/ppermute | solution.py:292
  97.4 16.0 %collective-permute-start.27 = (bf16[128,512]{1,0:T(8,128)(2,1)S(1)}, bf16[128,512]{1,0:T(8,128)(2,1)S(1)}, u32[]{:S(2)}, u32[]{:S(2)}) collective-permute-start(bf16[128,512]{1,0:T(8,128)(2,1)S(1)} %pad_maximum_fusion.5), channel_id=1, source_target_pairs={{0,16},{1,24},{2,0},{3,8},{8,17},{9,25},{10,1},{11,9},{16,18},{17,... | collective-permute-start | bytes 393224 | tf_op jit(solution)/shard_map/ppermute | solution.py:293
  (14 other events, 77.6 us)

commit v3 on v2

--- a/solution.py
+++ b/solution.py
@@ -12,6 +12,7 @@
 F32 = jnp.float32
 BF16 = jnp.bfloat16
 VMEM_LIMIT = 48 * 1024 * 1024
+PLACE_COST = 1 << 34
 
 
 def swap(value, axis, count, bit):
@@ -33,10 +34,11 @@
     copies = []
     for rel in range(n_dp):
         start = pl.multiple_of((k ^ rel) * width, 128)
-        for which, source in enumerate((tokens, cotangent)):
-            out = outs[which * n_dp + rel]
+        for which, (source, first) in enumerate(((tokens, 0), (cotangent, rows + META))):
             copy = pltpu.make_async_copy(
-                source.at[:, pl.ds(start, width)], out.at[pl.ds(0, rows), :], sems.at[which * n_dp + rel]
+                source.at[:, pl.ds(start, width)],
+                outs[rel].at[pl.ds(first, rows), :],
+                sems.at[which * n_dp + rel],
             )
             copy.start()
             copies.append(copy)
@@ -60,18 +62,18 @@
 
 def split(where, ids, tokens, cotangent, width, n_dp):
     rows = tokens.shape[0]
-    tall, low = (rows + META, width), (rows, width)
+    pack = (2 * rows + META, width)
     anywhere = pl.BlockSpec(memory_space=pl.ANY)
     return pl.pallas_call(
         functools.partial(split_kernel, width, n_dp),
-        out_shape=[jax.ShapeDtypeStruct(s, BF16) for s in [tall] * n_dp + [low] * n_dp],
+        out_shape=[jax.ShapeDtypeStruct(pack, BF16)] * n_dp,
         in_specs=[
             pl.BlockSpec(memory_space=pltpu.SMEM),
             pl.BlockSpec(memory_space=pltpu.VMEM),
             anywhere,
             anywhere,
         ],
-        out_specs=[anywhere] * (2 * n_dp),
+        out_specs=[anywhere] * n_dp,
         scratch_shapes=[pltpu.VMEM((META, width), BF16), pltpu.SemaphoreType.DMA((3 * n_dp,))],
         compiler_params=params(),
     )(where, ids, tokens, cotangent)
@@ -82,58 +84,59 @@
     return (every == row).astype(F32).astype(BF16)
 
 
-def place_kernel(order, first, after, where, *refs):
-    n_dp = len(order)
+def place_kernel(first, rows, where, mine, near, late, *refs):
+    n_dp = len(mine)
+    other = [near.at[0], near.at[1], late.at[0], late.at[1]]
     if first:
-        mine, other, refs = refs[:n_dp], refs[n_dp : 2 * n_dp], refs[2 * n_dp + after :]
-        placed, lines = refs
+        placed, lines = refs[-2:]
     else:
-        mine, lines, refs = refs[:n_dp], refs[n_dp], refs[n_dp + 1 :]
-        halves, (placed,) = refs[: len(refs) - after - 1], refs[-1:]
-        other = [half.at[i] for half in halves for i in range(half.shape[0])]
+        lines, placed = refs[0], refs[-1]
     local_experts, slot_rows, width = placed.shape
     slots = slot_rows // n_dp
-    rows = mine[0].shape[0] - (META if first else 0)
-    for at, rel in enumerate(order):
-        pair = mine[rel], other[rel]
+    for rel in range(n_dp):
         if first:
+            pair = [b[0 : rows + META, :] for b in (mine[rel], other[rel])]
             metas = [b[rows:, 0:rows].astype(F32) for b in pair]
             ids = jnp.concatenate([m[0:1] for m in metas], axis=1)
             place = jnp.concatenate([m[1:2] for m in metas], axis=1)
             low = (where[1] * local_experts).astype(F32)
             row = ((ids - low) * slots + place).astype(jnp.int32)
             lines[rel] = jnp.broadcast_to(row, (8, row.shape[1]))
+            pair = [b[0:rows] for b in pair]
         else:
             row = lines[rel][0:1]
+            pair = [b[b.shape[0] - rows :, :] for b in (mine[rel], other[rel])]
         placer = placer_of(row, local_experts * slots)
-        values = jnp.concatenate([b[0:rows, :] for b in pair], axis=0)
-        found = jnp.dot(placer, values, preferred_element_type=F32).astype(BF16)
-        placed[:, at * slots : (at + 1) * slots, :] = found.reshape(local_experts, slots, width)
-
-
-def place(order, where, mine, other, lines, local_experts, after, cost):
+        found = jnp.dot(placer, jnp.concatenate(pair, axis=0), preferred_element_type=F32).astype(BF16)
+        placed[:, rel * slots : (rel + 1) * slots, :] = found.reshape(local_experts, slots, width)
+
+
+def place(where, mine, near, late, lines, rows, local_experts, after):
     first = lines is None
-    n_dp, slots = len(order), 2 * CAP
+    n_dp, slots = len(mine), 2 * CAP
     width = mine[0].shape[1]
-    rows = mine[0].shape[0] - (META if first else 0)
     placed = jax.ShapeDtypeStruct((local_experts, n_dp * slots, width), BF16)
     line = jax.ShapeDtypeStruct((n_dp, 8, 2 * rows), jnp.int32)
-    near = pl.BlockSpec(memory_space=pltpu.VMEM)
-    operands = [*mine] + ([] if first else [lines]) + [*other]
+    vmem = pl.BlockSpec(memory_space=pltpu.VMEM)
+    operands = [near, late] + ([] if first else [lines])
+
+    def kernel(where, *refs):
+        place_kernel(first, rows, where, refs[:n_dp], *refs[n_dp:])
+
     return pl.pallas_call(
-        functools.partial(place_kernel, order, first, len(after)),
+        kernel,
         out_shape=[placed, line] if first else placed,
         in_specs=[pl.BlockSpec(memory_space=pltpu.SMEM)]
-        + [near] * len(operands)
+        + [vmem] * (n_dp + len(operands))
         + [pl.BlockSpec(memory_space=pl.ANY)] * len(after),
-        out_specs=[near, near] if first else near,
+        out_specs=[vmem, vmem] if first else vmem,
         compiler_params=params(),
-        cost_estimate=pl.CostEstimate(flops=cost, bytes_accessed=4 * rows * width * n_dp, transcendentals=0),
-    )(where, *operands, *after)
-
-
-def back_kernel(n_dp, where, lines, h0, h1, h2, h3, gate, up, keep_x, send_x, keep_z, send_z, near, held, sems):
-    parts = (h0, h1, h2, h3)
+        cost_estimate=pl.CostEstimate(flops=PLACE_COST, bytes_accessed=4 * rows * width * n_dp, transcendentals=0),
+    )(where, *mine, *operands, *after)
+
+
+def back_kernel(rels, lines, h0, h1, gate, up, own0, own1, other0, other1, near, held, sems):
+    parts = (h0, h1)
     local_experts, slots = h0.shape[1], h0.shape[2]
     per_copy = local_experts // sems.shape[1]
 
@@ -153,48 +156,39 @@
             value = jnp.dot(gate_grad, near[0, e], preferred_element_type=F32)
             value = value + jnp.dot(up_grad, near[1, e], preferred_element_type=F32)
             value = value.astype(BF16)
-            for rel in range(n_dp):
-                held[rel, e * slots : (e + 1) * slots, :] = value[rel * slots : (rel + 1) * slots]
-
-    rows, half = keep_x.shape[1], keep_x.shape[2]
-    for r in range(n_dp):
-        rel = where[2] ^ r
-        placer = placer_of(lines[rel][0:1], held.shape[1])
+            for i in range(2):
+                held[i, e * slots : (e + 1) * slots, :] = value[i * slots : (i + 1) * slots]
+
+    rows = own0.shape[0]
+    for i, (own, other) in enumerate(((own0, other0), (own1, other1))):
+        placer = placer_of(lines[rels[i]][0:1], held.shape[1])
         token_rows = lax.dot_general(
-            placer, held[rel], (((0,), (0,)), ((), ())), preferred_element_type=F32
+            placer, held[i], (((0,), (0,)), ((), ())), preferred_element_type=F32
         ).astype(BF16)
-        keep_x[r] = token_rows[0:rows, 0:half]
-        send_x[r] = token_rows[rows:, 0:half]
-        out = send_z if r & 1 else keep_z
-        out[0, r // 2] = token_rows[0:rows, half:]
-        out[1, r // 2] = token_rows[rows:, half:]
-
-
-def back(where, lines, parts, gate, up, rows):
-    n_dp = len(parts)
+        own[...] = token_rows[0:rows]
+        other[...] = token_rows[rows:]
+
+
+def back(rels, lines, parts, gate, up, rows):
     local_experts, hidden, width = gate.shape
     slots = parts[0].shape[2]
-    shape_x = (n_dp, rows, width // 2)
-    shape_z = (2, n_dp // 2, rows, width // 2)
-    near = pl.BlockSpec(memory_space=pltpu.VMEM)
-    flops = 4 * local_experts * n_dp * slots * width * hidden
+    vmem = pl.BlockSpec(memory_space=pltpu.VMEM)
+    flops = 4 * local_experts * 2 * slots * width * hidden
     return pl.pallas_call(
-        functools.partial(back_kernel, n_dp),
-        out_shape=[jax.ShapeDtypeStruct(s, BF16) for s in (shape_x, shape_x, shape_z, shape_z)],
-        in_specs=[pl.BlockSpec(memory_space=pltpu.SMEM)]
-        + [near] * (1 + n_dp)
-        + [pl.BlockSpec(memory_space=pl.ANY)] * 2,
-        out_specs=[near] * 4,
+        functools.partial(back_kernel, rels),
+        out_shape=[jax.ShapeDtypeStruct((rows, width), BF16)] * 4,
+        in_specs=[vmem] * 3 + [pl.BlockSpec(memory_space=pl.ANY)] * 2,
+        out_specs=[vmem] * 4,
         scratch_shapes=[
             pltpu.VMEM((2, local_experts, hidden, width), BF16),
-            pltpu.VMEM((n_dp, local_experts * slots, width), BF16),
+            pltpu.VMEM((2, local_experts * slots, width), BF16),
             pltpu.SemaphoreType.DMA((2, 8 if local_experts % 8 == 0 else 1)),
         ],
         compiler_params=params(),
         cost_estimate=pl.CostEstimate(
             flops=4 * flops, bytes_accessed=2 * local_experts * width * hidden * 2, transcendentals=0
         ),
-    )(where, lines, *parts, gate, up)
+    )(lines, *parts, gate, up)
 
 
 def weight_kernel(which, order, placed, h0, h1, h2, h3, out):
@@ -242,16 +236,15 @@
     k, x, t = lax.axis_index("dp"), lax.axis_index("expert"), lax.axis_index("tensor")
     width = gate_weight.shape[1]
     rows = tokens.shape[0]
-    half = width // 2
-    where = jnp.stack([k, x, k ^ t]).astype(jnp.int32)
-
-    chunks = split(where, expert_ids.reshape(1, rows), tokens, cotangent, width, n_dp)
-
-    own = [c if i % n_dp == 0 else swap(c, "dp", n_dp, i % n_dp) for i, c in enumerate(chunks)]
-    own_tokens, own_grads = own[:n_dp], own[n_dp:]
-    other_tokens = [swap(c, "expert", n_x, 1) for c in own_tokens]
-    all_grads = jnp.stack(own_grads)
-    other_grads = swap(all_grads, "expert", n_x, 1)
+    where = jnp.stack([k, x]).astype(jnp.int32)
+    packs = split(where, expert_ids.reshape(1, rows), tokens, cotangent, width, n_dp)
+    own = [pack if rel == 0 else swap(pack, "dp", n_dp, rel) for rel, pack in enumerate(packs)]
+    near_packs = swap(jnp.stack(own[:2]), "expert", n_x, 1)
+    leaving_tokens = jnp.stack([o[: rows + META] for o in own[2:]])
+    near_packs, leaving_tokens = lax.optimization_barrier((near_packs, leaving_tokens))
+    late_tokens = swap(leaving_tokens, "expert", n_x, 1)
+    leaving_grads = jnp.stack([o[rows + META :] for o in own[2:]])
+    late_grads = swap(leaving_grads, "expert", n_x, 1)
     gate_weight, up_weight, down_weight = (
         jnp.swapaxes(weight, 1, 2) for weight in (gate_weight, up_weight, down_weight)
     )
@@ -266,12 +259,12 @@
         near, far = swap(act[1], "dp", n_dp, 1), swap(act[3], "dp", n_dp, 1)
         return plus(act[0], near), plus(act[2], far).astype(BF16)
 
-    placed, lines = place(order, where, own_tokens, other_tokens, None, local_experts, [all_grads], 1 << 34)
+    placed, lines = place(where, own, near_packs, late_tokens, None, rows, local_experts, [leaving_grads])
     gate_near, gate_far = near_and_far(project(placed, gate_weight))
     up_near, up_far = near_and_far(project(placed, up_weight))
     far = jnp.stack([gate_far, up_far])
     there = swap(far, "dp", n_dp, 2)
-    placed_grads = place(order, where, own_grads, [other_grads], lines, local_experts, [far], 1 << 34)
+    placed_grads = place(where, own, near_packs, late_grads, lines, rows, local_experts, [far])
     hidden_act = project(placed_grads, down_weight)
     hidden_grad = hidden_act[0].astype(F32)
     for rel in range(1, n_dp):
@@ -279,19 +272,35 @@
     acts = plus(gate_near, there[0]), plus(up_near, there[1])
     part = jnp.stack(swiglu_grads(acts[0], acts[1], hidden_grad))
     far = swap(part, "dp", n_dp, 2)
-    parts = [part, swap(part, "dp", n_dp, 1), far, swap(far, "dp", n_dp, 1)]
-
-    keep_x, send_x, keep_z, send_z = back(where, lines, parts, gate_weight, up_weight, rows)
-    sum_x = plus(keep_x, swap(send_x, "expert", n_x, 1))
-    sum_z = plus(keep_z, swap(send_z, "tensor", n_t, 1))
-    from_z = swap(jnp.stack([sum_x[1], sum_x[3]]).astype(BF16), "tensor", n_t, 1)
-    from_x = swap(sum_z[1].astype(BF16), "expert", n_x, 1)
-    near = jnp.concatenate([plus(sum_x[0], from_z[0]), plus(sum_z[0, 0], from_x[0])], axis=1).astype(BF16)
-    far = jnp.concatenate([plus(sum_x[2], from_z[1]), plus(sum_z[0, 1], from_x[1])], axis=1).astype(BF16)
-    pairs = [(i, j) for i in range(n_dp) for j in range(n_t)]
-    near = lax.ppermute(near, ("dp", "tensor"), [(i * n_t + j, j * n_t + i) for i, j in pairs])
-    far = lax.ppermute(far, ("dp", "tensor"), [(i * n_t + j, (j ^ 2) * n_t + i) for i, j in pairs])
-    grad_tokens = plus(near, far).astype(BF16)
+    beside = swap(part, "dp", n_dp, 1)
+    near_back = back((0, 1), lines, [part, beside], gate_weight, up_weight, rows)
+    far, near_back = lax.optimization_barrier((far, near_back))
+    parts = [part, beside, far, swap(far, "dp", n_dp, 1)]
+    far_back = back((2, 3), lines, parts[2:], gate_weight, up_weight, rows)
+
+    def to_owner(value, rel, flip):
+        if rel == 0 and flip == 0:
+            return value
+        pairs = [
+            (i * n_x + j, (i ^ rel) * n_x + (j ^ flip)) for i in range(n_dp) for j in range(n_x)
+        ]
+        return lax.ppermute(value, ("dp", "expert"), pairs)
+
+    def blocks(rels, own0, own1, other0, other1):
+        terms = [
+            plus(to_owner(own_r, rel, 0), to_owner(other_r, rel, 1)).astype(BF16)
+            for rel, own_r, other_r in zip(rels, (own0, own1), (other0, other1))
+        ]
+        odd = ((k ^ t) & 1) == 1
+        keep = jnp.where(odd, terms[1], terms[0])
+        leaving = jnp.where(odd, terms[0], terms[1])
+        return plus(keep, swap(leaving, "tensor", n_t, 1))
+
+    first, second = blocks((0, 1), *near_back), blocks((2, 3), *far_back)
+    swapped = ((k ^ t) & 2) == 2
+    keep = jnp.where(swapped, second, first)
+    leaving = jnp.where(swapped, first, second).astype(BF16)
+    grad_tokens = plus(keep, swap(leaving, "tensor", n_t, 2)).astype(BF16)
 
     grad_gate = jnp.swapaxes(weight_grad(0, order, placed, parts, 4), 1, 2)
     grad_up = jnp.swapaxes(weight_grad(1, order, placed, parts, 4), 1, 2)

time: 114 us -> 111 us (0.974)
  waiting for transfers between devices: 54.4 us -> 48.6 us
  Pallas kernels: 16.8 us -> 21.1 us
  starting transfers between devices: 31.1 us -> 27.2 us
  matrix products: 4.95 us -> 7.61 us
    ppermute x26 -> x20, waiting for transfers between devices: 47.7 us -> 40.8 us  [swap(): return lax.ppermute(value, axis, [(i, i ^ bit) for i in range(count)])]
    ppermute x26 -> x20, starting transfers between devices: 25 us -> 20.3 us  [swap(): return lax.ppermute(value, axis, [(i, i ^ bit) for i in range(count)])]
    pallas_call x3 -> x4, Pallas kernels: 7.74 us -> 12 us  [the longest x2 10.1 us: back(): pl.pallas_call(functools.partial(back_kernel, rels), out_shape=[jax.Shape...]
    dot_general x3, matrix products: 4.95 us -> 7.61 us  [project(): jnp.einsum('esd,ehd->esh', values, weight, preferred_element_type=F32)]
    ppermute x2 -> x7, waiting for transfers between devices: 6.65 us -> 7.73 us  [to_owner(): return lax.ppermute(value, ('dp', 'expert'), pairs)]
    ppermute x2 -> x7, starting transfers between devices: 6.01 us -> 6.99 us  [to_owner(): return lax.ppermute(value, ('dp', 'expert'), pairs)]
    unnamed x20 -> x14, local copies, waits for them, and re-layouts: 3.19 us -> 3.17 us
  transfers between devices with their start and end apart: 28 -> 27, of which waited for: 15 -> 11; matrix products, arithmetic and copies ran while one was open for 5% -> 7% of each run, Pallas kernels for 9% -> 18%
where the time goes in v3:
time: 111 us
  waiting for transfers between devices  48.6 us (44%)
  starting transfers between devices  27.2 us (25%)
  Pallas kernels  21.1 us (19%)
  matrix products  7.61 us (7%)
  local copies, waits for them, and re-layouts  3.36 us (3%)
  other arithmetic  1.91 us (2%)
    ppermute x20, waiting for transfers between devices, swap(): return lax.ppermute(value, axis, [(i, i ^ bit) for i in range(count)])  40.8 us
    ppermute x20, starting transfers between devices, swap(): return lax.ppermute(value, axis, [(i, i ^ bit) for i in range(count)])  20.3 us
    pallas_call x2, Pallas kernels, back(): pl.pallas_call(functools.partial(back_kernel, rels), out_shape=[jax.Shape...  10.1 us
    pallas_call x2, Pallas kernels, weight_grad(): pl.pallas_call(functools.partial(weight_kernel, which, order), grid=(loca...  8.08 us
    ppermute x7, waiting for transfers between devices, to_owner(): return lax.ppermute(value, ('dp', 'expert'), pairs)  7.73 us
    dot_general x3, matrix products, project(): jnp.einsum('esd,ehd->esh', values, weight, preferred_element_type=F32)  7.61 us
    ppermute x7, starting transfers between devices, to_owner(): return lax.ppermute(value, ('dp', 'expert'), pairs)  6.99 us
    unnamed x14, local copies, waits for them, and re-layouts  3.17 us
  transfers between devices with their start and end apart: 27, of which 11 were waited for; matrix products, arithmetic and copies ran while one was open for 7% of the time, Pallas kernels for 18%

profile of v3, /device:TPU:0, one launch (start us, length us, event | category | flops | bytes accessed | tf_op | source)
XLA Modules:
  0.0 110.7 jit_solution(1010090040561963574)
XLA Ops:
  5.0 2.6 %collective-permute-start.1 = (bf16[272,512]{1,0:T(8,128)(2,1)S(1)}, bf16[272,512]{1,0:T(8,128)(2,1)S(1)}, u32[]{:S(2)}, u32[]{:S(2)}) collective-permute-start(bf16[272,512]{1,0:T(8,128)(2,1)S(1)} %get-tuple-element.26), channel_id=1, source_target_pairs={{0,16},{8,24},{16,0},{24,8},{1,17},{9,25},{17,1},{25,9},{2,18},{10... | collective-permute-start | bytes 835592 | tf_op jit(solution)/shard_map/ppermute | solution.py:19
  7.7 1.8 %collective-permute-start.3 = (bf16[2,272,512]{2,1,0:T(8,128)(2,1)S(1)}, bf16[2,272,512]{2,1,0:T(8,128)(2,1)S(1)}, u32[]{:S(2)}, u32[]{:S(2)}) collective-permute-start(bf16[2,272,512]{2,1,0:T(8,128)(2,1)S(1)} %pad_maximum_fusion), channel_id=1, source_target_pairs={{0,4},{4,0},{1,5},{5,1},{2,6},{6,2},{3,7},{7,3},{8,12},{12,8},{9,1... | collective-permute-start | bytes 1671176 | tf_op jit(solution)/shard_map/ppermute | solution.py:19
  9.5 5.6 %collective-permute-done.1.refs_2_ = bf16[272,512]{1,0:T(8,128)(2,1)S(1)} collective-permute-done((bf16[272,512]{1,0:T(8,128)(2,1)S(1)}, bf16[272,512]{1,0:T(8,128)(2,1)S(1)}, u32[]{:S(2)}, u32[]{:S(2)}) %collective-permute-start.1) | collective-permute-done | bytes 278560 | tf_op jit(solution)/shard_map/ppermute | solution.py:19
  15.1 5.4 %collective-permute-done.2.refs_3_ = bf16[272,512]{1,0:T(8,128)(2,1)S(1)} collective-permute-done((bf16[272,512]{1,0:T(8,128)(2,1)S(1)}, bf16[272,512]{1,0:T(8,128)(2,1)S(1)}, u32[]{:S(2)}, u32[]{:S(2)}) %collective-permute-start.2) | collective-permute-done | bytes 278560 | tf_op jit(solution)/shard_map/ppermute | solution.py:19
  20.6 2.0 %collective-permute-done.3.refs_4_ = bf16[2,272,512]{2,1,0:T(8,128)(2,1)S(1)} collective-permute-done((bf16[2,272,512]{2,1,0:T(8,128)(2,1)S(1)}, bf16[2,272,512]{2,1,0:T(8,128)(2,1)S(1)}, u32[]{:S(2)}, u32[]{:S(2)}) %collective-permute-start.3) | collective-permute-done | bytes 557088 | tf_op jit(solution)/shard_map/ppermute | solution.py:19
  22.6 1.7 %collective-permute-start.4 = (bf16[2,144,512]{2,1,0:T(8,128)(2,1)S(1)}, bf16[2,144,512]{2,1,0:T(8,128)(2,1)S(1)}, u32[]{:S(2)}, u32[]{:S(2)}) collective-permute-start(bf16[2,144,512]{2,1,0:T(8,128)(2,1)S(1)} %pad_maximum_fusion.3), channel_id=1, source_target_pairs={{0,4},{4,0},{1,5},{5,1},{2,6},{6,2},{3,7},{7,3},{8,12},{12,8},{9,1... | collective-permute-start | bytes 884744 | tf_op jit(solution)/shard_map/ppermute | solution.py:19
  24.8 7.8 %collective-permute-done.4.refs_5_ = bf16[2,144,512]{2,1,0:T(8,128)(2,1)S(1)} collective-permute-done((bf16[2,144,512]{2,1,0:T(8,128)(2,1)S(1)}, bf16[2,144,512]{2,1,0:T(8,128)(2,1)S(1)}, u32[]{:S(2)}, u32[]{:S(2)}) %collective-permute-start.4) | collective-permute-done | bytes 294944 | tf_op jit(solution)/shard_map/ppermute | solution.py:19
  33.5 4.3 %convolution_convert_fusion.1 = bf16[16,64,352]{2,1,0:T(8,128)(2,1)S(1)} fusion(bf16[16,64,512]{2,1,0:T(8,128)(2,1)S(1)} %get-tuple-element.31.placed, bf16[16,512,352]{1,2,0:T(8,128)(2,1)} %param.10), kind=kOutput, calls=%fused_computation.1 | convolution fusion | flops 369459200 | bytes 7536640 | tf_op jit(solution)/shard_map/esd,ehd->esh/dot_general | solution.py:255
  38.5 1.7 %convolution_convert_fusion.2 = bf16[16,64,352]{2,1,0:T(8,128)(2,1)S(1)} fusion(bf16[16,64,512]{2,1,0:T(8,128)(2,1)S(1)} %get-tuple-element.31.placed, bf16[16,512,352]{1,2,0:T(8,128)(2,1)S(1)} %bitcast.51), kind=kOutput, calls=%fused_computation.2 | convolution fusion | flops 369459200 | bytes 7536640 | tf_op jit(solution)/shard_map/esd,ehd->esh/dot_general | solution.py:255
  41.8 1.8 %collective-permute-start.12 = (bf16[2,16,16,352]{3,2,1,0:T(8,128)(2,1)S(1)}, bf16[2,16,16,352]{3,2,1,0:T(8,128)(2,1)S(1)}, u32[]{:S(2)}, u32[]{:S(2)}) collective-permute-start(bf16[2,16,16,352]{3,2,1,0:T(8,128)(2,1)S(1)} %pad_maximum_fusion.1.refs_7_), channel_id=1, source_target_pairs={{0,16},{8,24},{16,0},{24,8},{1,17},{9,25},{17,1},{25,9},{2,18},{10... | collective-permute-start | bytes 1081352 | tf_op jit(solution)/shard_map/ppermute | solution.py:19
  49.0 8.3 %collective-permute-done.10 = bf16[16,16,352]{2,1,0:T(8,128)(2,1)S(1)} collective-permute-done((bf16[16,16,352]{2,1,0:T(8,128)(2,1)S(1)}, bf16[16,16,352]{2,1,0:T(8,128)(2,1)S(1)}, u32[]{:S(2)}, u32[]{:S(2)}) %collective-permute-start.10) | collective-permute-done | bytes 180256 | tf_op jit(solution)/shard_map/ppermute | solution.py:19
  57.4 4.2 %collective-permute-done.9 = bf16[16,16,352]{2,1,0:T(8,128)(2,1)S(1)} collective-permute-done((bf16[16,16,352]{2,1,0:T(8,128)(2,1)S(1)}, bf16[16,16,352]{2,1,0:T(8,128)(2,1)S(1)}, u32[]{:S(2)}, u32[]{:S(2)}) %collective-permute-start.9) | collective-permute-done | bytes 180256 | tf_op jit(solution)/shard_map/ppermute | solution.py:19
  62.1 1.8 %collective-permute-start.14 = (bf16[2,16,16,352]{3,2,1,0:T(8,128)(2,1)S(1)}, bf16[2,16,16,352]{3,2,1,0:T(8,128)(2,1)S(1)}, u32[]{:S(2)}, u32[]{:S(2)}) collective-permute-start(bf16[2,16,16,352]{3,2,1,0:T(8,128)(2,1)S(1)} %pad_maximum_fusion.2.h0), channel_id=1, source_target_pairs={{0,16},{8,24},{16,0},{24,8},{1,17},{9,25},{17,1},{25,9},{2,18},{10... | collective-permute-start | bytes 1081352 | tf_op jit(solution)/shard_map/ppermute | solution.py:19
  63.9 5.0 %shard_map.88 = (bf16[128,512]{1,0:T(8,128)(2,1)S(1)}, bf16[128,512]{1,0:T(8,128)(2,1)S(1)}, bf16[128,512]{1,0:T(8,128)(2,1)S(1)}, bf16[128,512]{1,0:T(8,128)(2,1)S(1)}) custom-call(s32[4,8,256]{2,1,0:T(8,128)S(1)} %get-tuple-element.30.refs_6_.lines, bf16[2,16,16,352]{3,2,1,0:T(8,128)(2,1)S(1)} %pad_maximum_fusion.2.h0, ...), custom_call_target="tpu_custom_call" | custom-call | flops 1476395008 | bytes 11534336 | tf_op jit(solution)/shard_map/pallas_call | solution.py:177
  68.9 4.7 %collective-permute-done.14.h0.h2 = bf16[2,16,16,352]{3,2,1,0:T(8,128)(2,1)S(1)} collective-permute-done((bf16[2,16,16,352]{3,2,1,0:T(8,128)(2,1)S(1)}, bf16[2,16,16,352]{3,2,1,0:T(8,128)(2,1)S(1)}, u32[]{:S(2)}, u32[]{:S(2)}) %collective-permute-start.14) | collective-permute-done | bytes 360480 | tf_op jit(solution)/shard_map/ppermute | solution.py:19
  75.9 5.0 %shard_map.89 = (bf16[128,512]{1,0:T(8,128)(2,1)S(1)}, bf16[128,512]{1,0:T(8,128)(2,1)S(1)}, bf16[128,512]{1,0:T(8,128)(2,1)S(1)}, bf16[128,512]{1,0:T(8,128)(2,1)S(1)}) custom-call(s32[4,8,256]{2,1,0:T(8,128)S(1)} %get-tuple-element.30.refs_6_.lines, bf16[2,16,16,352]{3,2,1,0:T(8,128)(2,1)S(1)} %collective-permute-done.14.h0.h2, ...), custom_call_target="tpu_custom_call" | custom-call | flops 1476395008 | bytes 11534336 | tf_op jit(solution)/shard_map/pallas_call | solution.py:177
  85.7 1.8 %collective-permute-start.25 = (bf16[128,512]{1,0:T(8,128)(2,1)S(1)}, bf16[128,512]{1,0:T(8,128)(2,1)S(1)}, u32[]{:S(2)}, u32[]{:S(2)}) collective-permute-start(bf16[128,512]{1,0:T(8,128)(2,1)S(1)} %broadcast_select_fusion), channel_id=1, source_target_pairs={{0,1},{1,0},{2,3},{3,2},{4,5},{5,4},{6,7},{7,6},{8,9},{9,8},{10,11... | collective-permute-start | bytes 393224 | tf_op jit(solution)/shard_map/ppermute | solution.py:19
  87.5 4.6 %collective-permute-done.17 = bf16[128,512]{1,0:T(8,128)(2,1)S(1)} collective-permute-done((bf16[128,512]{1,0:T(8,128)(2,1)S(1)}, bf16[128,512]{1,0:T(8,128)(2,1)S(1)}, u32[]{:S(2)}, u32[]{:S(2)}) %collective-permute-start.17) | collective-permute-done | bytes 131104 | tf_op jit(solution)/shard_map/ppermute | solution.py:287
  92.1 3.1 %collective-permute-done.19 = bf16[128,512]{1,0:T(8,128)(2,1)S(1)} collective-permute-done((bf16[128,512]{1,0:T(8,128)(2,1)S(1)}, bf16[128,512]{1,0:T(8,128)(2,1)S(1)}, u32[]{:S(2)}, u32[]{:S(2)}) %collective-permute-start.19) | collective-permute-done | bytes 131104 | tf_op jit(solution)/shard_map/ppermute | solution.py:287
  95.3 1.8 %collective-permute-start.21 = (bf16[128,512]{1,0:T(8,128)(2,1)S(1)}, bf16[128,512]{1,0:T(8,128)(2,1)S(1)}, u32[]{:S(2)}, u32[]{:S(2)}) collective-permute-start(bf16[128,512]{1,0:T(8,128)(2,1)S(1)} %broadcast_select_fusion.2), channel_id=1, source_target_pairs={{0,1},{1,0},{2,3},{3,2},{4,5},{5,4},{6,7},{7,6},{8,9},{9,8},{10,11... | collective-permute-start | bytes 393224 | tf_op jit(solution)/shard_map/ppermute | solution.py:19
  97.0 4.0 %shard_map.91 = bf16[16,352,512]{2,1,0:T(8,128)(2,1)} custom-call(bf16[16,64,512]{2,1,0:T(8,128)(2,1)S(1)} %get-tuple-element.31.placed, bf16[2,16,16,352]{3,2,1,0:T(8,128)(2,1)S(1)} %pad_maximum_fusion.2.h0, bf16[2,16,16,352]{3,2,1,0:T(8,128)(2,1)S(1)} %collective-permute-done.15.h1, bf16[2,16,16,352]{3,2,1,0:T(8,128)(2,1)S(1)} %collective-permute-done.14.h0.h2, ...), custom_call_target="tpu_custom_call" | custom-call | flops 1476395008 | bytes 5767168 | tf_op jit(solution)/shard_map/pallas_call | solution.py:208
  101.3 2.7 %collective-permute-start.26 = (bf16[128,512]{1,0:T(8,128)(2,1)S(1)}, bf16[128,512]{1,0:T(8,128)(2,1)S(1)}, u32[]{:S(2)}, u32[]{:S(2)}) collective-permute-start(bf16[128,512]{1,0:T(8,128)(2,1)S(1)} %get-tuple-element.45), channel_id=1, source_target_pairs={{0,2},{1,3},{2,0},{3,1},{4,6},{5,7},{6,4},{7,5},{8,10},{9,11},{10,... | collective-permute-start | bytes 393224 | tf_op jit(solution)/shard_map/ppermute | solution.py:19
  103.9 4.0 %shard_map.90 = bf16[16,352,512]{2,1,0:T(8,128)(2,1)} custom-call(bf16[16,64,512]{2,1,0:T(8,128)(2,1)S(1)} %get-tuple-element.31.placed, bf16[2,16,16,352]{3,2,1,0:T(8,128)(2,1)S(1)} %pad_maximum_fusion.2.h0, bf16[2,16,16,352]{3,2,1,0:T(8,128)(2,1)S(1)} %collective-permute-done.15.h1, bf16[2,16,16,352]{3,2,1,0:T(8,128)(2,1)S(1)} %collective-permute-done.14.h0.h2, ...), custom_call_target="tpu_custom_call" | custom-call | flops 1476395008 | bytes 5767168 | tf_op jit(solution)/shard_map/pallas_call | solution.py:208
  108.0 2.0 %collective-permute-done.26 = bf16[128,512]{1,0:T(8,128)(2,1)S(1)} collective-permute-done((bf16[128,512]{1,0:T(8,128)(2,1)S(1)}, bf16[128,512]{1,0:T(8,128)(2,1)S(1)}, u32[]{:S(2)}, u32[]{:S(2)}) %collective-permute-start.26) | collective-permute-done | bytes 131104 | tf_op jit(solution)/shard_map/ppermute | solution.py:19
  (76 shorter events, 22.1 us)
Async XLA Ops:
  4.5 3.2 %collective-permute-start = (bf16[272,512]{1,0:T(8,128)(2,1)S(1)}, bf16[272,512]{1,0:T(8,128)(2,1)S(1)}, u32[]{:S(2)}, u32[]{:S(2)}) collective-permute-start(bf16[272,512]{1,0:T(8,128)(2,1)S(1)} %get-tuple-element.25), channel_id=1, source_target_pairs={{0,8},{8,0},{16,24},{24,16},{1,9},{9,1},{17,25},{25,17},{2,10},{10... | collective-permute-start | bytes 835592 | tf_op jit(solution)/shard_map/ppermute | solution.py:19
  5.0 10.1 %collective-permute-start.1 = (bf16[272,512]{1,0:T(8,128)(2,1)S(1)}, bf16[272,512]{1,0:T(8,128)(2,1)S(1)}, u32[]{:S(2)}, u32[]{:S(2)}) collective-permute-start(bf16[272,512]{1,0:T(8,128)(2,1)S(1)} %get-tuple-element.26), channel_id=1, source_target_pairs={{0,16},{8,24},{16,0},{24,8},{1,17},{9,25},{17,1},{25,9},{2,18},{10... | collective-permute-start | bytes 835592 | tf_op jit(solution)/shard_map/ppermute | solution.py:19
  7.6 13.0 %collective-permute-start.2 = (bf16[272,512]{1,0:T(8,128)(2,1)S(1)}, bf16[272,512]{1,0:T(8,128)(2,1)S(1)}, u32[]{:S(2)}, u32[]{:S(2)}) collective-permute-start(bf16[272,512]{1,0:T(8,128)(2,1)S(1)} %get-tuple-element.27), channel_id=1, source_target_pairs={{0,24},{8,16},{16,8},{24,0},{1,25},{9,17},{17,9},{25,1},{2,26},{10... | collective-permute-start | bytes 835592 | tf_op jit(solution)/shard_map/ppermute | solution.py:19
  7.7 14.9 %collective-permute-start.3 = (bf16[2,272,512]{2,1,0:T(8,128)(2,1)S(1)}, bf16[2,272,512]{2,1,0:T(8,128)(2,1)S(1)}, u32[]{:S(2)}, u32[]{:S(2)}) collective-permute-start(bf16[2,272,512]{2,1,0:T(8,128)(2,1)S(1)} %pad_maximum_fusion), channel_id=1, source_target_pairs={{0,4},{4,0},{1,5},{5,1},{2,6},{6,2},{3,7},{7,3},{8,12},{12,8},{9,1... | collective-permute-start | bytes 1671176 | tf_op jit(solution)/shard_map/ppermute | solution.py:19
  22.6 9.9 %collective-permute-start.4 = (bf16[2,144,512]{2,1,0:T(8,128)(2,1)S(1)}, bf16[2,144,512]{2,1,0:T(8,128)(2,1)S(1)}, u32[]{:S(2)}, u32[]{:S(2)}) collective-permute-start(bf16[2,144,512]{2,1,0:T(8,128)(2,1)S(1)} %pad_maximum_fusion.3), channel_id=1, source_target_pairs={{0,4},{4,0},{1,5},{5,1},{2,6},{6,2},{3,7},{7,3},{8,12},{12,8},{9,1... | collective-permute-start | bytes 884744 | tf_op jit(solution)/shard_map/ppermute | solution.py:19
  24.4 19.3 %collective-permute-start.5 = (bf16[2,128,512]{2,1,0:T(8,128)(2,1)S(1)}, bf16[2,128,512]{2,1,0:T(8,128)(2,1)S(1)}, u32[]{:S(2)}, u32[]{:S(2)}) collective-permute-start(bf16[2,128,512]{2,1,0:T(8,128)(2,1)S(1)} %pad_maximum_fusion.4.refs_6_), channel_id=1, source_target_pairs={{0,4},{4,0},{1,5},{5,1},{2,6},{6,2},{3,7},{7,3},{8,12},{12,8},{9,1... | collective-permute-start | bytes 786440 | tf_op jit(solution)/shard_map/ppermute | solution.py:19
  37.9 9.6 %collective-permute-start.11 = (bf16[16,16,352]{2,1,0:T(8,128)(2,1)S(1)}, bf16[16,16,352]{2,1,0:T(8,128)(2,1)S(1)}, u32[]{:S(2)}, u32[]{:S(2)}) collective-permute-start(bf16[16,16,352]{2,1,0:T(8,128)(2,1)S(1)} %get-tuple-element.50), channel_id=1, source_target_pairs={{0,8},{8,0},{16,24},{24,16},{1,9},{9,1},{17,25},{25,17},{2,10},{10... | collective-permute-start | bytes 540680 | tf_op jit(solution)/shard_map/ppermute | solution.py:19
  38.0 2.8 %collective-permute-start.7 = (bf16[16,16,352]{2,1,0:T(8,128)(2,1)S(1)}, bf16[16,16,352]{2,1,0:T(8,128)(2,1)S(1)}, u32[]{:S(2)}, u32[]{:S(2)}) collective-permute-start(bf16[16,16,352]{2,1,0:T(8,128)(2,1)S(1)} %get-tuple-element.51), channel_id=1, source_target_pairs={{0,8},{8,0},{16,24},{24,16},{1,9},{9,1},{17,25},{25,17},{2,10},{10... | collective-permute-start | bytes 540680 | tf_op jit(solution)/shard_map/ppermute | solution.py:19
  40.3 8.7 %collective-permute-start.13 = (bf16[16,16,352]{2,1,0:T(8,128)(2,1)S(1)}, bf16[16,16,352]{2,1,0:T(8,128)(2,1)S(1)}, u32[]{:S(2)}, u32[]{:S(2)}) collective-permute-start(bf16[16,16,352]{2,1,0:T(8,128)(2,1)S(1)} %get-tuple-element.56), channel_id=1, source_target_pairs={{0,8},{8,0},{16,24},{24,16},{1,9},{9,1},{17,25},{25,17},{2,10},{10... | collective-permute-start | bytes 540680 | tf_op jit(solution)/shard_map/ppermute | solution.py:19
  41.8 19.7 %collective-permute-start.12 = (bf16[2,16,16,352]{3,2,1,0:T(8,128)(2,1)S(1)}, bf16[2,16,16,352]{3,2,1,0:T(8,128)(2,1)S(1)}, u32[]{:S(2)}, u32[]{:S(2)}) collective-permute-start(bf16[2,16,16,352]{3,2,1,0:T(8,128)(2,1)S(1)} %pad_maximum_fusion.1.refs_7_), channel_id=1, source_target_pairs={{0,16},{8,24},{16,0},{24,8},{1,17},{9,25},{17,1},{25,9},{2,18},{10... | collective-permute-start | bytes 1081352 | tf_op jit(solution)/shard_map/ppermute | solution.py:19
  46.9 10.5 %collective-permute-start.10 = (bf16[16,16,352]{2,1,0:T(8,128)(2,1)S(1)}, bf16[16,16,352]{2,1,0:T(8,128)(2,1)S(1)}, u32[]{:S(2)}, u32[]{:S(2)}) collective-permute-start(bf16[16,16,352]{2,1,0:T(8,128)(2,1)S(1)} %get-tuple-element.53), channel_id=1, source_target_pairs={{0,24},{8,16},{16,8},{24,0},{1,25},{9,17},{17,9},{25,1},{2,26},{10... | collective-permute-start | bytes 540680 | tf_op jit(solution)/shard_map/ppermute | solution.py:19
  47.5 14.0 %collective-permute-start.9 = (bf16[16,16,352]{2,1,0:T(8,128)(2,1)S(1)}, bf16[16,16,352]{2,1,0:T(8,128)(2,1)S(1)}, u32[]{:S(2)}, u32[]{:S(2)}) collective-permute-start(bf16[16,16,352]{2,1,0:T(8,128)(2,1)S(1)} %get-tuple-element.54), channel_id=1, source_target_pairs={{0,16},{8,24},{16,0},{24,8},{1,17},{9,25},{17,1},{25,9},{2,18},{10... | collective-permute-start | bytes 540680 | tf_op jit(solution)/shard_map/ppermute | solution.py:19
  62.1 11.5 %collective-permute-start.14 = (bf16[2,16,16,352]{3,2,1,0:T(8,128)(2,1)S(1)}, bf16[2,16,16,352]{3,2,1,0:T(8,128)(2,1)S(1)}, u32[]{:S(2)}, u32[]{:S(2)}) collective-permute-start(bf16[2,16,16,352]{3,2,1,0:T(8,128)(2,1)S(1)} %pad_maximum_fusion.2.h0), channel_id=1, source_target_pairs={{0,16},{8,24},{16,0},{24,8},{1,17},{9,25},{17,1},{25,9},{2,18},{10... | collective-permute-start | bytes 1081352 | tf_op jit(solution)/shard_map/ppermute | solution.py:19
  73.6 2.3 %collective-permute-start.16 = (bf16[2,16,16,352]{3,2,1,0:T(8,128)(2,1)S(1)}, bf16[2,16,16,352]{3,2,1,0:T(8,128)(2,1)S(1)}, u32[]{:S(2)}, u32[]{:S(2)}) collective-permute-start(bf16[2,16,16,352]{3,2,1,0:T(8,128)(2,1)S(1)} %collective-permute-done.14.h0.h2), channel_id=1, source_target_pairs={{0,8},{8,0},{16,24},{24,16},{1,9},{9,1},{17,25},{25,17},{2,10},{10... | collective-permute-start | bytes 1081352 | tf_op jit(solution)/shard_map/ppermute | solution.py:19
  73.6 10.2 %collective-permute-start.22 = (bf16[128,512]{1,0:T(8,128)(2,1)S(1)}, bf16[128,512]{1,0:T(8,128)(2,1)S(1)}, u32[]{:S(2)}, u32[]{:S(2)}) collective-permute-start(bf16[128,512]{1,0:T(8,128)(2,1)S(1)} %get-tuple-element.41), channel_id=1, source_target_pairs={{0,8},{4,12},{8,0},{12,4},{16,24},{20,28},{24,16},{28,20},{1,9},{5... | collective-permute-start | bytes 393224 | tf_op jit(solution)/shard_map/ppermute | solution.py:287
  74.1 11.2 %collective-permute-start.23 = (bf16[128,512]{1,0:T(8,128)(2,1)S(1)}, bf16[128,512]{1,0:T(8,128)(2,1)S(1)}, u32[]{:S(2)}, u32[]{:S(2)}) collective-permute-start(bf16[128,512]{1,0:T(8,128)(2,1)S(1)} %get-tuple-element.42), channel_id=1, source_target_pairs={{0,12},{4,8},{8,4},{12,0},{16,28},{20,24},{24,20},{28,16},{1,13},{... | collective-permute-start | bytes 393224 | tf_op jit(solution)/shard_map/ppermute | solution.py:287
  75.4 10.2 %collective-permute-start.24 = (bf16[128,512]{1,0:T(8,128)(2,1)S(1)}, bf16[128,512]{1,0:T(8,128)(2,1)S(1)}, u32[]{:S(2)}, u32[]{:S(2)}) collective-permute-start(bf16[128,512]{1,0:T(8,128)(2,1)S(1)} %get-tuple-element.44), channel_id=1, source_target_pairs={{0,4},{4,0},{8,12},{12,8},{16,20},{20,16},{24,28},{28,24},{1,5},{5... | collective-permute-start | bytes 393224 | tf_op jit(solution)/shard_map/ppermute | solution.py:287
  80.9 11.2 %collective-permute-start.17 = (bf16[128,512]{1,0:T(8,128)(2,1)S(1)}, bf16[128,512]{1,0:T(8,128)(2,1)S(1)}, u32[]{:S(2)}, u32[]{:S(2)}) collective-permute-start(bf16[128,512]{1,0:T(8,128)(2,1)S(1)} %get-tuple-element.37), channel_id=1, source_target_pairs={{0,24},{4,28},{8,16},{12,20},{16,8},{20,12},{24,0},{28,4},{1,25},{... | collective-permute-start | bytes 393224 | tf_op jit(solution)/shard_map/ppermute | solution.py:287
  82.5 9.6 %collective-permute-start.18 = (bf16[128,512]{1,0:T(8,128)(2,1)S(1)}, bf16[128,512]{1,0:T(8,128)(2,1)S(1)}, u32[]{:S(2)}, u32[]{:S(2)}) collective-permute-start(bf16[128,512]{1,0:T(8,128)(2,1)S(1)} %get-tuple-element.38), channel_id=1, source_target_pairs={{0,28},{4,24},{8,20},{12,16},{16,12},{20,8},{24,4},{28,0},{1,29},{... | collective-permute-start | bytes 393224 | tf_op jit(solution)/shard_map/ppermute | solution.py:287
  83.8 11.4 %collective-permute-start.19 = (bf16[128,512]{1,0:T(8,128)(2,1)S(1)}, bf16[128,512]{1,0:T(8,128)(2,1)S(1)}, u32[]{:S(2)}, u32[]{:S(2)}) collective-permute-start(bf16[128,512]{1,0:T(8,128)(2,1)S(1)} %get-tuple-element.39), channel_id=1, source_target_pairs={{0,16},{4,20},{8,24},{12,28},{16,0},{20,4},{24,8},{28,12},{1,17},{... | collective-permute-start | bytes 393224 | tf_op jit(solution)/shard_map/ppermute | solution.py:287
  85.3 9.9 %collective-permute-start.20 = (bf16[128,512]{1,0:T(8,128)(2,1)S(1)}, bf16[128,512]{1,0:T(8,128)(2,1)S(1)}, u32[]{:S(2)}, u32[]{:S(2)}) collective-permute-start(bf16[128,512]{1,0:T(8,128)(2,1)S(1)} %get-tuple-element.40), channel_id=1, source_target_pairs={{0,20},{4,16},{8,28},{12,24},{16,4},{20,0},{24,12},{28,8},{1,21},{... | collective-permute-start | bytes 393224 | tf_op jit(solution)/shard_map/ppermute | solution.py:287
  85.7 15.3 %collective-permute-start.25 = (bf16[128,512]{1,0:T(8,128)(2,1)S(1)}, bf16[128,512]{1,0:T(8,128)(2,1)S(1)}, u32[]{:S(2)}, u32[]{:S(2)}) collective-permute-start(bf16[128,512]{1,0:T(8,128)(2,1)S(1)} %broadcast_select_fusion), channel_id=1, source_target_pairs={{0,1},{1,0},{2,3},{3,2},{4,5},{5,4},{6,7},{7,6},{8,9},{9,8},{10,11... | collective-permute-start | bytes 393224 | tf_op jit(solution)/shard_map/ppermute | solution.py:19
  95.3 5.8 %collective-permute-start.21 = (bf16[128,512]{1,0:T(8,128)(2,1)S(1)}, bf16[128,512]{1,0:T(8,128)(2,1)S(1)}, u32[]{:S(2)}, u32[]{:S(2)}) collective-permute-start(bf16[128,512]{1,0:T(8,128)(2,1)S(1)} %broadcast_select_fusion.2), channel_id=1, source_target_pairs={{0,1},{1,0},{2,3},{3,2},{4,5},{5,4},{6,7},{7,6},{8,9},{9,8},{10,11... | collective-permute-start | bytes 393224 | tf_op jit(solution)/shard_map/ppermute | solution.py:19
  101.3 8.6 %collective-permute-start.26 = (bf16[128,512]{1,0:T(8,128)(2,1)S(1)}, bf16[128,512]{1,0:T(8,128)(2,1)S(1)}, u32[]{:S(2)}, u32[]{:S(2)}) collective-permute-start(bf16[128,512]{1,0:T(8,128)(2,1)S(1)} %get-tuple-element.45), channel_id=1, source_target_pairs={{0,2},{1,3},{2,0},{3,1},{4,6},{5,7},{6,4},{7,5},{8,10},{9,11},{10,... | collective-permute-start | bytes 393224 | tf_op jit(solution)/shard_map/ppermute | solution.py:19
  (10 other events, 41.8 us)

commit v4 on v3

--- a/solution.py
+++ b/solution.py
@@ -11,7 +11,8 @@
 META = 16
 F32 = jnp.float32
 BF16 = jnp.bfloat16
-VMEM_LIMIT = 48 * 1024 * 1024
+VMEM_LIMIT = 24 * 1024 * 1024
+SPLIT_VMEM_LIMIT = 63 * 1024 * 1024
 PLACE_COST = 1 << 34
 
 
@@ -34,10 +35,10 @@
     copies = []
     for rel in range(n_dp):
         start = pl.multiple_of((k ^ rel) * width, 128)
-        for which, (source, first) in enumerate(((tokens, 0), (cotangent, rows + META))):
+        for which, source in enumerate((tokens, cotangent)):
             copy = pltpu.make_async_copy(
                 source.at[:, pl.ds(start, width)],
-                outs[rel].at[pl.ds(first, rows), :],
+                outs[which * n_dp + rel].at[pl.ds(0, rows), :],
                 sems.at[which * n_dp + rel],
             )
             copy.start()
@@ -62,20 +63,20 @@
 
 def split(where, ids, tokens, cotangent, width, n_dp):
     rows = tokens.shape[0]
-    pack = (2 * rows + META, width)
+    shapes = [(rows + META, width)] * n_dp + [(rows, width)] * n_dp
     anywhere = pl.BlockSpec(memory_space=pl.ANY)
     return pl.pallas_call(
         functools.partial(split_kernel, width, n_dp),
-        out_shape=[jax.ShapeDtypeStruct(pack, BF16)] * n_dp,
+        out_shape=[jax.ShapeDtypeStruct(s, BF16) for s in shapes],
         in_specs=[
             pl.BlockSpec(memory_space=pltpu.SMEM),
             pl.BlockSpec(memory_space=pltpu.VMEM),
             anywhere,
             anywhere,
         ],
-        out_specs=[anywhere] * n_dp,
+        out_specs=[anywhere] * (2 * n_dp),
         scratch_shapes=[pltpu.VMEM((META, width), BF16), pltpu.SemaphoreType.DMA((3 * n_dp,))],
-        compiler_params=params(),
+        compiler_params=pltpu.CompilerParams(vmem_limit_bytes=SPLIT_VMEM_LIMIT),
     )(where, ids, tokens, cotangent)
 
 
@@ -84,9 +85,11 @@
     return (every == row).astype(F32).astype(BF16)
 
 
-def place_kernel(first, rows, where, mine, near, late, *refs):
+def place_kernel(first, rows, where, mine, others, *refs):
     n_dp = len(mine)
-    other = [near.at[0], near.at[1], late.at[0], late.at[1]]
+    other = []
+    for group in others:
+        other += [group] if len(group.shape) == 2 else [group.at[i] for i in range(group.shape[0])]
     if first:
         placed, lines = refs[-2:]
     else:
@@ -105,23 +108,24 @@
             pair = [b[0:rows] for b in pair]
         else:
             row = lines[rel][0:1]
-            pair = [b[b.shape[0] - rows :, :] for b in (mine[rel], other[rel])]
+            pair = [b[...] for b in (mine[rel], other[rel])]
         placer = placer_of(row, local_experts * slots)
         found = jnp.dot(placer, jnp.concatenate(pair, axis=0), preferred_element_type=F32).astype(BF16)
         placed[:, rel * slots : (rel + 1) * slots, :] = found.reshape(local_experts, slots, width)
 
 
-def place(where, mine, near, late, lines, rows, local_experts, after):
+def place(where, mine, others, lines, rows, local_experts, after):
     first = lines is None
     n_dp, slots = len(mine), 2 * CAP
     width = mine[0].shape[1]
     placed = jax.ShapeDtypeStruct((local_experts, n_dp * slots, width), BF16)
     line = jax.ShapeDtypeStruct((n_dp, 8, 2 * rows), jnp.int32)
     vmem = pl.BlockSpec(memory_space=pltpu.VMEM)
-    operands = [near, late] + ([] if first else [lines])
+    operands = [*others] + ([] if first else [lines])
 
     def kernel(where, *refs):
-        place_kernel(first, rows, where, refs[:n_dp], *refs[n_dp:])
+        split_at = n_dp + len(others)
+        place_kernel(first, rows, where, refs[:n_dp], refs[n_dp:split_at], *refs[split_at:])
 
     return pl.pallas_call(
         kernel,
@@ -237,14 +241,24 @@
     width = gate_weight.shape[1]
     rows = tokens.shape[0]
     where = jnp.stack([k, x]).astype(jnp.int32)
-    packs = split(where, expert_ids.reshape(1, rows), tokens, cotangent, width, n_dp)
-    own = [pack if rel == 0 else swap(pack, "dp", n_dp, rel) for rel, pack in enumerate(packs)]
-    near_packs = swap(jnp.stack(own[:2]), "expert", n_x, 1)
-    leaving_tokens = jnp.stack([o[: rows + META] for o in own[2:]])
-    near_packs, leaving_tokens = lax.optimization_barrier((near_packs, leaving_tokens))
-    late_tokens = swap(leaving_tokens, "expert", n_x, 1)
-    leaving_grads = jnp.stack([o[rows + META :] for o in own[2:]])
-    late_grads = swap(leaving_grads, "expert", n_x, 1)
+    chunks = split(where, expert_ids.reshape(1, rows), tokens, cotangent, width, n_dp)
+    def to_owner(value, rel, flip):
+        if rel == 0 and flip == 0:
+            return value
+        pairs = [
+            (i * n_x + j, (i ^ rel) * n_x + (j ^ flip)) for i in range(n_dp) for j in range(n_x)
+        ]
+        return lax.ppermute(value, ("dp", "expert"), pairs)
+
+    own_tokens = [to_owner(c, rel, 0) for rel, c in enumerate(chunks[:n_dp])]
+    near_tokens = [to_owner(c, rel, 1) for rel, c in enumerate(chunks[:2])]
+    far_tokens, *grads = lax.optimization_barrier((jnp.stack(own_tokens[2:]), *chunks[n_dp:]))
+    near_tokens, far_tokens = lax.optimization_barrier((near_tokens, far_tokens))
+    far_tokens = swap(far_tokens, "expert", n_x, 1)
+    own_grads = [to_owner(c, rel, 0) for rel, c in enumerate(grads)]
+    leaving_grads = jnp.stack(own_grads)
+    far_tokens, leaving_grads = lax.optimization_barrier((far_tokens, leaving_grads))
+    other_grads = swap(leaving_grads, "expert", n_x, 1)
     gate_weight, up_weight, down_weight = (
         jnp.swapaxes(weight, 1, 2) for weight in (gate_weight, up_weight, down_weight)
     )
@@ -259,12 +273,12 @@
         near, far = swap(act[1], "dp", n_dp, 1), swap(act[3], "dp", n_dp, 1)
         return plus(act[0], near), plus(act[2], far).astype(BF16)
 
-    placed, lines = place(where, own, near_packs, late_tokens, None, rows, local_experts, [leaving_grads])
+    placed, lines = place(where, own_tokens, [*near_tokens, far_tokens], None, rows, local_experts, [leaving_grads])
     gate_near, gate_far = near_and_far(project(placed, gate_weight))
     up_near, up_far = near_and_far(project(placed, up_weight))
     far = jnp.stack([gate_far, up_far])
     there = swap(far, "dp", n_dp, 2)
-    placed_grads = place(where, own, near_packs, late_grads, lines, rows, local_experts, [far])
+    placed_grads = place(where, own_grads, [other_grads], lines, rows, local_experts, [far])
     hidden_act = project(placed_grads, down_weight)
     hidden_grad = hidden_act[0].astype(F32)
     for rel in range(1, n_dp):
@@ -277,14 +291,6 @@
     far, near_back = lax.optimization_barrier((far, near_back))
     parts = [part, beside, far, swap(far, "dp", n_dp, 1)]
     far_back = back((2, 3), lines, parts[2:], gate_weight, up_weight, rows)
-
-    def to_owner(value, rel, flip):
-        if rel == 0 and flip == 0:
-            return value
-        pairs = [
-            (i * n_x + j, (i ^ rel) * n_x + (j ^ flip)) for i in range(n_dp) for j in range(n_x)
-        ]
-        return lax.ppermute(value, ("dp", "expert"), pairs)
 
     def blocks(rels, own0, own1, other0, other1):
         terms = [

time: 111 us -> 146 us (1.32)
  Pallas kernels: 21.1 us -> 59.4 us
  waiting for transfers between devices: 48.6 us -> 38.7 us
  local copies, waits for them, and re-layouts: 3.36 us -> 8.31 us
  matrix products: 7.61 us -> 4.97 us
  starting transfers between devices: 27.2 us -> 29.5 us
  other arithmetic: 1.91 us -> 3.54 us
    pallas_call x1, Pallas kernels: 1.01 us -> 33.6 us  [split(): pl.pallas_call(functools.partial(split_kernel, width, n_dp), out_shape=[j...]
    ppermute x20 -> x16, waiting for transfers between devices: 40.8 us -> 17.2 us  [swap(): return lax.ppermute(value, axis, [(i, i ^ bit) for i in range(count)])]
    ppermute x7 -> x15, waiting for transfers between devices: 7.73 us -> 21.5 us  [to_owner(): return lax.ppermute(value, ('dp', 'expert'), pairs)]
    ppermute x7 -> x15, starting transfers between devices: 6.99 us -> 13.8 us  [to_owner(): return lax.ppermute(value, ('dp', 'expert'), pairs)]
    pallas_call x2, Pallas kernels: 10.1 us -> 15.7 us  [back(): pl.pallas_call(functools.partial(back_kernel, rels), out_shape=[jax.Shape...]
    unnamed x14 -> x24, local copies, waits for them, and re-layouts: 3.17 us -> 8.16 us
    ppermute x20 -> x16, starting transfers between devices: 20.3 us -> 15.7 us  [swap(): return lax.ppermute(value, axis, [(i, i ^ bit) for i in range(count)])]
    dot_general x3, matrix products: 7.61 us -> 4.97 us  [project(): jnp.einsum('esd,ehd->esh', values, weight, preferred_element_type=F32)]
  transfers between devices with their start and end apart: 27 -> 31, of which waited for: 11 -> 15; matrix products, arithmetic and copies ran while one was open for 7% -> 5% of each run, Pallas kernels for 18% -> 18%
where the time goes in v4:
time: 146 us; the launch traced here: 145 us
  Pallas kernels  59.4 us (41%)
  waiting for transfers between devices  38.7 us (27%)
  starting transfers between devices  29.5 us (20%)
  local copies, waits for them, and re-layouts  8.31 us (6%)
  matrix products  4.97 us (3%)
  other arithmetic  3.54 us (2%)
    pallas_call x1, Pallas kernels, split(): pl.pallas_call(functools.partial(split_kernel, width, n_dp), out_shape=[j...  33.6 us
    ppermute x15, waiting for transfers between devices, to_owner(): return lax.ppermute(value, ('dp', 'expert'), pairs)  21.5 us
    ppermute x16, waiting for transfers between devices, swap(): return lax.ppermute(value, axis, [(i, i ^ bit) for i in range(count)])  17.2 us
    pallas_call x2, Pallas kernels, back(): pl.pallas_call(functools.partial(back_kernel, rels), out_shape=[jax.Shape...  15.7 us
    ppermute x16, starting transfers between devices, swap(): return lax.ppermute(value, axis, [(i, i ^ bit) for i in range(count)])  15.7 us
    ppermute x15, starting transfers between devices, to_owner(): return lax.ppermute(value, ('dp', 'expert'), pairs)  13.8 us
    unnamed x24, local copies, waits for them, and re-layouts  8.16 us
    pallas_call x2, Pallas kernels, weight_grad(): pl.pallas_call(functools.partial(weight_kernel, which, order), grid=(loca...  8.08 us
  transfers between devices with their start and end apart: 31, of which 15 were waited for; matrix products, arithmetic and copies ran while one was open for 5% of the time, Pallas kernels for 18%

profile of v4, /device:TPU:0, one launch (start us, length us, event | category | flops | bytes accessed | tf_op | source)
XLA Modules:
  0.0 145.3 jit_solution(2699669054676537443)
XLA Ops:
  1.3 33.6 %shard_map.85 = (bf16[144,512]{1,0:T(8,128)(2,1)}, bf16[144,512]{1,0:T(8,128)(2,1)}, bf16[144,512]{1,0:T(8,128)(2,1)}, bf16[144,512]{1,0:T(8,128)(2,1)}, bf16[12...) custom-call(s32[2]{0:T(128)} %pad_add_fusion.where, ...), custom_call_target="tpu_custom_call" | custom-call | tf_op jit(solution)/shard_map/pallas_call | solution.py:68
  35.0 3.0 %collective-permute-start.1 = (bf16[144,512]{1,0:T(8,128)(2,1)}, bf16[144,512]{1,0:T(8,128)(2,1)S(1)}, u32[]{:S(2)}, u32[]{:S(2)}) collective-permute-start(bf16[144,512]{1,0:T(8,128)(2,1)} %get-tuple-element.38), channel_id=1, source_target_pairs={{0,16},{4,20},{8,24},{12,28},{16,0},{20,4},{24,8},{28,12},{1,17},{... | collective-permute-start | bytes 442376 | tf_op jit(solution)/shard_map/ppermute | solution.py:251
  39.7 3.1 %collective-permute-done.1.refs_2_ = bf16[144,512]{1,0:T(8,128)(2,1)S(1)} collective-permute-done((bf16[144,512]{1,0:T(8,128)(2,1)}, bf16[144,512]{1,0:T(8,128)(2,1)S(1)}, u32[]{:S(2)}, u32[]{:S(2)}) %collective-permute-start.1) | collective-permute-done | bytes 147488 | tf_op jit(solution)/shard_map/ppermute | solution.py:251
  44.9 2.1 %collective-permute-done.4.refs_5_ = bf16[144,512]{1,0:T(8,128)(2,1)S(1)} collective-permute-done((bf16[144,512]{1,0:T(8,128)(2,1)}, bf16[144,512]{1,0:T(8,128)(2,1)S(1)}, u32[]{:S(2)}, u32[]{:S(2)}) %collective-permute-start.4) | collective-permute-done | bytes 147488 | tf_op jit(solution)/shard_map/ppermute | solution.py:251
  46.9 2.0 %collective-permute-start.5 = (bf16[2,144,512]{2,1,0:T(8,128)(2,1)S(1)}, bf16[2,144,512]{2,1,0:T(8,128)(2,1)S(1)}, u32[]{:S(2)}, u32[]{:S(2)}) collective-permute-start(bf16[2,144,512]{2,1,0:T(8,128)(2,1)S(1)} %pad_maximum_fusion.3), channel_id=1, source_target_pairs={{0,4},{4,0},{1,5},{5,1},{2,6},{6,2},{3,7},{7,3},{8,12},{12,8},{9,1... | collective-permute-start | bytes 884744 | tf_op jit(solution)/shard_map/ppermute | solution.py:20
  51.1 4.4 %collective-permute-done.7.refs_2_ = bf16[128,512]{1,0:T(8,128)(2,1)S(1)} collective-permute-done((bf16[128,512]{1,0:T(8,128)(2,1)}, bf16[128,512]{1,0:T(8,128)(2,1)S(1)}, u32[]{:S(2)}, u32[]{:S(2)}) %collective-permute-start.7) | collective-permute-done | bytes 131104 | tf_op jit(solution)/shard_map/ppermute | solution.py:251
  55.5 2.1 %collective-permute-done.8.refs_3_ = bf16[128,512]{1,0:T(8,128)(2,1)S(1)} collective-permute-done((bf16[128,512]{1,0:T(8,128)(2,1)}, bf16[128,512]{1,0:T(8,128)(2,1)S(1)}, u32[]{:S(2)}, u32[]{:S(2)}) %collective-permute-start.8) | collective-permute-done | bytes 131104 | tf_op jit(solution)/shard_map/ppermute | solution.py:251
  70.4 2.5 %collective-permute-done.9.refs_4_ = bf16[4,128,512]{2,1,0:T(8,128)(2,1)S(1)} collective-permute-done((bf16[4,128,512]{2,1,0:T(8,128)(2,1)S(1)}, bf16[4,128,512]{2,1,0:T(8,128)(2,1)S(1)}, u32[]{:S(2)}, u32[]{:S(2)}) %collective-permute-start.9) | collective-permute-done | bytes 524320 | tf_op jit(solution)/shard_map/ppermute | solution.py:20
  76.1 1.9 %collective-permute-start.14 = (bf16[16,16,352]{2,1,0:T(8,128)(2,1)S(1)}, bf16[16,16,352]{2,1,0:T(8,128)(2,1)S(1)}, u32[]{:S(2)}, u32[]{:S(2)}) collective-permute-start(bf16[16,16,352]{2,1,0:T(8,128)(2,1)S(1)} %get-tuple-element.77), channel_id=1, source_target_pairs={{0,24},{8,16},{16,8},{24,0},{1,25},{9,17},{17,9},{25,1},{2,26},{10... | collective-permute-start | bytes 540680 | tf_op jit(solution)/shard_map/ppermute | solution.py:20
  78.2 2.3 %collective-permute-done.16 = bf16[2,16,16,352]{3,2,1,0:T(8,128)(2,1)S(1)} collective-permute-done((bf16[2,16,16,352]{3,2,1,0:T(8,128)(2,1)S(1)}, bf16[2,16,16,352]{3,2,1,0:T(8,128)(2,1)S(1)}, u32[]{:S(2)}, u32[]{:S(2)}) %collective-permute-start.16) | collective-permute-done | bytes 360480 | tf_op jit(solution)/shard_map/ppermute | solution.py:20
  80.5 3.6 %collective-permute-done.14 = bf16[16,16,352]{2,1,0:T(8,128)(2,1)S(1)} collective-permute-done((bf16[16,16,352]{2,1,0:T(8,128)(2,1)S(1)}, bf16[16,16,352]{2,1,0:T(8,128)(2,1)S(1)}, u32[]{:S(2)}, u32[]{:S(2)}) %collective-permute-start.14) | collective-permute-done | bytes 180256 | tf_op jit(solution)/shard_map/ppermute | solution.py:20
  84.1 4.2 %collective-permute-done.13 = bf16[16,16,352]{2,1,0:T(8,128)(2,1)S(1)} collective-permute-done((bf16[16,16,352]{2,1,0:T(8,128)(2,1)S(1)}, bf16[16,16,352]{2,1,0:T(8,128)(2,1)S(1)}, u32[]{:S(2)}, u32[]{:S(2)}) %collective-permute-start.13) | collective-permute-done | bytes 180256 | tf_op jit(solution)/shard_map/ppermute | solution.py:20
  88.9 1.8 %collective-permute-start.18 = (bf16[2,16,16,352]{3,2,1,0:T(8,128)(2,1)S(1)}, bf16[2,16,16,352]{3,2,1,0:T(8,128)(2,1)S(1)}, u32[]{:S(2)}, u32[]{:S(2)}) collective-permute-start(bf16[2,16,16,352]{3,2,1,0:T(8,128)(2,1)S(1)} %pad_maximum_fusion.2.h0), channel_id=1, source_target_pairs={{0,16},{8,24},{16,0},{24,8},{1,17},{9,25},{17,1},{25,9},{2,18},{10... | collective-permute-start | bytes 1081352 | tf_op jit(solution)/shard_map/ppermute | solution.py:20
  90.7 7.9 %shard_map.88 = (bf16[128,512]{1,0:T(8,128)(2,1)S(1)}, bf16[128,512]{1,0:T(8,128)(2,1)S(1)}, bf16[128,512]{1,0:T(8,128)(2,1)S(1)}, bf16[128,512]{1,0:T(8,128)(2,1)S(1)}) custom-call(s32[4,8,256]{2,1,0:T(8,128)S(1)} %get-tuple-element.54.refs_5_.lines, bf16[2,16,16,352]{3,2,1,0:T(8,128)(2,1)S(1)} %pad_maximum_fusion.2.h0, ...), custom_call_target="tpu_custom_call" | custom-call | flops 1476395008 | bytes 11534336 | tf_op jit(solution)/shard_map/pallas_call | solution.py:181
  98.5 1.9 %collective-permute-done.18.h0.h2 = bf16[2,16,16,352]{3,2,1,0:T(8,128)(2,1)S(1)} collective-permute-done((bf16[2,16,16,352]{3,2,1,0:T(8,128)(2,1)S(1)}, bf16[2,16,16,352]{3,2,1,0:T(8,128)(2,1)S(1)}, u32[]{:S(2)}, u32[]{:S(2)}) %collective-permute-start.18) | collective-permute-done | bytes 360480 | tf_op jit(solution)/shard_map/ppermute | solution.py:20
  102.5 2.6 %copy-done = bf16[16,512,352]{1,2,0:T(8,128)(2,1)S(1)} copy-done((bf16[16,512,352]{1,2,0:T(8,128)(2,1)S(1)}, bf16[16,512,352]{1,2,0:T(8,128)(2,1)}, u32[]{:S(2)}) %copy-start) | copy-done | bytes 5767192
  105.2 2.6 %copy-done.1 = bf16[16,512,352]{1,2,0:T(8,128)(2,1)S(1)} copy-done((bf16[16,512,352]{1,2,0:T(8,128)(2,1)S(1)}, bf16[16,512,352]{1,2,0:T(8,128)(2,1)}, u32[]{:S(2)}) %copy-start.1) | copy-done | bytes 5767192
  107.8 7.9 %shard_map.89 = (bf16[128,512]{1,0:T(8,128)(2,1)S(1)}, bf16[128,512]{1,0:T(8,128)(2,1)S(1)}, bf16[128,512]{1,0:T(8,128)(2,1)S(1)}, bf16[128,512]{1,0:T(8,128)(2,1)S(1)}) custom-call(s32[4,8,256]{2,1,0:T(8,128)S(1)} %get-tuple-element.54.refs_5_.lines, bf16[2,16,16,352]{3,2,1,0:T(8,128)(2,1)S(1)} %collective-permute-done.18.h0.h2, ...), custom_call_target="tpu_custom_call" | custom-call | flops 1476395008 | bytes 11534336 | tf_op jit(solution)/shard_map/pallas_call | solution.py:181
  122.1 4.6 %collective-permute-done.21 = bf16[128,512]{1,0:T(8,128)(2,1)S(1)} collective-permute-done((bf16[128,512]{1,0:T(8,128)(2,1)S(1)}, bf16[128,512]{1,0:T(8,128)(2,1)S(1)}, u32[]{:S(2)}, u32[]{:S(2)}) %collective-permute-start.21) | collective-permute-done | bytes 131104 | tf_op jit(solution)/shard_map/ppermute | solution.py:251
  126.8 3.2 %collective-permute-done.23 = bf16[128,512]{1,0:T(8,128)(2,1)S(1)} collective-permute-done((bf16[128,512]{1,0:T(8,128)(2,1)S(1)}, bf16[128,512]{1,0:T(8,128)(2,1)S(1)}, u32[]{:S(2)}, u32[]{:S(2)}) %collective-permute-start.23) | collective-permute-done | bytes 131104 | tf_op jit(solution)/shard_map/ppermute | solution.py:251
  131.7 4.0 %shard_map.91 = bf16[16,352,512]{2,1,0:T(8,128)(2,1)} custom-call(bf16[16,64,512]{2,1,0:T(8,128)(2,1)S(1)} %get-tuple-element.55.placed, bf16[2,16,16,352]{3,2,1,0:T(8,128)(2,1)S(1)} %pad_maximum_fusion.2.h0, bf16[2,16,16,352]{3,2,1,0:T(8,128)(2,1)S(1)} %collective-permute-done.19.h1, bf16[2,16,16,352]{3,2,1,0:T(8,128)(2,1)S(1)} %collective-permute-done.18.h0.h2, ...), custom_call_target="tpu_custom_call" | custom-call | flops 1476395008 | bytes 5767168 | tf_op jit(solution)/shard_map/pallas_call | solution.py:212
  135.9 2.7 %collective-permute-start.30 = (bf16[128,512]{1,0:T(8,128)(2,1)S(1)}, bf16[128,512]{1,0:T(8,128)(2,1)S(1)}, u32[]{:S(2)}, u32[]{:S(2)}) collective-permute-start(bf16[128,512]{1,0:T(8,128)(2,1)S(1)} %get-tuple-element.69), channel_id=1, source_target_pairs={{0,2},{1,3},{2,0},{3,1},{4,6},{5,7},{6,4},{7,5},{8,10},{9,11},{10,... | collective-permute-start | bytes 393224 | tf_op jit(solution)/shard_map/ppermute | solution.py:20
  138.6 4.0 %shard_map.90 = bf16[16,352,512]{2,1,0:T(8,128)(2,1)} custom-call(bf16[16,64,512]{2,1,0:T(8,128)(2,1)S(1)} %get-tuple-element.55.placed, bf16[2,16,16,352]{3,2,1,0:T(8,128)(2,1)S(1)} %pad_maximum_fusion.2.h0, bf16[2,16,16,352]{3,2,1,0:T(8,128)(2,1)S(1)} %collective-permute-done.19.h1, bf16[2,16,16,352]{3,2,1,0:T(8,128)(2,1)S(1)} %collective-permute-done.18.h0.h2, ...), custom_call_target="tpu_custom_call" | custom-call | flops 1476395008 | bytes 5767168 | tf_op jit(solution)/shard_map/pallas_call | solution.py:212
  142.6 2.0 %collective-permute-done.30 = bf16[128,512]{1,0:T(8,128)(2,1)S(1)} collective-permute-done((bf16[128,512]{1,0:T(8,128)(2,1)S(1)}, bf16[128,512]{1,0:T(8,128)(2,1)S(1)}, u32[]{:S(2)}, u32[]{:S(2)}) %collective-permute-start.30) | collective-permute-done | bytes 131104 | tf_op jit(solution)/shard_map/ppermute | solution.py:20
  (90 shorter events, 34.5 us)
Async XLA Ops:
  35.0 7.9 %collective-permute-start.1 = (bf16[144,512]{1,0:T(8,128)(2,1)}, bf16[144,512]{1,0:T(8,128)(2,1)S(1)}, u32[]{:S(2)}, u32[]{:S(2)}) collective-permute-start(bf16[144,512]{1,0:T(8,128)(2,1)} %get-tuple-element.38), channel_id=1, source_target_pairs={{0,16},{4,20},{8,24},{12,28},{16,0},{20,4},{24,8},{28,12},{1,17},{... | collective-permute-start | bytes 442376 | tf_op jit(solution)/shard_map/ppermute | solution.py:251
  38.0 6.6 %collective-permute-start.2 = (bf16[144,512]{1,0:T(8,128)(2,1)}, bf16[144,512]{1,0:T(8,128)(2,1)S(1)}, u32[]{:S(2)}, u32[]{:S(2)}) collective-permute-start(bf16[144,512]{1,0:T(8,128)(2,1)} %get-tuple-element.39), channel_id=1, source_target_pairs={{0,24},{4,28},{8,16},{12,20},{16,8},{20,12},{24,0},{28,4},{1,25},{... | collective-permute-start | bytes 442376 | tf_op jit(solution)/shard_map/ppermute | solution.py:251
  38.0 6.9 %collective-permute-start.3 = (bf16[144,512]{1,0:T(8,128)(2,1)}, bf16[144,512]{1,0:T(8,128)(2,1)S(1)}, u32[]{:S(2)}, u32[]{:S(2)}) collective-permute-start(bf16[144,512]{1,0:T(8,128)(2,1)} %get-tuple-element.36.refs_0_), channel_id=1, source_target_pairs={{0,4},{4,0},{8,12},{12,8},{16,20},{20,16},{24,28},{28,24},{1,5},{5... | collective-permute-start | bytes 442376 | tf_op jit(solution)/shard_map/ppermute | solution.py:251
  39.5 7.5 %collective-permute-start.4 = (bf16[144,512]{1,0:T(8,128)(2,1)}, bf16[144,512]{1,0:T(8,128)(2,1)S(1)}, u32[]{:S(2)}, u32[]{:S(2)}) collective-permute-start(bf16[144,512]{1,0:T(8,128)(2,1)} %get-tuple-element.37), channel_id=1, source_target_pairs={{0,12},{4,8},{8,4},{12,0},{16,28},{20,24},{24,20},{28,16},{1,13},{... | collective-permute-start | bytes 442376 | tf_op jit(solution)/shard_map/ppermute | solution.py:251
  46.9 11.8 %collective-permute-start.5 = (bf16[2,144,512]{2,1,0:T(8,128)(2,1)S(1)}, bf16[2,144,512]{2,1,0:T(8,128)(2,1)S(1)}, u32[]{:S(2)}, u32[]{:S(2)}) collective-permute-start(bf16[2,144,512]{2,1,0:T(8,128)(2,1)S(1)} %pad_maximum_fusion.3), channel_id=1, source_target_pairs={{0,4},{4,0},{1,5},{5,1},{2,6},{6,2},{3,7},{7,3},{8,12},{12,8},{9,1... | collective-permute-start | bytes 884744 | tf_op jit(solution)/shard_map/ppermute | solution.py:20
  49.0 6.5 %collective-permute-start.7 = (bf16[128,512]{1,0:T(8,128)(2,1)}, bf16[128,512]{1,0:T(8,128)(2,1)S(1)}, u32[]{:S(2)}, u32[]{:S(2)}) collective-permute-start(bf16[128,512]{1,0:T(8,128)(2,1)} %get-tuple-element.50), channel_id=1, source_target_pairs={{0,16},{4,20},{8,24},{12,28},{16,0},{20,4},{24,8},{28,12},{1,17},{... | collective-permute-start | bytes 393224 | tf_op jit(solution)/shard_map/ppermute | solution.py:251
  50.8 6.9 %collective-permute-start.8 = (bf16[128,512]{1,0:T(8,128)(2,1)}, bf16[128,512]{1,0:T(8,128)(2,1)S(1)}, u32[]{:S(2)}, u32[]{:S(2)}) collective-permute-start(bf16[128,512]{1,0:T(8,128)(2,1)} %get-tuple-element.51), channel_id=1, source_target_pairs={{0,24},{4,28},{8,16},{12,20},{16,8},{20,12},{24,0},{28,4},{1,25},{... | collective-permute-start | bytes 393224 | tf_op jit(solution)/shard_map/ppermute | solution.py:251
  50.9 8.6 %collective-permute-start = (bf16[144,512]{1,0:T(8,128)(2,1)}, bf16[144,512]{1,0:T(8,128)(2,1)S(1)}, u32[]{:S(2)}, u32[]{:S(2)}) collective-permute-start(bf16[144,512]{1,0:T(8,128)(2,1)} %get-tuple-element.37), channel_id=1, source_target_pairs={{0,8},{4,12},{8,0},{12,4},{16,24},{20,28},{24,16},{28,20},{1,9},{5... | collective-permute-start | bytes 442376 | tf_op jit(solution)/shard_map/ppermute | solution.py:251
  58.8 14.0 %collective-permute-start.9 = (bf16[4,128,512]{2,1,0:T(8,128)(2,1)S(1)}, bf16[4,128,512]{2,1,0:T(8,128)(2,1)S(1)}, u32[]{:S(2)}, u32[]{:S(2)}) collective-permute-start(bf16[4,128,512]{2,1,0:T(8,128)(2,1)S(1)} %pad_maximum_fusion.refs_7_), channel_id=1, source_target_pairs={{0,4},{4,0},{1,5},{5,1},{2,6},{6,2},{3,7},{7,3},{8,12},{12,8},{9,1... | collective-permute-start | bytes 1572872 | tf_op jit(solution)/shard_map/ppermute | solution.py:20
  64.7 13.3 %collective-permute-start.15 = (bf16[16,16,352]{2,1,0:T(8,128)(2,1)S(1)}, bf16[16,16,352]{2,1,0:T(8,128)(2,1)S(1)}, u32[]{:S(2)}, u32[]{:S(2)}) collective-permute-start(bf16[16,16,352]{2,1,0:T(8,128)(2,1)S(1)} %get-tuple-element.74), channel_id=1, source_target_pairs={{0,8},{8,0},{16,24},{24,16},{1,9},{9,1},{17,25},{25,17},{2,10},{10... | collective-permute-start | bytes 540680 | tf_op jit(solution)/shard_map/ppermute | solution.py:20
  67.2 11.0 %collective-permute-start.17 = (bf16[16,16,352]{2,1,0:T(8,128)(2,1)S(1)}, bf16[16,16,352]{2,1,0:T(8,128)(2,1)S(1)}, u32[]{:S(2)}, u32[]{:S(2)}) collective-permute-start(bf16[16,16,352]{2,1,0:T(8,128)(2,1)S(1)} %get-tuple-element.80), channel_id=1, source_target_pairs={{0,8},{8,0},{16,24},{24,16},{1,9},{9,1},{17,25},{25,17},{2,10},{10... | collective-permute-start | bytes 540680 | tf_op jit(solution)/shard_map/ppermute | solution.py:20
  68.6 11.9 %collective-permute-start.16 = (bf16[2,16,16,352]{3,2,1,0:T(8,128)(2,1)S(1)}, bf16[2,16,16,352]{3,2,1,0:T(8,128)(2,1)S(1)}, u32[]{:S(2)}, u32[]{:S(2)}) collective-permute-start(bf16[2,16,16,352]{3,2,1,0:T(8,128)(2,1)S(1)} %pad_maximum_fusion.1.refs_6_), channel_id=1, source_target_pairs={{0,16},{8,24},{16,0},{24,8},{1,17},{9,25},{17,1},{25,9},{2,18},{10... | collective-permute-start | bytes 1081352 | tf_op jit(solution)/shard_map/ppermute | solution.py:20
  76.1 8.0 %collective-permute-start.14 = (bf16[16,16,352]{2,1,0:T(8,128)(2,1)S(1)}, bf16[16,16,352]{2,1,0:T(8,128)(2,1)S(1)}, u32[]{:S(2)}, u32[]{:S(2)}) collective-permute-start(bf16[16,16,352]{2,1,0:T(8,128)(2,1)S(1)} %get-tuple-element.77), channel_id=1, source_target_pairs={{0,24},{8,16},{16,8},{24,0},{1,25},{9,17},{17,9},{25,1},{2,26},{10... | collective-permute-start | bytes 540680 | tf_op jit(solution)/shard_map/ppermute | solution.py:20
  77.9 10.4 %collective-permute-start.13 = (bf16[16,16,352]{2,1,0:T(8,128)(2,1)S(1)}, bf16[16,16,352]{2,1,0:T(8,128)(2,1)S(1)}, u32[]{:S(2)}, u32[]{:S(2)}) collective-permute-start(bf16[16,16,352]{2,1,0:T(8,128)(2,1)S(1)} %get-tuple-element.78), channel_id=1, source_target_pairs={{0,16},{8,24},{16,0},{24,8},{1,17},{9,25},{17,1},{25,9},{2,18},{10... | collective-permute-start | bytes 540680 | tf_op jit(solution)/shard_map/ppermute | solution.py:20
  88.9 11.5 %collective-permute-start.18 = (bf16[2,16,16,352]{3,2,1,0:T(8,128)(2,1)S(1)}, bf16[2,16,16,352]{3,2,1,0:T(8,128)(2,1)S(1)}, u32[]{:S(2)}, u32[]{:S(2)}) collective-permute-start(bf16[2,16,16,352]{3,2,1,0:T(8,128)(2,1)S(1)} %pad_maximum_fusion.2.h0), channel_id=1, source_target_pairs={{0,16},{8,24},{16,0},{24,8},{1,17},{9,25},{17,1},{25,9},{2,18},{10... | collective-permute-start | bytes 1081352 | tf_op jit(solution)/shard_map/ppermute | solution.py:20
  100.4 17.8 %collective-permute-start.26 = (bf16[128,512]{1,0:T(8,128)(2,1)S(1)}, bf16[128,512]{1,0:T(8,128)(2,1)S(1)}, u32[]{:S(2)}, u32[]{:S(2)}) collective-permute-start(bf16[128,512]{1,0:T(8,128)(2,1)S(1)} %get-tuple-element.65), channel_id=1, source_target_pairs={{0,8},{4,12},{8,0},{12,4},{16,24},{20,28},{24,16},{28,20},{1,9},{5... | collective-permute-start | bytes 393224 | tf_op jit(solution)/shard_map/ppermute | solution.py:251
  100.9 18.9 %collective-permute-start.27 = (bf16[128,512]{1,0:T(8,128)(2,1)S(1)}, bf16[128,512]{1,0:T(8,128)(2,1)S(1)}, u32[]{:S(2)}, u32[]{:S(2)}) collective-permute-start(bf16[128,512]{1,0:T(8,128)(2,1)S(1)} %get-tuple-element.66), channel_id=1, source_target_pairs={{0,12},{4,8},{8,4},{12,0},{16,28},{20,24},{24,20},{28,16},{1,13},{... | collective-permute-start | bytes 393224 | tf_op jit(solution)/shard_map/ppermute | solution.py:251
  101.8 18.6 %collective-permute-start.28 = (bf16[128,512]{1,0:T(8,128)(2,1)S(1)}, bf16[128,512]{1,0:T(8,128)(2,1)S(1)}, u32[]{:S(2)}, u32[]{:S(2)}) collective-permute-start(bf16[128,512]{1,0:T(8,128)(2,1)S(1)} %get-tuple-element.68), channel_id=1, source_target_pairs={{0,4},{4,0},{8,12},{12,8},{16,20},{20,16},{24,28},{28,24},{1,5},{5... | collective-permute-start | bytes 393224 | tf_op jit(solution)/shard_map/ppermute | solution.py:251
  115.7 11.1 %collective-permute-start.21 = (bf16[128,512]{1,0:T(8,128)(2,1)S(1)}, bf16[128,512]{1,0:T(8,128)(2,1)S(1)}, u32[]{:S(2)}, u32[]{:S(2)}) collective-permute-start(bf16[128,512]{1,0:T(8,128)(2,1)S(1)} %get-tuple-element.61), channel_id=1, source_target_pairs={{0,24},{4,28},{8,16},{12,20},{16,8},{20,12},{24,0},{28,4},{1,25},{... | collective-permute-start | bytes 393224 | tf_op jit(solution)/shard_map/ppermute | solution.py:251
  117.3 9.4 %collective-permute-start.22 = (bf16[128,512]{1,0:T(8,128)(2,1)S(1)}, bf16[128,512]{1,0:T(8,128)(2,1)S(1)}, u32[]{:S(2)}, u32[]{:S(2)}) collective-permute-start(bf16[128,512]{1,0:T(8,128)(2,1)S(1)} %get-tuple-element.62), channel_id=1, source_target_pairs={{0,28},{4,24},{8,20},{12,16},{16,12},{20,8},{24,4},{28,0},{1,29},{... | collective-permute-start | bytes 393224 | tf_op jit(solution)/shard_map/ppermute | solution.py:251
  118.2 11.8 %collective-permute-start.23 = (bf16[128,512]{1,0:T(8,128)(2,1)S(1)}, bf16[128,512]{1,0:T(8,128)(2,1)S(1)}, u32[]{:S(2)}, u32[]{:S(2)}) collective-permute-start(bf16[128,512]{1,0:T(8,128)(2,1)S(1)} %get-tuple-element.63), channel_id=1, source_target_pairs={{0,16},{4,20},{8,24},{12,28},{16,0},{20,4},{24,8},{28,12},{1,17},{... | collective-permute-start | bytes 393224 | tf_op jit(solution)/shard_map/ppermute | solution.py:251
  119.8 10.2 %collective-permute-start.24 = (bf16[128,512]{1,0:T(8,128)(2,1)S(1)}, bf16[128,512]{1,0:T(8,128)(2,1)S(1)}, u32[]{:S(2)}, u32[]{:S(2)}) collective-permute-start(bf16[128,512]{1,0:T(8,128)(2,1)S(1)} %get-tuple-element.64), channel_id=1, source_target_pairs={{0,20},{4,16},{8,28},{12,24},{16,4},{20,0},{24,12},{28,8},{1,21},{... | collective-permute-start | bytes 393224 | tf_op jit(solution)/shard_map/ppermute | solution.py:251
  120.5 15.2 %collective-permute-start.29 = (bf16[128,512]{1,0:T(8,128)(2,1)S(1)}, bf16[128,512]{1,0:T(8,128)(2,1)S(1)}, u32[]{:S(2)}, u32[]{:S(2)}) collective-permute-start(bf16[128,512]{1,0:T(8,128)(2,1)S(1)} %broadcast_select_fusion), channel_id=1, source_target_pairs={{0,1},{1,0},{2,3},{3,2},{4,5},{5,4},{6,7},{7,6},{8,9},{9,8},{10,11... | collective-permute-start | bytes 393224 | tf_op jit(solution)/shard_map/ppermute | solution.py:20
  135.9 8.7 %collective-permute-start.30 = (bf16[128,512]{1,0:T(8,128)(2,1)S(1)}, bf16[128,512]{1,0:T(8,128)(2,1)S(1)}, u32[]{:S(2)}, u32[]{:S(2)}) collective-permute-start(bf16[128,512]{1,0:T(8,128)(2,1)S(1)} %get-tuple-element.69), channel_id=1, source_target_pairs={{0,2},{1,3},{2,0},{3,1},{4,6},{5,7},{6,4},{7,5},{8,10},{9,11},{10,... | collective-permute-start | bytes 393224 | tf_op jit(solution)/shard_map/ppermute | solution.py:20
  (19 other events, 76.0 us)

commit v5 on v4

--- a/solution.py
+++ b/solution.py
@@ -11,8 +11,7 @@
 META = 16
 F32 = jnp.float32
 BF16 = jnp.bfloat16
-VMEM_LIMIT = 24 * 1024 * 1024
-SPLIT_VMEM_LIMIT = 63 * 1024 * 1024
+MIB = 1024 * 1024
 PLACE_COST = 1 << 34
 
 
@@ -24,25 +23,22 @@
     return pl.BlockSpec(shape, lambda *_: (0,) * len(shape))
 
 
-def params():
-    return pltpu.CompilerParams(vmem_limit_bytes=VMEM_LIMIT)
-
-
-def split_kernel(width, n_dp, where, ids, tokens, cotangent, *refs):
+def params(mib=16):
+    return pltpu.CompilerParams(vmem_limit_bytes=mib * MIB)
+
+
+def split_kernel(width, n_dp, where, ids, tokens, *refs):
     outs, (meta, sems) = refs[:-2], refs[-2:]
     k, x = where[0], where[1]
     rows = tokens.shape[0]
     copies = []
     for rel in range(n_dp):
         start = pl.multiple_of((k ^ rel) * width, 128)
-        for which, source in enumerate((tokens, cotangent)):
-            copy = pltpu.make_async_copy(
-                source.at[:, pl.ds(start, width)],
-                outs[which * n_dp + rel].at[pl.ds(0, rows), :],
-                sems.at[which * n_dp + rel],
-            )
-            copy.start()
-            copies.append(copy)
+        copy = pltpu.make_async_copy(
+            tokens.at[:, pl.ds(start, width)], outs[rel].at[pl.ds(0, rows), :], sems.at[rel]
+        )
+        copy.start()
+        copies.append(copy)
     along = ids[...].astype(F32)
     line = lax.broadcasted_iota(jnp.int32, (rows, rows), 0)
     lane = lax.broadcasted_iota(jnp.int32, (rows, rows), 1)
@@ -54,30 +50,28 @@
     meta[...] = jnp.zeros(meta.shape, BF16)
     meta[:, 0:rows] = jnp.where(at == 0, along, jnp.where(at == 1, place, 0.0)).astype(BF16)
     for rel in range(n_dp):
-        copy = pltpu.make_async_copy(meta, outs[rel].at[pl.ds(rows, META), :], sems.at[2 * n_dp + rel])
+        copy = pltpu.make_async_copy(meta, outs[rel].at[pl.ds(rows, META), :], sems.at[n_dp + rel])
         copy.start()
         copies.append(copy)
     for copy in copies:
         copy.wait()
 
 
-def split(where, ids, tokens, cotangent, width, n_dp):
+def split(where, ids, tokens, width, n_dp):
     rows = tokens.shape[0]
-    shapes = [(rows + META, width)] * n_dp + [(rows, width)] * n_dp
     anywhere = pl.BlockSpec(memory_space=pl.ANY)
     return pl.pallas_call(
         functools.partial(split_kernel, width, n_dp),
-        out_shape=[jax.ShapeDtypeStruct(s, BF16) for s in shapes],
+        out_shape=[jax.ShapeDtypeStruct((rows + META, width), BF16)] * n_dp,
         in_specs=[
             pl.BlockSpec(memory_space=pltpu.SMEM),
             pl.BlockSpec(memory_space=pltpu.VMEM),
             anywhere,
-            anywhere,
         ],
-        out_specs=[anywhere] * (2 * n_dp),
-        scratch_shapes=[pltpu.VMEM((META, width), BF16), pltpu.SemaphoreType.DMA((3 * n_dp,))],
-        compiler_params=pltpu.CompilerParams(vmem_limit_bytes=SPLIT_VMEM_LIMIT),
-    )(where, ids, tokens, cotangent)
+        out_specs=[anywhere] * n_dp,
+        scratch_shapes=[pltpu.VMEM((META, width), BF16), pltpu.SemaphoreType.DMA((2 * n_dp,))],
+        compiler_params=params(),
+    )(where, ids, tokens)
 
 
 def placer_of(row, slot_count):
@@ -188,7 +182,7 @@
             pltpu.VMEM((2, local_experts * slots, width), BF16),
             pltpu.SemaphoreType.DMA((2, 8 if local_experts % 8 == 0 else 1)),
         ],
-        compiler_params=params(),
+        compiler_params=params(48),
         cost_estimate=pl.CostEstimate(
             flops=4 * flops, bytes_accessed=2 * local_experts * width * hidden * 2, transcendentals=0
         ),
@@ -215,7 +209,7 @@
         out_shape=jax.ShapeDtypeStruct((local_experts, hidden, width), BF16),
         in_specs=[pl.BlockSpec((per_step, slot_rows, width), lambda e: (e, 0, 0))] + [part_spec] * len(parts),
         out_specs=pl.BlockSpec((per_step, hidden, width), lambda e: (e, 0, 0)),
-        compiler_params=params(),
+        compiler_params=params(48),
         cost_estimate=pl.CostEstimate(
             flops=4 * flops, bytes_accessed=local_experts * width * hidden * 2, transcendentals=0
         ),
@@ -241,7 +235,7 @@
     width = gate_weight.shape[1]
     rows = tokens.shape[0]
     where = jnp.stack([k, x]).astype(jnp.int32)
-    chunks = split(where, expert_ids.reshape(1, rows), tokens, cotangent, width, n_dp)
+    chunks = split(where, expert_ids.reshape(1, rows), tokens, width, n_dp)
     def to_owner(value, rel, flip):
         if rel == 0 and flip == 0:
             return value
@@ -250,9 +244,10 @@
         ]
         return lax.ppermute(value, ("dp", "expert"), pairs)
 
-    own_tokens = [to_owner(c, rel, 0) for rel, c in enumerate(chunks[:n_dp])]
+    own_tokens = [to_owner(c, rel, 0) for rel, c in enumerate(chunks)]
     near_tokens = [to_owner(c, rel, 1) for rel, c in enumerate(chunks[:2])]
-    far_tokens, *grads = lax.optimization_barrier((jnp.stack(own_tokens[2:]), *chunks[n_dp:]))
+    far_tokens, cotangent = lax.optimization_barrier((jnp.stack(own_tokens[2:]), cotangent))
+    grads = [lax.dynamic_slice_in_dim(cotangent, (k ^ rel) * width, width, axis=1) for rel in range(n_dp)]
     near_tokens, far_tokens = lax.optimization_barrier((near_tokens, far_tokens))
     far_tokens = swap(far_tokens, "expert", n_x, 1)
     own_grads = [to_owner(c, rel, 0) for rel, c in enumerate(grads)]

time: 146 us -> 105 us (0.72)
  Pallas kernels: 59.4 us -> 21 us
  local copies, waits for them, and re-layouts: 8.31 us -> 6.11 us
  waiting for transfers between devices: 38.7 us -> 40.9 us
  other arithmetic: 3.54 us -> 1.9 us
    pallas_call x1, Pallas kernels: 33.6 us -> 0.89 us  [split(): pl.pallas_call(functools.partial(split_kernel, width, n_dp), out_shape=[j...]
    pallas_call x2, Pallas kernels: 15.7 us -> 10.1 us  [back(): pl.pallas_call(functools.partial(back_kernel, rels), out_shape=[jax.Shape...]
    unnamed x24 -> x16, local copies, waits for them, and re-layouts: 8.16 us -> 4.84 us
    ppermute x16, waiting for transfers between devices: 17.2 us -> 19.9 us  [swap(): return lax.ppermute(value, axis, [(i, i ^ bit) for i in range(count)])]
  transfers between devices with their start and end apart: 31 -> 31, of which waited for: 15 -> 15; matrix products, arithmetic and copies ran while one was open for 5% -> 6% of each run, Pallas kernels for 18% -> 19%
where the time goes in v5:
time: 105 us
  waiting for transfers between devices  40.9 us (39%)
  starting transfers between devices  29.3 us (28%)
  Pallas kernels  21 us (20%)
  local copies, waits for them, and re-layouts  6.11 us (6%)
  matrix products  4.95 us (5%)
  other arithmetic  1.9 us (2%)
    ppermute x15, waiting for transfers between devices, to_owner(): return lax.ppermute(value, ('dp', 'expert'), pairs)  21 us
    ppermute x16, waiting for transfers between devices, swap(): return lax.ppermute(value, axis, [(i, i ^ bit) for i in range(count)])  19.9 us
    ppermute x16, starting transfers between devices, swap(): return lax.ppermute(value, axis, [(i, i ^ bit) for i in range(count)])  15.2 us
    ppermute x15, starting transfers between devices, to_owner(): return lax.ppermute(value, ('dp', 'expert'), pairs)  14.1 us
    pallas_call x2, Pallas kernels, back(): pl.pallas_call(functools.partial(back_kernel, rels), out_shape=[jax.Shape...  10.1 us
    pallas_call x2, Pallas kernels, weight_grad(): pl.pallas_call(functools.partial(weight_kernel, which, order), grid=(loca...  8.08 us
    dot_general x3, matrix products, project(): jnp.einsum('esd,ehd->esh', values, weight, preferred_element_type=F32)  4.95 us
    unnamed x16, local copies, waits for them, and re-layouts  4.84 us
  transfers between devices with their start and end apart: 31, of which 15 were waited for; matrix products, arithmetic and copies ran while one was open for 6% of the time, Pallas kernels for 19%

profile of v5, /device:TPU:0, one launch (start us, length us, event | category | flops | bytes accessed | tf_op | source)
XLA Modules:
  0.0 105.1 jit_solution(15903360003702799683)
XLA Ops:
  3.3 3.0 %collective-permute-start.1 = (bf16[144,512]{1,0:T(8,128)(2,1)S(1)}, bf16[144,512]{1,0:T(8,128)(2,1)S(1)}, u32[]{:S(2)}, u32[]{:S(2)}) collective-permute-start(bf16[144,512]{1,0:T(8,128)(2,1)S(1)} %get-tuple-element.31), channel_id=1, source_target_pairs={{0,16},{4,20},{8,24},{12,28},{16,0},{20,4},{24,8},{28,12},{1,17},{... | collective-permute-start | bytes 442376 | tf_op jit(solution)/shard_map/ppermute | solution.py:245
  8.1 2.9 %collective-permute-done.1.refs_2_ = bf16[144,512]{1,0:T(8,128)(2,1)S(1)} collective-permute-done((bf16[144,512]{1,0:T(8,128)(2,1)S(1)}, bf16[144,512]{1,0:T(8,128)(2,1)S(1)}, u32[]{:S(2)}, u32[]{:S(2)}) %collective-permute-start.1) | collective-permute-done | bytes 147488 | tf_op jit(solution)/shard_map/ppermute | solution.py:245
  13.0 2.1 %collective-permute-done.4.refs_5_ = bf16[144,512]{1,0:T(8,128)(2,1)S(1)} collective-permute-done((bf16[144,512]{1,0:T(8,128)(2,1)S(1)}, bf16[144,512]{1,0:T(8,128)(2,1)S(1)}, u32[]{:S(2)}, u32[]{:S(2)}) %collective-permute-start.4) | collective-permute-done | bytes 147488 | tf_op jit(solution)/shard_map/ppermute | solution.py:245
  15.1 2.0 %collective-permute-start.5 = (bf16[2,144,512]{2,1,0:T(8,128)(2,1)S(1)}, bf16[2,144,512]{2,1,0:T(8,128)(2,1)S(1)}, u32[]{:S(2)}, u32[]{:S(2)}) collective-permute-start(bf16[2,144,512]{2,1,0:T(8,128)(2,1)S(1)} %pad_maximum_fusion.3), channel_id=1, source_target_pairs={{0,4},{4,0},{1,5},{5,1},{2,6},{6,2},{3,7},{7,3},{8,12},{12,8},{9,1... | collective-permute-start | bytes 884744 | tf_op jit(solution)/shard_map/ppermute | solution.py:19
  20.7 3.2 %collective-permute-done.8.refs_3_ = bf16[128,512]{1,0:T(8,128)(2,1)S(1)} collective-permute-done((bf16[128,512]{1,0:T(8,128)(2,1)S(1)}, bf16[128,512]{1,0:T(8,128)(2,1)S(1)}, u32[]{:S(2)}, u32[]{:S(2)}) %collective-permute-start.8) | collective-permute-done | bytes 131104 | tf_op jit(solution)/shard_map/ppermute | solution.py:245
  23.9 3.1 %collective-permute-done.7.refs_2_ = bf16[128,512]{1,0:T(8,128)(2,1)S(1)} collective-permute-done((bf16[128,512]{1,0:T(8,128)(2,1)S(1)}, bf16[128,512]{1,0:T(8,128)(2,1)S(1)}, u32[]{:S(2)}, u32[]{:S(2)}) %collective-permute-start.7) | collective-permute-done | bytes 131104 | tf_op jit(solution)/shard_map/ppermute | solution.py:245
  29.1 1.7 %slice-done.3 = s8[1572864]{0:T(1024)(128)(4,1)S(1)} async-done(((s8[5767168]{0:T(1024)(128)(4,1)}), s8[1572864]{0:T(1024)(128)(4,1)S(1)}, s32[]{:S(2)}) %slice-start.3) | async-done | bytes 1572888
  36.5 1.9 %collective-permute-start.16 = (bf16[2,16,16,352]{3,2,1,0:T(8,128)(2,1)S(1)}, bf16[2,16,16,352]{3,2,1,0:T(8,128)(2,1)S(1)}, u32[]{:S(2)}, u32[]{:S(2)}) collective-permute-start(bf16[2,16,16,352]{3,2,1,0:T(8,128)(2,1)S(1)} %pad_maximum_fusion.1.refs_6_), channel_id=1, source_target_pairs={{0,16},{8,24},{16,0},{24,8},{1,17},{9,25},{17,1},{25,9},{2,18},{10... | collective-permute-start | bytes 1081352 | tf_op jit(solution)/shard_map/ppermute | solution.py:19
  38.3 2.5 %collective-permute-done.9.refs_4_ = bf16[4,128,512]{2,1,0:T(8,128)(2,1)S(1)} collective-permute-done((bf16[4,128,512]{2,1,0:T(8,128)(2,1)S(1)}, bf16[4,128,512]{2,1,0:T(8,128)(2,1)S(1)}, u32[]{:S(2)}, u32[]{:S(2)}) %collective-permute-start.9) | collective-permute-done | bytes 524320 | tf_op jit(solution)/shard_map/ppermute | solution.py:19
  44.0 2.2 %collective-permute-start.14 = (bf16[16,16,352]{2,1,0:T(8,128)(2,1)S(1)}, bf16[16,16,352]{2,1,0:T(8,128)(2,1)S(1)}, u32[]{:S(2)}, u32[]{:S(2)}) collective-permute-start(bf16[16,16,352]{2,1,0:T(8,128)(2,1)S(1)} %get-tuple-element.63), channel_id=1, source_target_pairs={{0,24},{8,16},{16,8},{24,0},{1,25},{9,17},{17,9},{25,1},{2,26},{10... | collective-permute-start | bytes 540680 | tf_op jit(solution)/shard_map/ppermute | solution.py:19
  46.2 1.8 %collective-permute-done.16 = bf16[2,16,16,352]{3,2,1,0:T(8,128)(2,1)S(1)} collective-permute-done((bf16[2,16,16,352]{3,2,1,0:T(8,128)(2,1)S(1)}, bf16[2,16,16,352]{3,2,1,0:T(8,128)(2,1)S(1)}, u32[]{:S(2)}, u32[]{:S(2)}) %collective-permute-start.16) | collective-permute-done | bytes 360480 | tf_op jit(solution)/shard_map/ppermute | solution.py:19
  48.0 3.6 %collective-permute-done.14 = bf16[16,16,352]{2,1,0:T(8,128)(2,1)S(1)} collective-permute-done((bf16[16,16,352]{2,1,0:T(8,128)(2,1)S(1)}, bf16[16,16,352]{2,1,0:T(8,128)(2,1)S(1)}, u32[]{:S(2)}, u32[]{:S(2)}) %collective-permute-start.14) | collective-permute-done | bytes 180256 | tf_op jit(solution)/shard_map/ppermute | solution.py:19
  51.7 4.5 %collective-permute-done.13 = bf16[16,16,352]{2,1,0:T(8,128)(2,1)S(1)} collective-permute-done((bf16[16,16,352]{2,1,0:T(8,128)(2,1)S(1)}, bf16[16,16,352]{2,1,0:T(8,128)(2,1)S(1)}, u32[]{:S(2)}, u32[]{:S(2)}) %collective-permute-start.13) | collective-permute-done | bytes 180256 | tf_op jit(solution)/shard_map/ppermute | solution.py:19
  56.7 1.8 %collective-permute-start.18 = (bf16[2,16,16,352]{3,2,1,0:T(8,128)(2,1)S(1)}, bf16[2,16,16,352]{3,2,1,0:T(8,128)(2,1)S(1)}, u32[]{:S(2)}, u32[]{:S(2)}) collective-permute-start(bf16[2,16,16,352]{3,2,1,0:T(8,128)(2,1)S(1)} %pad_maximum_fusion.2.h0), channel_id=1, source_target_pairs={{0,16},{8,24},{16,0},{24,8},{1,17},{9,25},{17,1},{25,9},{2,18},{10... | collective-permute-start | bytes 1081352 | tf_op jit(solution)/shard_map/ppermute | solution.py:19
  58.5 5.0 %shard_map.88 = (bf16[128,512]{1,0:T(8,128)(2,1)S(1)}, bf16[128,512]{1,0:T(8,128)(2,1)S(1)}, bf16[128,512]{1,0:T(8,128)(2,1)S(1)}, bf16[128,512]{1,0:T(8,128)(2,1)S(1)}) custom-call(s32[4,8,256]{2,1,0:T(8,128)S(1)} %get-tuple-element.40.refs_5_.lines, bf16[2,16,16,352]{3,2,1,0:T(8,128)(2,1)S(1)} %pad_maximum_fusion.2.h0, ...), custom_call_target="tpu_custom_call" | custom-call | flops 1476395008 | bytes 11534336 | tf_op jit(solution)/shard_map/pallas_call | solution.py:175
  63.6 4.7 %collective-permute-done.18.h0.h2 = bf16[2,16,16,352]{3,2,1,0:T(8,128)(2,1)S(1)} collective-permute-done((bf16[2,16,16,352]{3,2,1,0:T(8,128)(2,1)S(1)}, bf16[2,16,16,352]{3,2,1,0:T(8,128)(2,1)S(1)}, u32[]{:S(2)}, u32[]{:S(2)}) %collective-permute-start.18) | collective-permute-done | bytes 360480 | tf_op jit(solution)/shard_map/ppermute | solution.py:19
  70.4 5.0 %shard_map.89 = (bf16[128,512]{1,0:T(8,128)(2,1)S(1)}, bf16[128,512]{1,0:T(8,128)(2,1)S(1)}, bf16[128,512]{1,0:T(8,128)(2,1)S(1)}, bf16[128,512]{1,0:T(8,128)(2,1)S(1)}) custom-call(s32[4,8,256]{2,1,0:T(8,128)S(1)} %get-tuple-element.40.refs_5_.lines, bf16[2,16,16,352]{3,2,1,0:T(8,128)(2,1)S(1)} %collective-permute-done.18.h0.h2, ...), custom_call_target="tpu_custom_call" | custom-call | flops 1476395008 | bytes 11534336 | tf_op jit(solution)/shard_map/pallas_call | solution.py:175
  77.2 1.7 %collective-permute-start.23 = (bf16[128,512]{1,0:T(8,128)(2,1)S(1)}, bf16[128,512]{1,0:T(8,128)(2,1)S(1)}, u32[]{:S(2)}, u32[]{:S(2)}) collective-permute-start(bf16[128,512]{1,0:T(8,128)(2,1)S(1)} %get-tuple-element.49), channel_id=1, source_target_pairs={{0,16},{4,20},{8,24},{12,28},{16,0},{20,4},{24,8},{28,12},{1,17},{... | collective-permute-start | bytes 393224 | tf_op jit(solution)/shard_map/ppermute | solution.py:245
  81.9 4.6 %collective-permute-done.21 = bf16[128,512]{1,0:T(8,128)(2,1)S(1)} collective-permute-done((bf16[128,512]{1,0:T(8,128)(2,1)S(1)}, bf16[128,512]{1,0:T(8,128)(2,1)S(1)}, u32[]{:S(2)}, u32[]{:S(2)}) %collective-permute-start.21) | collective-permute-done | bytes 131104 | tf_op jit(solution)/shard_map/ppermute | solution.py:245
  86.5 3.2 %collective-permute-done.23 = bf16[128,512]{1,0:T(8,128)(2,1)S(1)} collective-permute-done((bf16[128,512]{1,0:T(8,128)(2,1)S(1)}, bf16[128,512]{1,0:T(8,128)(2,1)S(1)}, u32[]{:S(2)}, u32[]{:S(2)}) %collective-permute-start.23) | collective-permute-done | bytes 131104 | tf_op jit(solution)/shard_map/ppermute | solution.py:245
  91.5 4.0 %shard_map.91 = bf16[16,352,512]{2,1,0:T(8,128)(2,1)} custom-call(bf16[16,64,512]{2,1,0:T(8,128)(2,1)S(1)} %get-tuple-element.41.placed, bf16[2,16,16,352]{3,2,1,0:T(8,128)(2,1)S(1)} %pad_maximum_fusion.2.h0, bf16[2,16,16,352]{3,2,1,0:T(8,128)(2,1)S(1)} %collective-permute-done.19.h1, bf16[2,16,16,352]{3,2,1,0:T(8,128)(2,1)S(1)} %collective-permute-done.18.h0.h2, ...), custom_call_target="tpu_custom_call" | custom-call | flops 1476395008 | bytes 5767168 | tf_op jit(solution)/shard_map/pallas_call | solution.py:206
  95.7 2.7 %collective-permute-start.30 = (bf16[128,512]{1,0:T(8,128)(2,1)S(1)}, bf16[128,512]{1,0:T(8,128)(2,1)S(1)}, u32[]{:S(2)}, u32[]{:S(2)}) collective-permute-start(bf16[128,512]{1,0:T(8,128)(2,1)S(1)} %get-tuple-element.55), channel_id=1, source_target_pairs={{0,2},{1,3},{2,0},{3,1},{4,6},{5,7},{6,4},{7,5},{8,10},{9,11},{10,... | collective-permute-start | bytes 393224 | tf_op jit(solution)/shard_map/ppermute | solution.py:19
  98.4 4.0 %shard_map.90 = bf16[16,352,512]{2,1,0:T(8,128)(2,1)} custom-call(bf16[16,64,512]{2,1,0:T(8,128)(2,1)S(1)} %get-tuple-element.41.placed, bf16[2,16,16,352]{3,2,1,0:T(8,128)(2,1)S(1)} %pad_maximum_fusion.2.h0, bf16[2,16,16,352]{3,2,1,0:T(8,128)(2,1)S(1)} %collective-permute-done.19.h1, bf16[2,16,16,352]{3,2,1,0:T(8,128)(2,1)S(1)} %collective-permute-done.18.h0.h2, ...), custom_call_target="tpu_custom_call" | custom-call | flops 1476395008 | bytes 5767168 | tf_op jit(solution)/shard_map/pallas_call | solution.py:206
  102.4 2.0 %collective-permute-done.30 = bf16[128,512]{1,0:T(8,128)(2,1)S(1)} collective-permute-done((bf16[128,512]{1,0:T(8,128)(2,1)S(1)}, bf16[128,512]{1,0:T(8,128)(2,1)S(1)}, u32[]{:S(2)}, u32[]{:S(2)}) %collective-permute-start.30) | collective-permute-done | bytes 131104 | tf_op jit(solution)/shard_map/ppermute | solution.py:19
  (83 shorter events, 31.0 us)
Async XLA Ops:
  3.3 7.7 %collective-permute-start.1 = (bf16[144,512]{1,0:T(8,128)(2,1)S(1)}, bf16[144,512]{1,0:T(8,128)(2,1)S(1)}, u32[]{:S(2)}, u32[]{:S(2)}) collective-permute-start(bf16[144,512]{1,0:T(8,128)(2,1)S(1)} %get-tuple-element.31), channel_id=1, source_target_pairs={{0,16},{4,20},{8,24},{12,28},{16,0},{20,4},{24,8},{28,12},{1,17},{... | collective-permute-start | bytes 442376 | tf_op jit(solution)/shard_map/ppermute | solution.py:245
  6.3 6.3 %collective-permute-start.2 = (bf16[144,512]{1,0:T(8,128)(2,1)S(1)}, bf16[144,512]{1,0:T(8,128)(2,1)S(1)}, u32[]{:S(2)}, u32[]{:S(2)}) collective-permute-start(bf16[144,512]{1,0:T(8,128)(2,1)S(1)} %get-tuple-element.32), channel_id=1, source_target_pairs={{0,24},{4,28},{8,16},{12,20},{16,8},{20,12},{24,0},{28,4},{1,25},{... | collective-permute-start | bytes 442376 | tf_op jit(solution)/shard_map/ppermute | solution.py:245
  6.3 6.7 %collective-permute-start.3 = (bf16[144,512]{1,0:T(8,128)(2,1)S(1)}, bf16[144,512]{1,0:T(8,128)(2,1)S(1)}, u32[]{:S(2)}, u32[]{:S(2)}) collective-permute-start(bf16[144,512]{1,0:T(8,128)(2,1)S(1)} %get-tuple-element.29.refs_0_), channel_id=1, source_target_pairs={{0,4},{4,0},{8,12},{12,8},{16,20},{20,16},{24,28},{28,24},{1,5},{5... | collective-permute-start | bytes 442376 | tf_op jit(solution)/shard_map/ppermute | solution.py:245
  7.8 7.2 %collective-permute-start.4 = (bf16[144,512]{1,0:T(8,128)(2,1)S(1)}, bf16[144,512]{1,0:T(8,128)(2,1)S(1)}, u32[]{:S(2)}, u32[]{:S(2)}) collective-permute-start(bf16[144,512]{1,0:T(8,128)(2,1)S(1)} %get-tuple-element.30), channel_id=1, source_target_pairs={{0,12},{4,8},{8,4},{12,0},{16,28},{20,24},{24,20},{28,16},{1,13},{... | collective-permute-start | bytes 442376 | tf_op jit(solution)/shard_map/ppermute | solution.py:245
  15.1 11.9 %collective-permute-start.5 = (bf16[2,144,512]{2,1,0:T(8,128)(2,1)S(1)}, bf16[2,144,512]{2,1,0:T(8,128)(2,1)S(1)}, u32[]{:S(2)}, u32[]{:S(2)}) collective-permute-start(bf16[2,144,512]{2,1,0:T(8,128)(2,1)S(1)} %pad_maximum_fusion.3), channel_id=1, source_target_pairs={{0,4},{4,0},{1,5},{5,1},{2,6},{6,2},{3,7},{7,3},{8,12},{12,8},{9,1... | collective-permute-start | bytes 884744 | tf_op jit(solution)/shard_map/ppermute | solution.py:19
  19.5 7.4 %collective-permute-start.7 = (bf16[128,512]{1,0:T(8,128)(2,1)S(1)}, bf16[128,512]{1,0:T(8,128)(2,1)S(1)}, u32[]{:S(2)}, u32[]{:S(2)}) collective-permute-start(bf16[128,512]{1,0:T(8,128)(2,1)S(1)} %get-tuple-element.69), channel_id=1, source_target_pairs={{0,16},{4,20},{8,24},{12,28},{16,0},{20,4},{24,8},{28,12},{1,17},{... | collective-permute-start | bytes 393224 | tf_op jit(solution)/shard_map/ppermute | solution.py:245
  20.2 6.7 %collective-permute-start.6 = (bf16[128,512]{1,0:T(8,128)(2,1)S(1)}, bf16[128,512]{1,0:T(8,128)(2,1)S(1)}, u32[]{:S(2)}, u32[]{:S(2)}) collective-permute-start(bf16[128,512]{1,0:T(8,128)(2,1)S(1)} %get-tuple-element.70), channel_id=1, source_target_pairs={{0,8},{4,12},{8,0},{12,4},{16,24},{20,28},{24,16},{28,20},{1,9},{5... | collective-permute-start | bytes 393224 | tf_op jit(solution)/shard_map/ppermute | solution.py:245
  20.2 6.9 %collective-permute-start = (bf16[144,512]{1,0:T(8,128)(2,1)S(1)}, bf16[144,512]{1,0:T(8,128)(2,1)S(1)}, u32[]{:S(2)}, u32[]{:S(2)}) collective-permute-start(bf16[144,512]{1,0:T(8,128)(2,1)S(1)} %get-tuple-element.30), channel_id=1, source_target_pairs={{0,8},{4,12},{8,0},{12,4},{16,24},{20,28},{24,16},{28,20},{1,9},{5... | collective-permute-start | bytes 442376 | tf_op jit(solution)/shard_map/ppermute | solution.py:245
  27.0 13.8 %collective-permute-start.9 = (bf16[4,128,512]{2,1,0:T(8,128)(2,1)S(1)}, bf16[4,128,512]{2,1,0:T(8,128)(2,1)S(1)}, u32[]{:S(2)}, u32[]{:S(2)}) collective-permute-start(bf16[4,128,512]{2,1,0:T(8,128)(2,1)S(1)} %pad_maximum_fusion.refs_7_), channel_id=1, source_target_pairs={{0,4},{4,0},{1,5},{5,1},{2,6},{6,2},{3,7},{7,3},{8,12},{12,8},{9,1... | collective-permute-start | bytes 1572872 | tf_op jit(solution)/shard_map/ppermute | solution.py:19
  32.5 13.6 %collective-permute-start.15 = (bf16[16,16,352]{2,1,0:T(8,128)(2,1)S(1)}, bf16[16,16,352]{2,1,0:T(8,128)(2,1)S(1)}, u32[]{:S(2)}, u32[]{:S(2)}) collective-permute-start(bf16[16,16,352]{2,1,0:T(8,128)(2,1)S(1)} %get-tuple-element.60), channel_id=1, source_target_pairs={{0,8},{8,0},{16,24},{24,16},{1,9},{9,1},{17,25},{25,17},{2,10},{10... | collective-permute-start | bytes 540680 | tf_op jit(solution)/shard_map/ppermute | solution.py:19
  35.0 11.3 %collective-permute-start.17 = (bf16[16,16,352]{2,1,0:T(8,128)(2,1)S(1)}, bf16[16,16,352]{2,1,0:T(8,128)(2,1)S(1)}, u32[]{:S(2)}, u32[]{:S(2)}) collective-permute-start(bf16[16,16,352]{2,1,0:T(8,128)(2,1)S(1)} %get-tuple-element.66), channel_id=1, source_target_pairs={{0,8},{8,0},{16,24},{24,16},{1,9},{9,1},{17,25},{25,17},{2,10},{10... | collective-permute-start | bytes 540680 | tf_op jit(solution)/shard_map/ppermute | solution.py:19
  36.5 11.6 %collective-permute-start.16 = (bf16[2,16,16,352]{3,2,1,0:T(8,128)(2,1)S(1)}, bf16[2,16,16,352]{3,2,1,0:T(8,128)(2,1)S(1)}, u32[]{:S(2)}, u32[]{:S(2)}) collective-permute-start(bf16[2,16,16,352]{3,2,1,0:T(8,128)(2,1)S(1)} %pad_maximum_fusion.1.refs_6_), channel_id=1, source_target_pairs={{0,16},{8,24},{16,0},{24,8},{1,17},{9,25},{17,1},{25,9},{2,18},{10... | collective-permute-start | bytes 1081352 | tf_op jit(solution)/shard_map/ppermute | solution.py:19
  44.0 7.7 %collective-permute-start.14 = (bf16[16,16,352]{2,1,0:T(8,128)(2,1)S(1)}, bf16[16,16,352]{2,1,0:T(8,128)(2,1)S(1)}, u32[]{:S(2)}, u32[]{:S(2)}) collective-permute-start(bf16[16,16,352]{2,1,0:T(8,128)(2,1)S(1)} %get-tuple-element.63), channel_id=1, source_target_pairs={{0,24},{8,16},{16,8},{24,0},{1,25},{9,17},{17,9},{25,1},{2,26},{10... | collective-permute-start | bytes 540680 | tf_op jit(solution)/shard_map/ppermute | solution.py:19
  46.2 10.0 %collective-permute-start.13 = (bf16[16,16,352]{2,1,0:T(8,128)(2,1)S(1)}, bf16[16,16,352]{2,1,0:T(8,128)(2,1)S(1)}, u32[]{:S(2)}, u32[]{:S(2)}) collective-permute-start(bf16[16,16,352]{2,1,0:T(8,128)(2,1)S(1)} %get-tuple-element.64), channel_id=1, source_target_pairs={{0,16},{8,24},{16,0},{24,8},{1,17},{9,25},{17,1},{25,9},{2,18},{10... | collective-permute-start | bytes 540680 | tf_op jit(solution)/shard_map/ppermute | solution.py:19
  56.7 11.5 %collective-permute-start.18 = (bf16[2,16,16,352]{3,2,1,0:T(8,128)(2,1)S(1)}, bf16[2,16,16,352]{3,2,1,0:T(8,128)(2,1)S(1)}, u32[]{:S(2)}, u32[]{:S(2)}) collective-permute-start(bf16[2,16,16,352]{3,2,1,0:T(8,128)(2,1)S(1)} %pad_maximum_fusion.2.h0), channel_id=1, source_target_pairs={{0,16},{8,24},{16,0},{24,8},{1,17},{9,25},{17,1},{25,9},{2,18},{10... | collective-permute-start | bytes 1081352 | tf_op jit(solution)/shard_map/ppermute | solution.py:19
  68.3 9.0 %collective-permute-start.26 = (bf16[128,512]{1,0:T(8,128)(2,1)S(1)}, bf16[128,512]{1,0:T(8,128)(2,1)S(1)}, u32[]{:S(2)}, u32[]{:S(2)}) collective-permute-start(bf16[128,512]{1,0:T(8,128)(2,1)S(1)} %get-tuple-element.51), channel_id=1, source_target_pairs={{0,8},{4,12},{8,0},{12,4},{16,24},{20,28},{24,16},{28,20},{1,9},{5... | collective-permute-start | bytes 393224 | tf_op jit(solution)/shard_map/ppermute | solution.py:245
  68.8 10.2 %collective-permute-start.27 = (bf16[128,512]{1,0:T(8,128)(2,1)S(1)}, bf16[128,512]{1,0:T(8,128)(2,1)S(1)}, u32[]{:S(2)}, u32[]{:S(2)}) collective-permute-start(bf16[128,512]{1,0:T(8,128)(2,1)S(1)} %get-tuple-element.52), channel_id=1, source_target_pairs={{0,12},{4,8},{8,4},{12,0},{16,28},{20,24},{24,20},{28,16},{1,13},{... | collective-permute-start | bytes 393224 | tf_op jit(solution)/shard_map/ppermute | solution.py:245
  68.9 11.3 %collective-permute-start.28 = (bf16[128,512]{1,0:T(8,128)(2,1)S(1)}, bf16[128,512]{1,0:T(8,128)(2,1)S(1)}, u32[]{:S(2)}, u32[]{:S(2)}) collective-permute-start(bf16[128,512]{1,0:T(8,128)(2,1)S(1)} %get-tuple-element.54), channel_id=1, source_target_pairs={{0,4},{4,0},{8,12},{12,8},{16,20},{20,16},{24,28},{28,24},{1,5},{5... | collective-permute-start | bytes 393224 | tf_op jit(solution)/shard_map/ppermute | solution.py:245
  75.5 11.1 %collective-permute-start.21 = (bf16[128,512]{1,0:T(8,128)(2,1)S(1)}, bf16[128,512]{1,0:T(8,128)(2,1)S(1)}, u32[]{:S(2)}, u32[]{:S(2)}) collective-permute-start(bf16[128,512]{1,0:T(8,128)(2,1)S(1)} %get-tuple-element.47), channel_id=1, source_target_pairs={{0,24},{4,28},{8,16},{12,20},{16,8},{20,12},{24,0},{28,4},{1,25},{... | collective-permute-start | bytes 393224 | tf_op jit(solution)/shard_map/ppermute | solution.py:245
  77.1 9.4 %collective-permute-start.22 = (bf16[128,512]{1,0:T(8,128)(2,1)S(1)}, bf16[128,512]{1,0:T(8,128)(2,1)S(1)}, u32[]{:S(2)}, u32[]{:S(2)}) collective-permute-start(bf16[128,512]{1,0:T(8,128)(2,1)S(1)} %get-tuple-element.48), channel_id=1, source_target_pairs={{0,28},{4,24},{8,20},{12,16},{16,12},{20,8},{24,4},{28,0},{1,29},{... | collective-permute-start | bytes 393224 | tf_op jit(solution)/shard_map/ppermute | solution.py:245
  77.2 12.5 %collective-permute-start.23 = (bf16[128,512]{1,0:T(8,128)(2,1)S(1)}, bf16[128,512]{1,0:T(8,128)(2,1)S(1)}, u32[]{:S(2)}, u32[]{:S(2)}) collective-permute-start(bf16[128,512]{1,0:T(8,128)(2,1)S(1)} %get-tuple-element.49), channel_id=1, source_target_pairs={{0,16},{4,20},{8,24},{12,28},{16,0},{20,4},{24,8},{28,12},{1,17},{... | collective-permute-start | bytes 393224 | tf_op jit(solution)/shard_map/ppermute | solution.py:245
  79.0 10.8 %collective-permute-start.24 = (bf16[128,512]{1,0:T(8,128)(2,1)S(1)}, bf16[128,512]{1,0:T(8,128)(2,1)S(1)}, u32[]{:S(2)}, u32[]{:S(2)}) collective-permute-start(bf16[128,512]{1,0:T(8,128)(2,1)S(1)} %get-tuple-element.50), channel_id=1, source_target_pairs={{0,20},{4,16},{8,28},{12,24},{16,4},{20,0},{24,12},{28,8},{1,21},{... | collective-permute-start | bytes 393224 | tf_op jit(solution)/shard_map/ppermute | solution.py:245
  80.3 15.2 %collective-permute-start.29 = (bf16[128,512]{1,0:T(8,128)(2,1)S(1)}, bf16[128,512]{1,0:T(8,128)(2,1)S(1)}, u32[]{:S(2)}, u32[]{:S(2)}) collective-permute-start(bf16[128,512]{1,0:T(8,128)(2,1)S(1)} %broadcast_select_fusion), channel_id=1, source_target_pairs={{0,1},{1,0},{2,3},{3,2},{4,5},{5,4},{6,7},{7,6},{8,9},{9,8},{10,11... | collective-permute-start | bytes 393224 | tf_op jit(solution)/shard_map/ppermute | solution.py:19
  95.7 8.6 %collective-permute-start.30 = (bf16[128,512]{1,0:T(8,128)(2,1)S(1)}, bf16[128,512]{1,0:T(8,128)(2,1)S(1)}, u32[]{:S(2)}, u32[]{:S(2)}) collective-permute-start(bf16[128,512]{1,0:T(8,128)(2,1)S(1)} %get-tuple-element.55), channel_id=1, source_target_pairs={{0,2},{1,3},{2,0},{3,1},{4,6},{5,7},{6,4},{7,5},{8,10},{9,11},{10,... | collective-permute-start | bytes 393224 | tf_op jit(solution)/shard_map/ppermute | solution.py:19
  (15 other events, 51.5 us)
